TPU v7x, 32 devices: a whole 2x2x4 slice. The times are simulated.
32 devices in a mesh: dp: 4 (over z), ctx: 8 (over y, x, core).
Axes of the slice: x: 2, y: 2, z: 4, core: 2. Of those that a mesh axis runs over, the one named last changes fastest.
Arguments:
- tokens: bfloat16 [4, 1024, 2048], P('dp', 'ctx'), may hold values from -6 to 6
- routes: int32 [4, 1024, 8], P('dp', 'ctx'), may hold values from 0 to 15, all different within a row; in each aligned block of 128 rows (0 to 127, 128 to 255, ..., all dimensions but the last counted through in order) at most 96 rows name the same one
- cotangent: bfloat16 [4, 1024, 2048], P('dp', 'ctx'), may hold values from -6 to 6
- attn_gain: bfloat16 [2048], P(('dp', 'ctx')), may hold values from 0.099609375 to 1.8984375
- query_weight: bfloat16 [2048, 2048], P(('dp', 'ctx')), may hold values from -0.125 to 0.125
- key_weight: bfloat16 [2048, 2048], P(('dp', 'ctx')), may hold values from -0.125 to 0.125
- value_weight: bfloat16 [2048, 2048], P(('dp', 'ctx')), may hold values from -0.125 to 0.125
- query_gain: bfloat16 [2048], P(('dp', 'ctx')), may hold values from 0.099609375 to 1.8984375
- key_gain: bfloat16 [2048], P(('dp', 'ctx')), may hold values from 0.099609375 to 1.8984375
- out_weight: bfloat16 [2048, 2048], P(('dp', 'ctx')), may hold values from -2 to 2
- mlp_gain: bfloat16 [2048], P(('dp', 'ctx')), may hold values from 0.099609375 to 1.8984375
- router_weight: bfloat16 [2048, 16], P(('dp', 'ctx')), may hold values from -0.0625 to 0.0625
- gate_weight: bfloat16 [32, 2048, 512], P(('dp', 'ctx')), may hold values from -0.125 to 0.125
- up_weight: bfloat16 [32, 2048, 512], P(('dp', 'ctx')), may hold values from -0.125 to 0.125
- down_weight: bfloat16 [32, 512, 2048], P(('dp', 'ctx')), may hold values from -2.5 to 2.5
Outputs:
- layer_out: bfloat16 [4, 1024, 2048], P('dp', 'ctx')
- grad_tokens: bfloat16 [4, 1024, 2048], P('dp', 'ctx')
- grad_attn_gain: float32 [2048], P(('dp', 'ctx'))
- grad_query_weight: float32 [2048, 2048], P(('dp', 'ctx'))
- grad_key_weight: float32 [2048, 2048], P(('dp', 'ctx'))
- grad_value_weight: float32 [2048, 2048], P(('dp', 'ctx'))
- grad_query_gain: float32 [2048], P(('dp', 'ctx'))
- grad_key_gain: float32 [2048], P(('dp', 'ctx'))
- grad_out_weight: float32 [2048, 2048], P(('dp', 'ctx'))
- grad_mlp_gain: float32 [2048], P(('dp', 'ctx'))
- grad_router_weight: float32 [2048, 16], P(('dp', 'ctx'))
- grad_gate_weight: float32 [32, 2048, 512], P(('dp', 'ctx'))
- grad_up_weight: float32 [32, 2048, 512], P(('dp', 'ctx'))
- grad_down_weight: float32 [32, 512, 2048], P(('dp', 'ctx'))
Inputs may be any that keep to these rules, and one draw needn't show every extreme that they name: `routes`: within the 128 rows of one device at most 96 rows name the same expert, a bound that some block reaches of them; a row names 8 different experts.
All inputs are finite; a program needn't handle non-finite values.
Results may differ from a plain program's by a relative error of at most 0.028.
Values may be sent and summed in bfloat16 or wider, within the bound.
No kernel may reach another device: no remote copies, remote signals or barrier semaphores. Data moves between devices by JAX's collectives and lax.ppermute only.
A program may use at most 320 MiB of HBM per device.

v0:
```python
import math

import jax
import jax.numpy as jnp
from jax import lax
from jax.sharding import PartitionSpec as P

HEADS = 16
HEAD_DIM = 128
TOP = 8


EPSILON = 1e-05
NEG_LARGE = -1e30


def contract_rows(left, right):
    return lax.dot_general(
        left, right, (((0,), (0,)), ((), ())), preferred_element_type=jnp.float32
    )


def times_transposed(left, right):
    return lax.dot_general(
        left, right, (((1,), (1,)), ((), ())), preferred_element_type=jnp.float32
    )


def layout_positions(row_index, tok_rows, half_rows, ctx_count):
    device = row_index // tok_rows
    within = row_index % tok_rows
    return jnp.where(
        within < half_rows,
        device * half_rows + within,
        (2 * ctx_count - 1 - device) * half_rows + within - half_rows,
    )


def rotary_tables(position, head_dim):
    freq_index = jnp.arange(head_dim // 2, dtype=jnp.float32)
    inverse = jnp.exp(freq_index * (-2.0 * math.log(10000.0) / head_dim))
    angles = position.astype(jnp.float32)[:, None] * inverse[None, :]
    return (jnp.cos(angles), jnp.sin(angles))


def rotate(tensor, cosine, sine_table, direction):
    half_dim = tensor.shape[-1] // 2
    first_half = tensor[..., :half_dim]
    second_half = tensor[..., half_dim:]
    cos_part = cosine[:, None, :]
    sin_part = sine_table[:, None, :] * direction
    return jnp.concatenate(
        [
            first_half * cos_part - second_half * sin_part,
            second_half * cos_part + first_half * sin_part,
        ],
        axis=-1,
    )


def norm_forward(tensor, gain_vec):
    inverse = lax.rsqrt(jnp.mean(tensor * tensor, axis=-1, keepdims=True) + EPSILON)
    return (tensor * inverse * gain_vec, inverse)


def norm_backward(tensor, inverse, gain_vec, grad_in):
    scaled = grad_in * gain_vec
    grad_gain = jnp.sum(grad_in * tensor * inverse, axis=0)
    grad_tensor = inverse * scaled - tensor * (inverse * inverse * inverse) * jnp.mean(
        scaled * tensor, axis=-1, keepdims=True
    )
    return (grad_tensor, grad_gain)


def block_scores(queries, keys_part, query_pos, key_part_pos, score_scale):
    scores = (
        jnp.einsum("qhd,khd->hqk", queries, keys_part, preferred_element_type=jnp.float32)
        * score_scale
    )
    allowed = key_part_pos[None, None, :] <= query_pos[None, :, None]
    return (scores, allowed)


def score_grads(
    queries,
    keys_part,
    values_part,
    grad_heads,
    query_pos,
    key_part_pos,
    log_total,
    row_delta,
    score_scale,
):
    scores, allowed = block_scores(queries, keys_part, query_pos, key_part_pos, score_scale)
    weights_part = jnp.where(allowed, jnp.exp(scores - log_total[..., None]), 0.0)
    grad_weights = jnp.einsum(
        "qhd,khd->hqk", grad_heads, values_part, preferred_element_type=jnp.float32
    )
    grad_scores = (weights_part * (grad_weights - row_delta[..., None])).astype(jnp.bfloat16)
    return (grad_scores, weights_part.astype(jnp.bfloat16))


def body(
    tokens,
    routes,
    cotangent,
    attn_gain,
    query_weight,
    key_weight,
    value_weight,
    query_gain,
    key_gain,
    out_weight,
    mlp_gain,
    router_weight,
    gate_weight,
    up_weight,
    down_weight,
):
    attn_full, query_w, key_w, value_w, qgain_full, kgain_full, out_w, mlp_full, router_w = (
        lax.all_gather(attn_gain, ("dp", "ctx"), axis=0, tiled=True),
        lax.all_gather(query_weight, ("dp", "ctx"), axis=0, tiled=True),
        lax.all_gather(key_weight, ("dp", "ctx"), axis=0, tiled=True),
        lax.all_gather(value_weight, ("dp", "ctx"), axis=0, tiled=True),
        lax.all_gather(query_gain, ("dp", "ctx"), axis=0, tiled=True),
        lax.all_gather(key_gain, ("dp", "ctx"), axis=0, tiled=True),
        lax.all_gather(out_weight, ("dp", "ctx"), axis=0, tiled=True),
        lax.all_gather(mlp_gain, ("dp", "ctx"), axis=0, tiled=True),
        lax.all_gather(router_weight, ("dp", "ctx"), axis=0, tiled=True),
    )
    attn_gain_f = attn_full.astype(jnp.float32)
    qgain_f = qgain_full.astype(jnp.float32)
    kgain_f = kgain_full.astype(jnp.float32)
    mlp_gain_f = mlp_full.astype(jnp.float32)
    tok_rows = tokens.shape[1]
    model_width = tokens.shape[2]
    expert_count = router_w.shape[1]
    ctx_count = lax.axis_size("ctx")
    ctx_index = lax.axis_index("ctx")
    half_rows = tok_rows // 2
    seq_rows = tok_rows * ctx_count
    capacity = 3 * tok_rows * TOP // (2 * expert_count)
    key_block = min(512, seq_rows)
    block_count = seq_rows // key_block
    score_scale = 1.0 / math.sqrt(HEAD_DIM)
    inputs_f = tokens[0].astype(jnp.float32)
    normed_f, attn_inv = norm_forward(inputs_f, attn_gain_f)
    normed = normed_f.astype(jnp.bfloat16)
    query_pre = jnp.dot(normed, query_w, preferred_element_type=jnp.float32)
    key_pre = jnp.dot(normed, key_w, preferred_element_type=jnp.float32)
    value_rows = jnp.dot(normed, value_w, preferred_element_type=jnp.float32).astype(jnp.bfloat16)
    own_pos = layout_positions(
        ctx_index * tok_rows + jnp.arange(tok_rows, dtype=jnp.int32), tok_rows, half_rows, ctx_count
    )
    own_cos, own_sin = rotary_tables(own_pos, HEAD_DIM)
    query_normed, query_inv = norm_forward(query_pre, qgain_f)
    key_normed, key_inv = norm_forward(key_pre, kgain_f)
    query_rot = rotate(
        query_normed.reshape(tok_rows, HEADS, HEAD_DIM), own_cos, own_sin, 1.0
    ).astype(jnp.bfloat16)
    key_rot = rotate(key_normed.reshape(tok_rows, HEADS, HEAD_DIM), own_cos, own_sin, 1.0).astype(
        jnp.bfloat16
    )
    keys_all, values_all = (
        lax.all_gather(key_rot.reshape(tok_rows, model_width), "ctx", axis=0, tiled=True),
        lax.all_gather(value_rows, "ctx", axis=0, tiled=True),
    )
    key_pos = layout_positions(
        jnp.arange(seq_rows, dtype=jnp.int32), tok_rows, half_rows, ctx_count
    )
    key_blocks = keys_all.reshape(block_count, key_block, HEADS, HEAD_DIM)
    value_blocks = values_all.reshape(block_count, key_block, HEADS, HEAD_DIM)
    pos_blocks = key_pos.reshape(block_count, key_block)

    def running_total(state_in, inputs):
        running_top, exp_total = state_in
        keys_part, part_pos = inputs
        scores, allowed = block_scores(query_rot, keys_part, own_pos, part_pos, score_scale)
        masked = jnp.where(allowed, scores, NEG_LARGE)
        new_top = jnp.maximum(running_top, jnp.max(masked, axis=-1))
        fresh = jnp.sum(jnp.where(allowed, jnp.exp(masked - new_top[..., None]), 0.0), axis=-1)
        return ((new_top, exp_total * jnp.exp(running_top - new_top) + fresh), None)

    start_top = jnp.full((HEADS, tok_rows), NEG_LARGE, jnp.float32)
    (running_top, exp_total), ignored = lax.scan(
        running_total,
        (start_top, jnp.zeros((HEADS, tok_rows), jnp.float32)),
        (key_blocks, pos_blocks),
    )
    log_total = running_top + jnp.log(exp_total)

    def weighted_sum(accum_in, inputs):
        keys_part, values_part, part_pos = inputs
        scores, allowed = block_scores(query_rot, keys_part, own_pos, part_pos, score_scale)
        weights_part = jnp.where(allowed, jnp.exp(scores - log_total[..., None]), 0.0)
        return (
            accum_in
            + jnp.einsum(
                "hqk,khd->qhd",
                weights_part.astype(jnp.bfloat16),
                values_part,
                preferred_element_type=jnp.float32,
            ),
            None,
        )

    attended, ignored = lax.scan(
        weighted_sum,
        jnp.zeros((tok_rows, HEADS, HEAD_DIM), jnp.float32),
        (key_blocks, value_blocks, pos_blocks),
    )
    attended_b = attended.reshape(tok_rows, model_width).astype(jnp.bfloat16)
    middle = inputs_f + jnp.dot(attended_b, out_w, preferred_element_type=jnp.float32)
    mlp_normed_f, mlp_inv = norm_forward(middle, mlp_gain_f)
    mlp_normed = mlp_normed_f.astype(jnp.bfloat16)
    logits = jnp.dot(mlp_normed, router_w, preferred_element_type=jnp.float32)
    router_probs = jax.nn.softmax(logits, axis=-1)
    flat_routes = routes[0].reshape(tok_rows * TOP)
    onehot = (flat_routes[:, None] == jnp.arange(expert_count, dtype=jnp.int32)[None, :]).astype(
        jnp.int32
    )
    slot_index = jnp.sum((jnp.cumsum(onehot, axis=0) - onehot) * onehot, axis=1)
    chosen = onehot.reshape(tok_rows, TOP, expert_count).astype(jnp.float32)
    gate_values = jnp.einsum("tke,te->tk", chosen, router_probs)

    def dispatch(rows_in):
        return (
            jnp.zeros((expert_count, capacity, model_width), jnp.bfloat16)
            .at[flat_routes, slot_index]
            .set(rows_in)
        )

    def collect(buffer):
        even_rows = buffer[2 * flat_routes, slot_index].astype(jnp.float32)
        odd_rows = buffer[2 * flat_routes + 1, slot_index].astype(jnp.float32)
        return (even_rows + odd_rows).reshape(tok_rows, TOP, model_width)

    received = lax.all_to_all(
        jnp.repeat(dispatch(jnp.repeat(mlp_normed, TOP, axis=0)), 2, axis=0),
        ("dp", "ctx"),
        split_axis=0,
        concat_axis=0,
        tiled=True,
    )
    flat_in = received.reshape(-1, model_width)
    gate_pre = jnp.dot(flat_in, gate_weight[0], preferred_element_type=jnp.float32)
    up_pre = jnp.dot(flat_in, up_weight[0], preferred_element_type=jnp.float32)
    hidden = (jax.nn.silu(gate_pre) * up_pre).astype(jnp.bfloat16)
    half_out = (
        jnp.dot(hidden, down_weight[0], preferred_element_type=jnp.float32)
        .astype(jnp.bfloat16)
        .reshape(received.shape)
    )
    expert_rows = collect(
        lax.all_to_all(half_out, ("dp", "ctx"), split_axis=0, concat_axis=0, tiled=True)
    )
    result = middle + jnp.einsum("tk,tkd->td", gate_values, expert_rows)
    grad_result = cotangent[0].astype(jnp.float32)
    grad_gates = jnp.einsum("td,tkd->tk", grad_result, expert_rows)
    grad_rows = (
        (gate_values[:, :, None] * grad_result[:, None, :])
        .astype(jnp.bfloat16)
        .reshape(tok_rows * TOP, model_width)
    )
    grad_received = lax.all_to_all(
        jnp.repeat(dispatch(grad_rows), 2, axis=0),
        ("dp", "ctx"),
        split_axis=0,
        concat_axis=0,
        tiled=True,
    )
    grad_flat = grad_received.reshape(-1, model_width)
    grad_down_w = contract_rows(hidden, grad_flat)
    grad_hidden = times_transposed(grad_flat, down_weight[0])
    sigmoid_val = jax.nn.sigmoid(gate_pre)
    grad_gate_pre = (
        grad_hidden * up_pre * sigmoid_val * (1.0 + gate_pre * (1.0 - sigmoid_val))
    ).astype(jnp.bfloat16)
    grad_up_pre = (grad_hidden * jax.nn.silu(gate_pre)).astype(jnp.bfloat16)
    grad_gate_w = contract_rows(flat_in, grad_gate_pre)
    grad_up_w = contract_rows(flat_in, grad_up_pre)
    grad_copy = (
        (
            times_transposed(grad_gate_pre, gate_weight[0])
            + times_transposed(grad_up_pre, up_weight[0])
        )
        .astype(jnp.bfloat16)
        .reshape(received.shape)
    )
    grad_mlp_normed = jnp.sum(
        collect(lax.all_to_all(grad_copy, ("dp", "ctx"), split_axis=0, concat_axis=0, tiled=True)),
        axis=1,
    )
    grad_probs = jnp.einsum("tk,tke->te", grad_gates, chosen)
    grad_logits = (
        router_probs * (grad_probs - jnp.sum(router_probs * grad_probs, axis=-1, keepdims=True))
    ).astype(jnp.bfloat16)
    grad_router_w = contract_rows(mlp_normed, grad_logits)
    grad_mlp_normed = grad_mlp_normed + times_transposed(grad_logits, router_w)
    grad_middle_norm, grad_mlp_gain = norm_backward(middle, mlp_inv, mlp_gain_f, grad_mlp_normed)
    grad_middle = grad_result + grad_middle_norm
    grad_branch = grad_middle.astype(jnp.bfloat16)
    grad_out_w = contract_rows(attended_b, grad_branch)
    grad_attended = times_transposed(grad_branch, out_w).astype(jnp.bfloat16)
    grad_heads = grad_attended.reshape(tok_rows, HEADS, HEAD_DIM)
    row_delta = jnp.einsum("qhd,qhd->hq", grad_heads.astype(jnp.float32), attended)

    def query_step(accum_in, inputs):
        keys_part, values_part, part_pos = inputs
        grad_scores, weights_b = score_grads(
            query_rot,
            keys_part,
            values_part,
            grad_heads,
            own_pos,
            part_pos,
            log_total,
            row_delta,
            score_scale,
        )
        grad_query_part = accum_in + jnp.einsum(
            "hqk,khd->qhd", grad_scores, keys_part, preferred_element_type=jnp.float32
        )
        grad_key_part = jnp.einsum(
            "hqk,qhd->khd", grad_scores, query_rot, preferred_element_type=jnp.float32
        )
        grad_value_part = jnp.einsum(
            "hqk,qhd->khd", weights_b, grad_heads, preferred_element_type=jnp.float32
        )
        return (grad_query_part, (grad_key_part, grad_value_part))

    zero_heads = jnp.zeros((tok_rows, HEADS, HEAD_DIM), jnp.float32)
    grad_query_rot, (key_terms, value_terms) = lax.scan(
        query_step, zero_heads, (key_blocks, value_blocks, pos_blocks)
    )
    grad_key_rot, grad_value_rows = (
        lax.psum_scatter(
            key_terms.reshape(seq_rows, model_width).astype(jnp.bfloat16),
            "ctx",
            scatter_dimension=0,
            tiled=True,
        ).astype(jnp.float32),
        lax.psum_scatter(
            value_terms.reshape(seq_rows, model_width).astype(jnp.bfloat16),
            "ctx",
            scatter_dimension=0,
            tiled=True,
        ).astype(jnp.float32),
    )
    grad_query_norm = rotate(grad_query_rot * score_scale, own_cos, own_sin, -1.0).reshape(
        tok_rows, model_width
    )
    grad_key_norm = rotate(
        grad_key_rot.reshape(tok_rows, HEADS, HEAD_DIM) * score_scale, own_cos, own_sin, -1.0
    ).reshape(tok_rows, model_width)
    grad_query_pre, grad_query_gain = norm_backward(query_pre, query_inv, qgain_f, grad_query_norm)
    grad_key_pre, grad_key_gain = norm_backward(key_pre, key_inv, kgain_f, grad_key_norm)
    query_grad_b = grad_query_pre.astype(jnp.bfloat16)
    key_grad_b = grad_key_pre.astype(jnp.bfloat16)
    value_grad_b = grad_value_rows.astype(jnp.bfloat16)
    grad_query_w = contract_rows(normed, query_grad_b)
    grad_key_w = contract_rows(normed, key_grad_b)
    grad_value_w = contract_rows(normed, value_grad_b)
    grad_normed = (
        times_transposed(query_grad_b, query_w)
        + times_transposed(key_grad_b, key_w)
        + times_transposed(value_grad_b, value_w)
    )
    grad_inputs_norm, grad_attn_gain = norm_backward(inputs_f, attn_inv, attn_gain_f, grad_normed)
    grad_inputs = grad_middle + grad_inputs_norm
    shares = (
        lax.psum_scatter(grad_attn_gain, ("dp", "ctx"), scatter_dimension=0, tiled=True),
        lax.psum_scatter(grad_query_w, ("dp", "ctx"), scatter_dimension=0, tiled=True),
        lax.psum_scatter(grad_key_w, ("dp", "ctx"), scatter_dimension=0, tiled=True),
        lax.psum_scatter(grad_value_w, ("dp", "ctx"), scatter_dimension=0, tiled=True),
        lax.psum_scatter(grad_query_gain, ("dp", "ctx"), scatter_dimension=0, tiled=True),
        lax.psum_scatter(grad_key_gain, ("dp", "ctx"), scatter_dimension=0, tiled=True),
        lax.psum_scatter(grad_out_w, ("dp", "ctx"), scatter_dimension=0, tiled=True),
        lax.psum_scatter(grad_mlp_gain, ("dp", "ctx"), scatter_dimension=0, tiled=True),
        lax.psum_scatter(grad_router_w, ("dp", "ctx"), scatter_dimension=0, tiled=True),
    )
    return (
        result.astype(jnp.bfloat16)[None],
        grad_inputs.astype(jnp.bfloat16)[None],
        shares[0],
        shares[1],
        shares[2],
        shares[3],
        shares[4],
        shares[5],
        shares[6],
        shares[7],
        shares[8],
        grad_gate_w[None],
        grad_up_w[None],
        grad_down_w[None],
    )


def solution(mesh):
    in_specs = (
        P("dp", "ctx", None),
        P("dp", "ctx", None),
        P("dp", "ctx", None),
        P(("dp", "ctx")),
        P(("dp", "ctx"), None),
        P(("dp", "ctx"), None),
        P(("dp", "ctx"), None),
        P(("dp", "ctx")),
        P(("dp", "ctx")),
        P(("dp", "ctx"), None),
        P(("dp", "ctx")),
        P(("dp", "ctx"), None),
        P(("dp", "ctx"), None, None),
        P(("dp", "ctx"), None, None),
        P(("dp", "ctx"), None, None),
    )
    out_specs = (
        P("dp", "ctx", None),
        P("dp", "ctx", None),
        P(("dp", "ctx")),
        P(("dp", "ctx"), None),
        P(("dp", "ctx"), None),
        P(("dp", "ctx"), None),
        P(("dp", "ctx")),
        P(("dp", "ctx")),
        P(("dp", "ctx"), None),
        P(("dp", "ctx")),
        P(("dp", "ctx"), None),
        P(("dp", "ctx"), None, None),
        P(("dp", "ctx"), None, None),
        P(("dp", "ctx"), None, None),
    )
    return jax.shard_map(body, mesh=mesh, in_specs=in_specs, out_specs=out_specs, check_vma=False)
```

profile of v0, /device:TPU:0, one launch (start us, length us, event | category | flops | bytes accessed | tf_op | source)
XLA Modules:
  0.0 2738.5 jit_solution(9976304849917250630)
XLA Ops:
  12.9 42.6 %all-reduce.9 = (bf16[2048]{0:T(1024)(128)(2,1)S(1)}, bf16[2048]{0:T(1024)(128)(2,1)S(1)}, bf16[2048]{0:T(1024)(128)(2,1)S(1)}, bf16[2048]{0:T(1024)(128)(2,1)S(1)}) all-reduce(bf16[2048]{0:T(1024)(128)(2,1)S(1)} %dynamic-update-slice, bf16[2048]{0:T(1024)(128)(2,1)S(1)} %dynamic-update-slice.1, ...), channel_id=1, replica_groups=mesh['dp'=4,'ctx'=8] {'dp','ctx'}, use_global_device_ids=true, to_apply=%add | all-reduce | flops 8192 | bytes 32768
  57.3 34.0 %all-gather.8.cloned.1.call-done = bf16[2048,2048]{1,0:T(8,128)(2,1)} async-done(((bf16[64,2048]{1,0:T(8,128)(2,1)}), bf16[2048,2048]{1,0:T(8,128)(2,1)}) %all-gather.8.cloned.1.call-update) | async-done | bytes 8388624 | tf_op jit(solution)/shard_map/all_gather | solution.py:125
  98.1 72.3 %all-gather.12.cloned.1.call-done = bf16[2048,2048]{1,0:T(8,128)(2,1)} async-done(((bf16[64,2048]{1,0:T(8,128)(2,1)}), bf16[2048,2048]{1,0:T(8,128)(2,1)}) %all-gather.12.cloned.1.call-update) | async-done | bytes 8388624 | tf_op jit(solution)/shard_map/all_gather | solution.py:124
  179.8 69.4 %all-gather.16.cloned.1.call-done = bf16[2048,2048]{1,0:T(8,128)(2,1)} async-done(((bf16[64,2048]{1,0:T(8,128)(2,1)}), bf16[2048,2048]{1,0:T(8,128)(2,1)}) %all-gather.16.cloned.1.call-update) | async-done | bytes 8388624 | tf_op jit(solution)/shard_map/all_gather | solution.py:123
  272.5 14.4 all-gather.10.cloned.1.call-done
  292.6 33.4 %all-gather.14.cloned.1.call-done = bf16[1024,2048]{1,0:T(8,128)(2,1)} async-done(((bf16[128,2048]{1,0:T(8,128)(2,1)}), bf16[1024,2048]{1,0:T(8,128)(2,1)}) %all-gather.14.cloned.1.call-update) | async-done | bytes 4194320 | tf_op jit(solution)/shard_map/all_gather | solution.py:166
  340.0 25.3 while.40
  367.6 38.6 %all-gather.18.cloned.1.call-done = bf16[2048,2048]{1,0:T(8,128)(2,1)} async-done(((bf16[64,2048]{1,0:T(8,128)(2,1)}), bf16[2048,2048]{1,0:T(8,128)(2,1)}) %all-gather.18.cloned.1.call-update) | async-done | bytes 8388624 | tf_op jit(solution)/shard_map/all_gather | solution.py:128
  435.3 242.1 %all-gather = bf16[32,64,16]{1,2,0:T(8,128)(2,1)S(1)} all-gather(bf16[1,64,16]{1,2,0:T(8,128)(2,1)S(1)} %bitcast.387), channel_id=1, replica_groups=mesh['dp'=4,'ctx'=8] {'dp','ctx'}, dimensions={0}, use_global_device_ids=true | all-gather | bytes 67584 | tf_op jit(solution)/shard_map/all_gather | solution.py:130
  690.8 23.5 all-to-all-done
  722.8 41.1 %all-to-all-start.2 = ((bf16[32,96,2048]{2,1,0:T(8,128)(2,1)}), bf16[32,96,2048]{2,1,0:T(8,128)(2,1)}, u32[]{:S(2)}, u32[]{:S(2)}) async-start(bf16[32,96,2048]{2,1,0:T(8,128)(2,1)} %bitcast.357), calls=%async_computation.2 | async-start | bytes 25165824 | tf_op jit(solution)/shard_map/all_to_all | solution.py:266
  763.9 12.2 fusion.70
  787.4 255.8 %all-to-all-done.2 = bf16[32,96,2048]{2,1,0:T(8,128)(2,1)} async-done(((bf16[32,96,2048]{2,1,0:T(8,128)(2,1)}), bf16[32,96,2048]{2,1,0:T(8,128)(2,1)}, u32[]{:S(2)}, u32[]{:S(2)}) %all-to-all-start.2) | async-done | bytes 12582944 | tf_op jit(solution)/shard_map/all_to_all | solution.py:266
  1043.3 17.7 multiply_convert_fusion
  1074.9 13.8 fusion.72
  1088.7 15.9 add_convert_fusion
  1104.6 249.2 %all-to-all-done.1 = bf16[32,96,2048]{2,1,0:T(8,128)(2,1)} async-done(((bf16[32,96,2048]{2,1,0:T(8,128)(2,1)}), bf16[32,96,2048]{2,1,0:T(8,128)(2,1)}, u32[]{:S(2)}, u32[]{:S(2)}) %all-to-all-start.1) | async-done | bytes 12582944 | tf_op jit(solution)/shard_map/all_to_all | solution.py:256
  1357.8 25.5 gather_fusion.1
  1383.4 25.6 gather_fusion
  1421.3 215.3 %all-to-all-done.3 = bf16[32,96,2048]{2,1,0:T(8,128)(2,1)} async-done(((bf16[32,96,2048]{2,1,0:T(8,128)(2,1)}), bf16[32,96,2048]{2,1,0:T(8,128)(2,1)}, u32[]{:S(2)}, u32[]{:S(2)}) %all-to-all-start.3) | async-done | bytes 12582944 | tf_op jit(solution)/shard_map/all_to_all | solution.py:292
  1636.6 25.4 gather_fusion.3
  1662.0 25.8 gather_fusion.2
  1709.9 27.3 while.41
  1766.9 26.6 reduce-scatter.12.cloned.1.call-done
  1804.0 45.2 %reduce-scatter.10.cloned.1.call-done = bf16[128,2048]{1,0:T(8,128)(2,1)} async-done(((bf16[1024,2048]{1,0:T(8,128)(2,1)}), bf16[128,2048]{1,0:T(8,128)(2,1)}) %reduce-scatter.10.cloned.1.call-update) | async-done | bytes 524304 | tf_op jit(solution)/shard_map/reduce_scatter | solution.py:338
  1876.6 12.1 convolution_bitcast_fusion
  1911.1 75.2 %reduce-scatter.22.cloned.1.call-done = f32[64,16]{1,0:T(8,128)} async-done(((f32[2048,16]{1,0:T(8,128)}), f32[64,16]{1,0:T(8,128)}) %reduce-scatter.22.cloned.1.call-update) | async-done | bytes 4112
  2004.9 40.8 %all-reduce.8 = (f32[2048]{0:T(1024)S(1)}, f32[2048]{0:T(1024)S(1)}, f32[2048]{0:T(1024)S(1)}, f32[2048]{0:T(1024)S(1)}) all-reduce(f32[2048]{0:T(1024)S(1)} %get-tuple-element.350, f32[2048]{0:T(1024)S(1)} %get-tuple-element.348, f32[2048]{0:T(1024)S(1)} %get-tuple-element.346, ...), channel_id=4, replica_groups=mesh['dp'=4,'ctx'=8] {'dp','ctx'}, use_global_device_ids=true, to_apply=%region_28.29.clone | all-reduce | flops 8192 | bytes 65536
  2050.8 118.4 %reduce-scatter.20.cloned.1.call-done = f32[64,2048]{1,0:T(8,128)} async-done(((f32[2048,2048]{1,0:T(8,128)}), f32[64,2048]{1,0:T(8,128)}) %reduce-scatter.20.cloned.1.call-update) | async-done | bytes 524304 | tf_op jit(solution)/shard_map/reduce_scatter | solution.py:379
  2169.3 187.4 %reduce-scatter.18.cloned.1.call-done = f32[64,2048]{1,0:T(8,128)} async-done(((f32[2048,2048]{1,0:T(8,128)}), f32[64,2048]{1,0:T(8,128)}) %reduce-scatter.18.cloned.1.call-update) | async-done | bytes 524304 | tf_op jit(solution)/shard_map/reduce_scatter | solution.py:376
  2356.6 187.3 %reduce-scatter.16.cloned.1.call-done = f32[64,2048]{1,0:T(8,128)} async-done(((f32[2048,2048]{1,0:T(8,128)}), f32[64,2048]{1,0:T(8,128)}) %reduce-scatter.16.cloned.1.call-update) | async-done | bytes 524304 | tf_op jit(solution)/shard_map/reduce_scatter | solution.py:375
  2544.0 187.6 %reduce-scatter.14.cloned.1.call-done = f32[64,2048]{1,0:T(8,128)} async-done(((f32[2048,2048]{1,0:T(8,128)}), f32[64,2048]{1,0:T(8,128)}) %reduce-scatter.14.cloned.1.call-update) | async-done | bytes 524304 | tf_op jit(solution)/shard_map/reduce_scatter | solution.py:374
  (357 shorter events, 355.7 us)
Async XLA Ops:
  7.2 1036.1 %copy-start = (bf16[1,512,2048]{2,1,0:T(8,128)(2,1)S(1)}, bf16[1,512,2048]{2,1,0:T(8,128)(2,1)}, u32[]{:S(2)}) copy-start(bf16[1,512,2048]{2,1,0:T(8,128)(2,1)} %param.35) | copy-start | bytes 6291460
  7.2 84.2 %all-gather.8.cloned.1.call-start = ((), (), s32[]{:S(2)}) async-start(), calls=%async_computation.11 | async-start | bytes 8650752 | tf_op jit(solution)/shard_map/all_gather | solution.py:125
  7.9 162.4 %all-gather.12.cloned.1.call-start = ((), (), s32[]{:S(2)}) async-start(), calls=%async_computation.13 | async-start | bytes 8650752 | tf_op jit(solution)/shard_map/all_gather | solution.py:124
  8.7 240.6 %all-gather.16.cloned.1.call-start = ((), (), s32[]{:S(2)}) async-start(), calls=%async_computation.15 | async-start | bytes 8650752 | tf_op jit(solution)/shard_map/all_gather | solution.py:123
  9.4 277.5 %all-gather.10.cloned.1.call-start = ((), (), s32[]{:S(2)}) async-start(), calls=%async_computation.12 | async-start | bytes 4718592 | tf_op jit(solution)/shard_map/all_gather | solution.py:167
  55.5 193.8 %copy-start.27 = (f32[2048]{0:T(1024)}, f32[2048]{0:T(1024)S(1)}, u32[]{:S(2)}) copy-start(f32[2048]{0:T(1024)S(1)} %convert_element_type.155) | copy-start | bytes 24580
  57.3 191.9 %copy-start.47 = (f32[128]{0:T(128)}, f32[128]{0:T(128)S(1)}, u32[]{:S(2)}) copy-start(f32[128]{0:T(128)S(1)} %get-tuple-element.441) | copy-start | bytes 1540
  91.4 78.9 %copy-start.7 = (bf16[1,128,2048]{2,1,0:T(8,128)(2,1)S(1)}, bf16[1,128,2048]{2,1,0:T(8,128)(2,1)}, u32[]{:S(2)}) copy-start(bf16[1,128,2048]{2,1,0:T(8,128)(2,1)} %param.21) | copy-start | bytes 1572868
  97.1 228.9 %all-gather.14.cloned.1.call-start = ((), (), s32[]{:S(2)}) async-start(), calls=%async_computation.14 | async-start | bytes 4718592 | tf_op jit(solution)/shard_map/all_gather | solution.py:166
  97.2 78.5 %copy-start.42 = (f32[2048]{0:T(1024)}, f32[2048]{0:T(1024)S(1)}, u32[]{:S(2)}) copy-start(f32[2048]{0:T(1024)S(1)} %convert_element_type.158) | copy-start | bytes 24580
  97.2 157.4 %copy-start.40 = (f32[2048]{0:T(1024)}, f32[2048]{0:T(1024)S(1)}, u32[]{:S(2)}) copy-start(f32[2048]{0:T(1024)S(1)} %convert_element_type.161) | copy-start | bytes 24580
  98.0 160.7 %copy-start.36 = (f32[128,64]{0,1:T(8,128)}, f32[128,64]{0,1:T(8,128)S(1)}, u32[]{:S(2)}) copy-start(f32[128,64]{0,1:T(8,128)S(1)} %get-tuple-element.439) | copy-start | bytes 98308
  262.4 143.8 %all-gather.18.cloned.1.call-start = ((), (), s32[]{:S(2)}) async-start(), calls=%async_computation.16 | async-start | bytes 8650752 | tf_op jit(solution)/shard_map/all_gather | solution.py:128
  263.4 148.3 %copy-start.44 = (f32[2048]{0:T(1024)}, f32[2048]{0:T(1024)S(1)}, u32[]{:S(2)}) copy-start(f32[2048]{0:T(1024)S(1)} %convert_element_type.166) | copy-start | bytes 24580
  412.3 266.4 %copy-start.16 = (bf16[128,2048]{1,0:T(8,128)(2,1)}, bf16[128,2048]{1,0:T(8,128)(2,1)S(1)}, u32[]{:S(2)}) copy-start(bf16[128,2048]{1,0:T(8,128)(2,1)S(1)} %multiply_convert_fusion.3) | copy-start | bytes 1572868
  431.2 246.4 %copy-start.29 = (bf16[1,128,2048]{2,1,0:T(8,128)(2,1)S(1)}, bf16[1,128,2048]{2,1,0:T(8,128)(2,1)}, u32[]{:S(2)}) copy-start(bf16[1,128,2048]{2,1,0:T(8,128)(2,1)} %param.23) | copy-start | bytes 1572868
  431.2 283.0 %all-to-all-start = ((bf16[32,96,2048]{2,1,0:T(8,128)(2,1)}), bf16[32,96,2048]{2,1,0:T(8,128)(2,1)}, u32[]{:S(2)}, u32[]{:S(2)}) async-start(bf16[32,96,2048]{2,1,0:T(8,128)(2,1)} %bitcast.356), calls=%async_computation | async-start | bytes 25165824 | tf_op jit(solution)/shard_map/all_to_all | solution.py:239
  722.8 320.4 %all-to-all-start.2 = ((bf16[32,96,2048]{2,1,0:T(8,128)(2,1)}), bf16[32,96,2048]{2,1,0:T(8,128)(2,1)}, u32[]{:S(2)}, u32[]{:S(2)}) async-start(bf16[32,96,2048]{2,1,0:T(8,128)(2,1)} %bitcast.357), calls=%async_computation.2 | async-start | bytes 25165824 | tf_op jit(solution)/shard_map/all_to_all | solution.py:266
  1071.0 282.8 %all-to-all-start.1 = ((bf16[32,96,2048]{2,1,0:T(8,128)(2,1)}), bf16[32,96,2048]{2,1,0:T(8,128)(2,1)}, u32[]{:S(2)}, u32[]{:S(2)}) async-start(bf16[32,96,2048]{2,1,0:T(8,128)(2,1)} %bitcast.366), calls=%async_computation.1 | async-start | bytes 25165824 | tf_op jit(solution)/shard_map/all_to_all | solution.py:256
  1353.8 282.8 %all-to-all-start.3 = ((bf16[32,96,2048]{2,1,0:T(8,128)(2,1)}), bf16[32,96,2048]{2,1,0:T(8,128)(2,1)}, u32[]{:S(2)}, u32[]{:S(2)}) async-start(bf16[32,96,2048]{2,1,0:T(8,128)(2,1)} %bitcast.365), calls=%async_computation.3 | async-start | bytes 25165824 | tf_op jit(solution)/shard_map/all_to_all | solution.py:292
  1357.7 435.8 %reduce-scatter.12.cloned.1.call-start = ((), (), s32[]{:S(2)}) async-start(), calls=%async_computation.18 | async-start | bytes 4718592 | tf_op jit(solution)/shard_map/reduce_scatter | solution.py:344
  1697.7 60.6 %copy-start.9 = (f32[128,2048]{1,0:T(8,128)}, f32[128,2048]{1,0:T(8,128)S(1)}, u32[]{:S(2)}) copy-start(f32[128,2048]{1,0:T(8,128)S(1)} %get-tuple-element.427) | copy-start | bytes 3145732
  1746.2 103.0 %reduce-scatter.10.cloned.1.call-start = ((), (), s32[]{:S(2)}) async-start(), calls=%async_computation.17 | async-start | bytes 4718592 | tf_op jit(solution)/shard_map/reduce_scatter | solution.py:338
  1755.9 230.4 %reduce-scatter.22.cloned.1.call-start = ((), (), s32[]{:S(2)}) async-start(), calls=%async_computation.23 | async-start | bytes 1081344
  1758.2 411.0 %reduce-scatter.20.cloned.1.call-start = ((), (), s32[]{:S(2)}) async-start(), calls=%async_computation.22 | async-start | bytes 17301504 | tf_op jit(solution)/shard_map/reduce_scatter | solution.py:379
  1766.9 589.7 %reduce-scatter.18.cloned.1.call-start = ((), (), s32[]{:S(2)}) async-start(), calls=%async_computation.21 | async-start | bytes 17301504 | tf_op jit(solution)/shard_map/reduce_scatter | solution.py:376
  1802.9 48.8 %copy-start.37 = (f32[128,64]{0,1:T(8,128)S(1)}, f32[128,64]{0,1:T(8,128)}, u32[]{:S(2)}) copy-start(f32[128,64]{0,1:T(8,128)} %copy-done.36) | copy-start | bytes 98308
  1802.9 48.8 %copy-start.46 = (f32[128,64]{0,1:T(8,128)S(1)}, f32[128,64]{0,1:T(8,128)}, u32[]{:S(2)}) copy-start(f32[128,64]{0,1:T(8,128)} %get-tuple-element.437) | copy-start | bytes 98308
  1802.9 741.1 %reduce-scatter.16.cloned.1.call-start = ((), (), s32[]{:S(2)}) async-start(), calls=%async_computation.20 | async-start | bytes 17301504 | tf_op jit(solution)/shard_map/reduce_scatter | solution.py:375
  1804.0 47.7 %copy-start.26 = (f32[128,16,128]{0,2,1:T(8,128)S(1)}, f32[128,16,128]{0,2,1:T(8,128)}, u32[]{:S(2)}) copy-start(f32[128,16,128]{0,2,1:T(8,128)} %broadcast_multiply_fusion) | copy-start | bytes 3145732
  1865.9 865.7 %reduce-scatter.14.cloned.1.call-start = ((), (), s32[]{:S(2)}) async-start(), calls=%async_computation.19 | async-start | bytes 17301504 | tf_op jit(solution)/shard_map/reduce_scatter | solution.py:374
  2000.8 730.7 %copy-start.1 = (bf16[1,512,2048]{2,1,0:T(8,128)(2,1)S(1)}, bf16[1,512,2048]{2,1,0:T(8,128)(2,1)}, u32[]{:S(2)}) copy-start(bf16[1,512,2048]{2,1,0:T(8,128)(2,1)} %param.35) | copy-start | bytes 6291460
  (61 other events, 578.7 us)
Sparse Core Ops, SparseCore 0:
  10.9 80.4 all-gather.7
  94.2 76.0 all-gather.11
  173.2 76.0 all-gather.15
  251.6 35.3 all-gather.9
  289.2 36.7 all-gather.13
  328.7 77.4 all-gather.17
  1746.4 47.1 reduce-scatter.11
  1797.9 51.3 reduce-scatter.9
  1851.5 134.7 reduce-scatter.21
  1989.1 180.1 reduce-scatter.19
  2172.2 184.3 reduce-scatter.17
  2359.5 184.4 reduce-scatter.15
  2546.9 184.5 reduce-scatter.13
where the time goes:
time: 2750 us; the launch traced here: 2740 us
  waiting for transfers between devices  1840 us (67%)
  blocking collectives  326 us (12%)
  matrix products  234 us (9%)
  local copies, waits for them, and re-layouts  218 us (8%)
  other arithmetic  54.9 us (2%)
  starting transfers between devices  54.2 us (2%)
    all_to_all x1, waiting for transfers between devices, body(): lax.all_to_all(jnp.repeat(dispatch(grad_rows), 2, axis=0), ('dp', 'ctx'),...  256 us
    all_to_all x1, waiting for transfers between devices, body(): lax.all_to_all(half_out, ('dp', 'ctx'), split_axis=0, concat_axis=0, tile...  249 us
    all_gather x1, blocking collectives, body(): lax.all_gather(router_weight, ('dp', 'ctx'), axis=0, tiled=True)  242 us
    all_to_all x1, waiting for transfers between devices, body(): lax.all_to_all(grad_copy, ('dp', 'ctx'), split_axis=0, concat_axis=0, til...  215 us
    reduce_scatter x1, waiting for transfers between devices, body(): lax.psum_scatter(grad_query_w, ('dp', 'ctx'), scatter_dimension=0, tiled=...  188 us
    reduce_scatter x1, waiting for transfers between devices, body(): lax.psum_scatter(grad_value_w, ('dp', 'ctx'), scatter_dimension=0, tiled=...  187 us
    reduce_scatter x1, waiting for transfers between devices, body(): lax.psum_scatter(grad_key_w, ('dp', 'ctx'), scatter_dimension=0, tiled=True)  187 us
    reduce_scatter x1, waiting for transfers between devices, body(): lax.psum_scatter(grad_out_w, ('dp', 'ctx'), scatter_dimension=0, tiled=True)  118 us
  transfers between devices with their start and end apart: 17, of which 17 were waited for; matrix products, arithmetic and copies ran while one was open for 12% of the time, Pallas kernels for 0%

commit v1 on v0

v1 whole, which is shorter than its diff:
```python
import math

import jax
import jax.numpy as jnp
import numpy as np
from jax import lax
from jax.sharding import PartitionSpec as P

HEADS = 16
HEAD_DIM = 128
TOP = 8

EPSILON = 1e-05
NEG_LARGE = -1e30
BF = jnp.bfloat16
F32 = jnp.float32
ALL = ("dp", "ctx")


def dot(left, right):
    return jnp.dot(left, right, preferred_element_type=F32)


def contract_rows(left, right):
    return lax.dot_general(left, right, (((0,), (0,)), ((), ())), preferred_element_type=F32)


def times_transposed(left, right):
    return lax.dot_general(left, right, (((1,), (1,)), ((), ())), preferred_element_type=F32)


def rotary_tables(position, head_dim):
    freq_index = jnp.arange(head_dim // 2, dtype=F32)
    inverse = jnp.exp(freq_index * (-2.0 * math.log(10000.0) / head_dim))
    angles = position.astype(F32)[:, None] * inverse[None, :]
    return (jnp.cos(angles), jnp.sin(angles))


def rotate(tensor, cosine, sine_table, direction):
    half_dim = tensor.shape[-1] // 2
    first_half = tensor[..., :half_dim]
    second_half = tensor[..., half_dim:]
    cos_part = cosine[:, None, :]
    sin_part = sine_table[:, None, :] * direction
    return jnp.concatenate(
        [
            first_half * cos_part - second_half * sin_part,
            second_half * cos_part + first_half * sin_part,
        ],
        axis=-1,
    )


def inverse_rms(tensor):
    return lax.rsqrt(jnp.mean(tensor * tensor, axis=-1, keepdims=True) + EPSILON)


def norm_backward(tensor, inverse, gain_vec, grad_in):
    scaled = grad_in * gain_vec
    grad_gain = jnp.sum(grad_in * tensor * inverse, axis=0)
    grad_tensor = inverse * scaled - tensor * (inverse * inverse * inverse) * jnp.mean(
        scaled * tensor, axis=-1, keepdims=True
    )
    return (grad_tensor, grad_gain)


class Layout:
    def __init__(self, rb):
        self.nz = lax.axis_size("dp")
        self.nc = lax.axis_size("ctx")
        self.dz = lax.axis_index("dp")
        self.cx = lax.axis_index("ctx")
        nz, nc = self.nz, self.nc
        order = [0] + list(range(1, nz, 2)) + list(range(nz - 2 + nz % 2, 0, -2))
        self.order = np.array(order, np.int32)
        place = np.zeros(nz, np.int32)
        place[self.order] = np.arange(nz)
        self.place = place
        self.ring = [(order[i], order[(i + 1) % nz]) for i in range(nz)]
        self.pos = jnp.asarray(place)[self.dz]
        bits = [1 << b for b in range(1, (nc - 1).bit_length())]
        self.bits = (bits + [1], bits[::-1] + [1])
        self.slots = []
        for steps in self.bits:
            held = [0]
            for bit in steps:
                held = held + [h ^ bit for h in held]
            self.slots.append(np.array(held, np.int32))
        self.where = []
        for held in self.slots:
            inv = np.zeros(nc, np.int32)
            inv[held] = np.arange(nc)
            self.where.append(inv)
        self.hpd = HEADS // nc
        self.cols = self.hpd * HEAD_DIM
        self.group = HEAD_DIM // rb
        self.rb = rb

    def swap(self, value, bit):
        return lax.ppermute(value, "ctx", [(i, i ^ bit) for i in range(self.nc)])

    def ring_step(self, value):
        return lax.ppermute(value, "dp", self.ring)

    def layer_at(self, step):
        return jnp.asarray(self.order)[(self.pos - step) % self.nz]

    def gather_ring(self, block):
        blocks = [block]
        for _ in range(self.nz - 1):
            blocks.append(self.ring_step(blocks[-1]))
        return blocks

    def assemble_ring(self, blocks):
        rows = blocks[0].shape[0]
        whole = jnp.zeros((self.nz * rows,) + blocks[0].shape[1:], blocks[0].dtype)
        for step, block in enumerate(blocks):
            whole = lax.dynamic_update_slice_in_dim(whole, block, self.layer_at(step) * rows, 0)
        return whole

    def gather_ctx(self, value):
        half = value.shape[0] // 2
        outs = []
        for color in (0, 1):
            held = value[color * half : (color + 1) * half][None]
            for bit in self.bits[color]:
                held = jnp.concatenate([held, self.swap(held, bit)], axis=0)
            outs.append(held)
        return outs

    def reduce_ctx(self, value, color):
        for bit in self.bits[color][::-1]:
            keep = value.shape[0] // 2
            other = self.swap(value[keep:], bit)
            value = (value[:keep].astype(F32) + other.astype(F32)).astype(BF)
        return value[0]

    def reduce_ring(self, parts):
        total = parts(1)
        for step in list(range(2, self.nz)) + [0]:
            total = (self.ring_step(total).astype(F32) + parts(step).astype(F32)).astype(BF)
        return total

    def slots_to_devices(self, value):
        devices = jnp.arange(self.nc) ^ self.cx
        return jnp.stack([value[k][jnp.asarray(self.where[k])[devices]] for k in (0, 1)])

    def devices_to_slots(self, value):
        return jnp.stack([value[k][jnp.asarray(self.slots[k]) ^ self.cx] for k in (0, 1)])

    def head_blocks(self, value):
        rows = value.shape[0]
        split = value.reshape(rows, self.group, self.hpd, self.nc // self.group, HEAD_DIM)
        return split.transpose(3, 1, 0, 2, 4).reshape(self.nc, rows, self.cols)

    def head_rows(self, value):
        rows = value.shape[1]
        split = value.reshape(self.nc // self.group, self.group, rows, self.hpd, HEAD_DIM)
        return split.transpose(2, 1, 3, 0, 4).reshape(rows, self.nc * self.cols)

    def own_heads(self, vector):
        return self.head_blocks(vector[None])[self.cx, 0]

    def all_heads(self, vector):
        whole = jnp.zeros((self.nc, 1, self.cols), vector.dtype)
        whole = lax.dynamic_update_slice(whole, vector[None, None], (self.cx, 0, 0))
        return self.head_rows(whole)[0]


def a2a(value, axes):
    return lax.all_to_all(value, axes, split_axis=0, concat_axis=0, tiled=True)


def experts_gathered(lay, mlp_normed, routes, router_probs, dy_all, gate_w, up_w, down_w):
    nz, nc = lay.nz, lay.nc
    devices = nz * nc
    tok_rows, width = mlp_normed.shape
    half = tok_rows // 2
    expert_count = router_probs.shape[1]
    chosen = jnp.any(routes[:, :, None] == jnp.arange(expert_count, dtype=jnp.int32), axis=1)
    combine = jnp.where(chosen, router_probs, 0.0)
    gates = a2a(jnp.repeat(combine.T, 2, axis=0), ALL)
    layers = jnp.stack([lay.layer_at(step) for step in range(nz)])
    gates = gates.reshape(nz, nc, 2, half)[layers]
    gates = jnp.stack(
        [gates[:, jnp.asarray(lay.slots[k]) ^ lay.cx, k] for k in (0, 1)], axis=1
    ).reshape(devices * tok_rows, 1)
    dy = dy_all.reshape(nz, nc, 2, half, width)[layers]
    dy = jnp.stack(
        [dy[:, jnp.asarray(lay.slots[k]) ^ lay.cx, k] for k in (0, 1)], axis=1
    ).reshape(devices * tok_rows, width)
    chunks = []
    for block in lay.gather_ring(mlp_normed):
        chunks += lay.gather_ctx(block)
    rows = jnp.concatenate(chunks, axis=0).reshape(devices * tok_rows, width)
    gate_pre = dot(rows, gate_w)
    up_pre = dot(rows, up_w)
    sigmoid_val = jax.nn.sigmoid(gate_pre)
    silu = gate_pre * sigmoid_val
    hidden_f = silu * up_pre
    hidden = hidden_f.astype(BF)
    partial_out = (gates * dot(hidden, down_w)).astype(BF)
    grad_hidden = times_transposed(dy, down_w)
    weighted = jnp.sum(grad_hidden * hidden.astype(F32), axis=-1) * gates[:, 0]
    grad_hidden = grad_hidden * gates
    grad_gate_pre = (
        grad_hidden * up_pre * sigmoid_val * (1.0 + gate_pre * (1.0 - sigmoid_val))
    ).astype(BF)
    grad_up_pre = (grad_hidden * silu).astype(BF)
    grad_copy = (
        times_transposed(grad_gate_pre, gate_w) + times_transposed(grad_up_pre, up_w)
    ).astype(BF)
    grad_down_w = contract_rows((hidden.astype(F32) * gates).astype(BF), dy)
    grad_gate_w = contract_rows(rows, grad_gate_pre)
    grad_up_w = contract_rows(rows, grad_up_pre)

    def reduce_all(value):
        value = value.reshape(nz, 2, nc, half, width)

        def parts(step):
            return jnp.concatenate([lay.reduce_ctx(value[step, k], k) for k in (0, 1)], axis=0)

        return lay.reduce_ring(parts).astype(F32)

    places = jnp.asarray(lay.place)
    weighted = weighted.reshape(nz, 2, nc, half)[(lay.pos - places) % nz]
    flip = jnp.arange(nc) ^ lay.cx
    weighted = jnp.concatenate(
        [weighted[:, k][:, jnp.asarray(lay.where[k])[flip]] for k in (0, 1)], axis=-1
    ).reshape(devices, tok_rows)
    weighted = a2a(weighted, ALL).reshape(expert_count, 2, tok_rows).sum(1).T
    grad_sum = reduce_all(grad_copy)
    mixture = reduce_all(partial_out)
    return (mixture, grad_sum, weighted, grad_gate_w, grad_up_w, grad_down_w)


def experts_sent(lay, mlp_normed, routes, router_probs, grad_result, gate_w, up_w, down_w):
    tok_rows, width = mlp_normed.shape
    expert_count = router_probs.shape[1]
    capacity = 3 * tok_rows * TOP // (2 * expert_count)
    flat_routes = routes.reshape(tok_rows * TOP)
    onehot = (flat_routes[:, None] == jnp.arange(expert_count, dtype=jnp.int32)[None, :]).astype(
        jnp.int32
    )
    slot_index = jnp.sum((jnp.cumsum(onehot, axis=0) - onehot) * onehot, axis=1)
    chosen = onehot.reshape(tok_rows, TOP, expert_count).astype(F32)
    gate_values = jnp.einsum("tke,te->tk", chosen, router_probs)

    def dispatch(rows_in):
        sent = jnp.zeros((expert_count, capacity, width), BF).at[flat_routes, slot_index].set(rows_in)
        return a2a(jnp.repeat(sent, 2, axis=0), ALL)

    def collect(buffer):
        even_rows = buffer[2 * flat_routes, slot_index].astype(F32)
        odd_rows = buffer[2 * flat_routes + 1, slot_index].astype(F32)
        return (even_rows + odd_rows).reshape(tok_rows, TOP, width)

    received = dispatch(jnp.repeat(mlp_normed, TOP, axis=0))
    flat_in = received.reshape(-1, width)
    gate_pre = dot(flat_in, gate_w)
    up_pre = dot(flat_in, up_w)
    hidden = (jax.nn.silu(gate_pre) * up_pre).astype(BF)
    half_out = dot(hidden, down_w).astype(BF).reshape(received.shape)
    expert_rows = collect(a2a(half_out, ALL))
    mixture = jnp.einsum("tk,tkd->td", gate_values, expert_rows)
    grad_gates = jnp.einsum("td,tkd->tk", grad_result, expert_rows)
    grad_rows = (
        (gate_values[:, :, None] * grad_result[:, None, :])
        .astype(BF)
        .reshape(tok_rows * TOP, width)
    )
    grad_flat = dispatch(grad_rows).reshape(-1, width)
    grad_down_w = contract_rows(hidden, grad_flat)
    grad_hidden = times_transposed(grad_flat, down_w)
    sigmoid_val = jax.nn.sigmoid(gate_pre)
    grad_gate_pre = (
        grad_hidden * up_pre * sigmoid_val * (1.0 + gate_pre * (1.0 - sigmoid_val))
    ).astype(BF)
    grad_up_pre = (grad_hidden * jax.nn.silu(gate_pre)).astype(BF)
    grad_gate_w = contract_rows(flat_in, grad_gate_pre)
    grad_up_w = contract_rows(flat_in, grad_up_pre)
    grad_copy = (
        (times_transposed(grad_gate_pre, gate_w) + times_transposed(grad_up_pre, up_w))
        .astype(BF)
        .reshape(received.shape)
    )
    grad_sum = jnp.sum(collect(a2a(grad_copy, ALL)), axis=1)
    weighted = router_probs * jnp.einsum("tk,tke->te", grad_gates, chosen)
    return (mixture, grad_sum, weighted, grad_gate_w, grad_up_w, grad_down_w)


def body(
    tokens,
    routes,
    cotangent,
    attn_gain,
    query_weight,
    key_weight,
    value_weight,
    query_gain,
    key_gain,
    out_weight,
    mlp_gain,
    router_weight,
    gate_weight,
    up_weight,
    down_weight,
):
    rb = query_weight.shape[0]
    lay = Layout(rb)
    nz, nc, cx = lay.nz, lay.nc, lay.cx
    tok_rows = tokens.shape[1]
    width = tokens.shape[2]
    half = tok_rows // 2
    seq_rows = tok_rows * nc
    expert_count = router_weight.shape[1]
    hpd, cols = lay.hpd, lay.cols
    devices = nz * nc
    score_scale = 1.0 / math.sqrt(HEAD_DIM)
    capacity = 3 * tok_rows * TOP // (2 * expert_count)
    gathered = devices * tok_rows <= 4 * expert_count * capacity

    lanes = -(-(expert_count + 4) // 128) * 128
    small = jnp.concatenate(
        [router_weight]
        + [g[:, None] for g in (attn_gain, query_gain, key_gain, mlp_gain)]
        + [jnp.zeros((rb, lanes - expert_count - 4), BF)],
        axis=1,
    )
    small = lax.all_gather(small, ALL, axis=0, tiled=True)
    router_w = small[:, :expert_count]
    attn_gain_f, qgain_f, kgain_f, mlp_gain_f = (
        small[:, expert_count + k].astype(F32) for k in range(4)
    )
    sent = jnp.concatenate(
        [lay.head_blocks(w) for w in (query_weight, key_weight, value_weight)], axis=-1
    )
    block = a2a(sent, "ctx").reshape(nc * rb, 3 * cols)
    qkv_w = lay.assemble_ring(lay.gather_ring(block))
    inputs_all = jnp.concatenate(lay.gather_ctx(tokens[0]), axis=0).reshape(seq_rows, width)
    out_w = lax.all_gather(out_weight, ALL, axis=0, tiled=True)
    dy_all = lax.all_gather(cotangent[0], ALL, axis=0, tiled=True) if gathered else None

    inputs_all = inputs_all.astype(F32)
    attn_inv_all = inverse_rms(inputs_all)
    normed = (inputs_all * attn_inv_all * attn_gain_f).astype(BF)
    qkv = dot(normed, qkv_w)
    query_pre, key_pre = qkv[:, :cols], qkv[:, cols : 2 * cols]
    value_rows = qkv[:, 2 * cols :].astype(BF).reshape(seq_rows, hpd, HEAD_DIM)

    def sum_heads(first, second):
        stats = jnp.stack([jnp.sum(first, axis=-1), jnp.sum(second, axis=-1)], axis=-1)
        stats = lay.slots_to_devices(stats.reshape(2, nc, half, 2))
        stats = stats.reshape(2 * nc * half * 2 // 128, 128)
        stats = lax.all_gather(stats, "ctx", axis=0).sum(0)
        stats = lay.devices_to_slots(stats.reshape(2, nc, half, 2)).reshape(seq_rows, 2)
        return stats[:, :1] / width, stats[:, 1:] / width

    query_ms, key_ms = sum_heads(query_pre * query_pre, key_pre * key_pre)
    query_inv, key_inv = lax.rsqrt(query_ms + EPSILON), lax.rsqrt(key_ms + EPSILON)
    own_qgain, own_kgain = lay.own_heads(qgain_f), lay.own_heads(kgain_f)
    row = jnp.arange(half, dtype=jnp.int32)
    owners = [jnp.asarray(lay.slots[k]) ^ cx for k in (0, 1)]
    positions = jnp.concatenate(
        [
            (owners[0][:, None] * half + row).reshape(-1),
            ((2 * nc - 1 - owners[1])[:, None] * half + row).reshape(-1),
        ]
    )
    cosine, sine = rotary_tables(positions, HEAD_DIM)
    query_rot = rotate(
        (query_pre * query_inv * own_qgain).reshape(seq_rows, hpd, HEAD_DIM), cosine, sine, 1.0
    ).astype(BF)
    key_rot = rotate(
        (key_pre * key_inv * own_kgain).reshape(seq_rows, hpd, HEAD_DIM), cosine, sine, 1.0
    ).astype(BF)

    allowed = positions[None, None, :] <= positions[None, :, None]
    scores = jnp.einsum("qhd,khd->hqk", query_rot, key_rot, preferred_element_type=F32) * score_scale
    masked = jnp.where(allowed, scores, NEG_LARGE)
    top = jnp.max(masked, axis=-1, keepdims=True)
    unnormed = jnp.exp(masked - top)
    total = jnp.sum(unnormed, axis=-1, keepdims=True)
    probs_f = unnormed / total
    probs_b = probs_f.astype(BF)
    attended_f = jnp.einsum("hqk,khd->qhd", probs_b, value_rows, preferred_element_type=F32)
    attended_b = attended_f.reshape(seq_rows, cols).astype(BF)

    def rows_to_devices(value):
        value = lay.slots_to_devices(value.reshape(2, nc, half, cols))
        return a2a(value.transpose(1, 0, 2, 3).reshape(nc, tok_rows, cols), "ctx")

    attended_own = lay.head_rows(rows_to_devices(attended_b))
    inputs_f = tokens[0].astype(F32)
    middle = inputs_f + dot(attended_own, out_w)
    mlp_inv = inverse_rms(middle)
    mlp_normed = (middle * mlp_inv * mlp_gain_f).astype(BF)
    router_probs = jax.nn.softmax(dot(mlp_normed, router_w), axis=-1)
    grad_result = cotangent[0].astype(F32)
    if gathered:
        moe = experts_gathered(
            lay, mlp_normed, routes[0], router_probs, dy_all, gate_weight[0], up_weight[0], down_weight[0]
        )
    else:
        moe = experts_sent(
            lay, mlp_normed, routes[0], router_probs, grad_result, gate_weight[0], up_weight[0], down_weight[0]
        )
    mixture, grad_mlp_normed, weighted, grad_gate_w, grad_up_w, grad_down_w = moe
    result = middle + mixture
    grad_logits = (weighted - router_probs * jnp.sum(weighted, axis=-1, keepdims=True)).astype(BF)
    grad_router_w = contract_rows(mlp_normed, grad_logits)
    grad_mlp_normed = grad_mlp_normed + times_transposed(grad_logits, router_w)
    grad_middle_norm, grad_mlp_gain = norm_backward(middle, mlp_inv, mlp_gain_f, grad_mlp_normed)
    grad_middle = grad_result + grad_middle_norm
    grad_branch = grad_middle.astype(BF)
    grad_attended = times_transposed(grad_branch, out_w).astype(BF)
    grad_heads = a2a(lay.head_blocks(grad_attended), "ctx").reshape(nc, 2, half, cols)
    grad_heads = lay.devices_to_slots(grad_heads.transpose(1, 0, 2, 3))
    grad_heads = grad_heads.reshape(seq_rows, hpd, HEAD_DIM)

    branch_all = jnp.concatenate(lay.gather_ctx(grad_branch), axis=0).reshape(seq_rows, width)
    grad_out = contract_rows(attended_b, branch_all).astype(BF).reshape(hpd, lay.group, rb, width)
    share = cx % lay.group
    terms = []
    for k in range(lay.group):
        term = lax.dynamic_index_in_dim(grad_out, share ^ k, 1, keepdims=False)
        terms.append(lay.swap(term, k) if k else term)
    terms = jnp.stack(terms)

    def out_part(step):
        layer = lay.layer_at(step)
        return terms[(layer // hpd) ^ share, layer % hpd]

    grad_out_w = lay.reduce_ring(out_part).astype(F32)

    row_delta = jnp.einsum("qhd,qhd->hq", grad_heads.astype(F32), attended_f)
    grad_probs = jnp.einsum("qhd,khd->hqk", grad_heads, value_rows, preferred_element_type=F32)
    grad_scores = (probs_f * (grad_probs - row_delta[..., None])).astype(BF)
    grad_query_rot = jnp.einsum("hqk,khd->qhd", grad_scores, key_rot, preferred_element_type=F32)
    grad_key_rot = jnp.einsum("hqk,qhd->khd", grad_scores, query_rot, preferred_element_type=F32)
    grad_value = jnp.einsum("hqk,qhd->khd", probs_b, grad_heads, preferred_element_type=F32)
    grad_query_norm = rotate(grad_query_rot * score_scale, cosine, sine, -1.0).reshape(seq_rows, cols)
    grad_key_norm = rotate(grad_key_rot * score_scale, cosine, sine, -1.0).reshape(seq_rows, cols)
    grad_query_gain = jnp.sum(grad_query_norm * query_pre * query_inv, axis=0)
    grad_key_gain = jnp.sum(grad_key_norm * key_pre * key_inv, axis=0)
    scaled_q, scaled_k = grad_query_norm * own_qgain, grad_key_norm * own_kgain
    query_dot, key_dot = sum_heads(scaled_q * query_pre, scaled_k * key_pre)
    grad_query_pre = query_inv * scaled_q - query_pre * (query_inv * query_inv * query_inv) * query_dot
    grad_key_pre = key_inv * scaled_k - key_pre * (key_inv * key_inv * key_inv) * key_dot
    grad_pre = jnp.concatenate(
        [
            grad_query_pre.astype(BF),
            grad_key_pre.astype(BF),
            grad_value.reshape(seq_rows, cols).astype(BF),
        ],
        axis=-1,
    )
    grad_qkv = contract_rows(normed, grad_pre).astype(BF)
    layer_rows = nc * rb

    def qkv_part(step):
        return lax.dynamic_slice_in_dim(grad_qkv, lay.layer_at(step) * layer_rows, layer_rows, 0)

    grad_qkv = a2a(lay.reduce_ring(qkv_part).reshape(nc, rb, 3 * cols), "ctx").astype(F32)
    grad_query_w, grad_key_w, grad_value_w = (
        lay.head_rows(grad_qkv[:, :, k * cols : (k + 1) * cols]) for k in range(3)
    )
    grad_normed = times_transposed(grad_pre, qkv_w).astype(BF).reshape(2, nc, half, width)
    grad_normed = jnp.concatenate([lay.reduce_ctx(grad_normed[k], k) for k in (0, 1)], axis=0)
    attn_inv = inverse_rms(inputs_f)
    grad_inputs_norm, grad_attn_gain = norm_backward(
        inputs_f, attn_inv, attn_gain_f, grad_normed.astype(F32)
    )
    grad_inputs = grad_middle + grad_inputs_norm

    packed = jnp.concatenate(
        [grad_router_w]
        + [
            g[:, None]
            for g in (
                grad_attn_gain,
                lay.all_heads(grad_query_gain),
                lay.all_heads(grad_key_gain),
                grad_mlp_gain,
            )
        ],
        axis=1,
    )
    packed = a2a(packed.reshape(devices, rb * (expert_count + 4)), ALL)
    packed = packed.sum(0).reshape(rb, expert_count + 4)
    gains = [packed[:, expert_count + k] for k in range(4)]
    return (
        result.astype(BF)[None],
        grad_inputs.astype(BF)[None],
        gains[0],
        grad_query_w,
        grad_key_w,
        grad_value_w,
        gains[1],
        gains[2],
        grad_out_w,
        gains[3],
        packed[:, :expert_count],
        grad_gate_w[None],
        grad_up_w[None],
        grad_down_w[None],
    )


def solution(mesh):
    both = ("dp", "ctx")
    in_specs = (
        P("dp", "ctx", None),
        P("dp", "ctx", None),
        P("dp", "ctx", None),
        P(both),
        P(both, None),
        P(both, None),
        P(both, None),
        P(both),
        P(both),
        P(both, None),
        P(both),
        P(both, None),
        P(both, None, None),
        P(both, None, None),
        P(both, None, None),
    )
    out_specs = (
        P("dp", "ctx", None),
        P("dp", "ctx", None),
        P(both),
        P(both, None),
        P(both, None),
        P(both, None),
        P(both),
        P(both),
        P(both, None),
        P(both),
        P(both, None),
        P(both, None, None),
        P(both, None, None),
        P(both, None, None),
    )
    return jax.shard_map(body, mesh=mesh, in_specs=in_specs, out_specs=out_specs, check_vma=False)
```

time: 2750 us -> 1090 us (0.40)
  waiting for transfers between devices: 1840 us -> 325 us
  blocking collectives: 326 us -> 59.6 us
  starting transfers between devices: 54.2 us -> 120 us
  other arithmetic: 54.9 us -> 110 us
  matrix products: 234 us -> 190 us
    reduce_scatter x6 -> x0, waiting for transfers between devices: 753 us -> none  [the longest x1 188 us: body(): lax.psum_scatter(grad_query_w, ('dp', 'ctx'), scatter_dimension=0, tiled=...]
    all_to_all x4 -> x7, waiting for transfers between devices: 744 us -> 23.3 us  [a2a(): return lax.all_to_all(value, axes, split_axis=0, concat_axis=0, tiled=True)]
    ppermute x0 -> x109, waiting for transfers between devices: none -> 301 us  [the longest x18 152 us: ring_step(): return lax.ppermute(value, 'dp', self.ring)]
    all_gather x6 -> x2, waiting for transfers between devices: 262 us -> 0.01 us  [the longest x1 0.01 us: body(): out_w = lax.all_gather(out_weight, ALL, axis=0, tiled=True)]
    all_gather x1 -> x3, blocking collectives: 242 us -> 59.6 us  [the longest x1 43.1 us: body(): small = lax.all_gather(small, ALL, axis=0, tiled=True)]
    ppermute x0 -> x109, starting transfers between devices: none -> 91.2 us  [the longest x91 76.2 us: swap(): return lax.ppermute(value, 'ctx', [(i, i ^ bit) for i in range(self.nc)])]
    unnamed x2 -> x0, blocking collectives: 83.4 us -> none
    unnamed x14 -> x2, waiting for transfers between devices: 77.4 us -> 0.7 us
  transfers between devices with their start and end apart: 17 -> 118, of which waited for: 17 -> 44; matrix products, arithmetic and copies ran while one was open for 12% -> 33% of each run, Pallas kernels for 0% -> 0%
where the time goes in v1:
time: 1090 us; the launch traced here: 1080 us
  waiting for transfers between devices  325 us (30%)
  local copies, waits for them, and re-layouts  241 us (22%)
  matrix products  190 us (17%)
  starting transfers between devices  120 us (11%)
  other arithmetic  110 us (10%)
  blocking collectives  59.6 us (5%)
  between operations  34 us (3%)
    ppermute x18, waiting for transfers between devices, ring_step(): return lax.ppermute(value, 'dp', self.ring)  152 us
    ppermute x91, waiting for transfers between devices, swap(): return lax.ppermute(value, 'ctx', [(i, i ^ bit) for i in range(self.nc)])  149 us
    unnamed x300, local copies, waits for them, and re-layouts  82.4 us
    ppermute x91, starting transfers between devices, swap(): return lax.ppermute(value, 'ctx', [(i, i ^ bit) for i in range(self.nc)])  76.2 us
    dot_general x6, matrix products, dot(): return jnp.dot(left, right, preferred_element_type=F32)  58.2 us
    dot_general x6, matrix products, times_transposed(): lax.dot_general(left, right, (((1,), (1,)), ((), ())), preferred_element_...  57.8 us
    dot_general x6, matrix products, contract_rows(): lax.dot_general(left, right, (((0,), (0,)), ((), ())), preferred_element_...  50 us
    all_gather x1, blocking collectives, body(): small = lax.all_gather(small, ALL, axis=0, tiled=True)  43.1 us
  transfers between devices with their start and end apart: 118, of which 44 were waited for; matrix products, arithmetic and copies ran while one was open for 33% of the time, Pallas kernels for 0%

profile of v1, /device:TPU:0, one launch (start us, length us, event | category | flops | bytes accessed | tf_op | source)
XLA Modules:
  0.0 1079.9 jit_solution(3609684457718544890)
XLA Ops:
  25.7 14.8 %collective-permute-done = bf16[1,64,2048]{2,1,0:T(8,128)(2,1)S(1)} collective-permute-done((bf16[1,64,2048]{2,1,0:T(8,128)(2,1)S(1)}, bf16[1,64,2048]{2,1,0:T(8,128)(2,1)S(1)}, u32[]{:S(2)}, u32[]{:S(2)}) %collective-permute-start) | collective-permute-done | bytes 262176 | tf_op jit(solution)/shard_map/ppermute | solution.py:100
  43.6 43.1 %all_gather.15 = bf16[2048,128]{1,0:T(8,128)(2,1)S(1)} all-gather(bf16[64,128]{1,0:T(8,128)(2,1)S(1)} %concatenate.191), channel_id=1, replica_groups=mesh['dp'=4,'ctx'=8] {'dp','ctx'}, dimensions={0}, use_global_device_ids=true | all-gather | bytes 540672 | tf_op jit(solution)/shard_map/all_gather | solution.py:330
  153.9 36.8 %collective-permute-done.8 = bf16[512,768]{1,0:T(8,128)(2,1)S(1)} collective-permute-done((bf16[512,768]{1,0:T(8,128)(2,1)}, bf16[512,768]{1,0:T(8,128)(2,1)S(1)}, u32[]{:S(2)}, u32[]{:S(2)}) %collective-permute-start.8) | collective-permute-done | bytes 786464 | tf_op jit(solution)/shard_map/ppermute | solution.py:103
  207.9 8.0 all_gather.16
  238.1 8.8 fusion.134
  271.8 8.4 all-to-all-done.1
  335.5 10.7 collective-permute-done.23
  351.1 10.4 collective-permute-done.29
  413.0 14.6 %fusion.43 = f32[4096,512]{0,1:T(8,128)} fusion(bf16[4096,2048]{1,0:T(8,128)(2,1)} %bitcast.609, bf16[1,2048,512]{2,1,0:T(8,128)(2,1)S(1)} %copy-done.113), kind=kOutput, calls=%fused_computation.109 | convolution fusion | flops 8589934592 | bytes 27262976 | tf_op jit(solution)/shard_map/dot_general | solution.py:21
  432.3 10.7 fusion.123
  474.0 10.5 gather_fusion.12
  484.5 10.5 gather_fusion.11
  495.0 8.0 pad_maximum_fusion
  511.4 11.4 %fusion.35 = f32[4096,512]{0,1:T(8,128)} fusion(bf16[4096,2048]{1,0:T(8,128)(2,1)S(1)} %bitcast.522, bf16[1,512,2048]{2,1,0:T(8,128)(2,1)S(1)} %copy-done.111), kind=kOutput, calls=%fused_computation.101 | convolution fusion | flops 8589934592 | bytes 27262976 | tf_op jit(solution)/shard_map/dot_general | solution.py:29
  522.8 21.9 %fusion.1 = (f32[4096]{0:T(1024)S(1)}, bf16[4096,512]{0,1:T(8,128)(2,1)}, bf16[4096,512]{0,1:T(8,128)(2,1)}, bf16[4096,512]{0,1:T(8,128)(2,1)}) fusion(f32[4096,512]{0,1:T(8,128)} %fusion.35, f32[4096,512]{0,1:T(8,128)} %fusion.43, f32[4096]{0:T(1024)S(1)} %mul.600, bf16[4096,2048]{1,0:T(8,128)(2,1)} %bitcast.610, bf16[1,2048,512]{2,1,0:T(8,128)(2,1)S(1)} %copy-done), kind=kOutput, calls=%fused_computation.31 | convolution fusion | flops 8629776384 | bytes 48267264 | tf_op jit(solution)/shard_map/dot_general | solution.py:21
  544.7 15.0 %fusion.14 = f32[1,512,2048]{2,1,0:T(8,128)} fusion(bf16[4096,2048]{1,0:T(8,128)(2,1)} %bitcast.523, bf16[4096,512]{0,1:T(8,128)(2,1)} %get-tuple-element.139, f32[4096]{0:T(1024)S(1)} %mul.600), kind=kOutput, calls=%fused_computation.55 | convolution fusion | flops 8596226048 | bytes 25182208 | tf_op jit(solution)/shard_map/dot_general | solution.py:25
  559.8 12.9 %multiply_convert_fusion = bf16[4096,2048]{1,0:T(8,128)(2,1)} fusion(bf16[4096,512]{0,1:T(8,128)(2,1)S(1)} %copy-done.116, f32[4096]{0:T(1024)S(1)} %mul.600, bf16[1,512,2048]{2,1,0:T(8,128)(2,1)S(1)} %copy-done.112), kind=kOutput, calls=%fused_computation.27 | convolution fusion | flops 8606711808 | bytes 23085056 | tf_op jit(solution)/shard_map/dot_general | solution.py:21
  572.6 15.1 %convolution_bitcast_fusion.1 = f32[1,2048,512]{2,1,0:T(8,128)} fusion(bf16[4096,2048]{1,0:T(8,128)(2,1)} %bitcast.611, bf16[4096,512]{0,1:T(8,128)(2,1)} %get-tuple-element.144), kind=kOutput, calls=%fused_computation.57 | convolution fusion | flops 8589934592 | bytes 25165824 | tf_op jit(solution)/shard_map/dot_general | solution.py:25
  591.2 18.1 %fusion.41 = f32[4096,2048]{1,0:T(8,128)} fusion(bf16[4096,512]{0,1:T(8,128)(2,1)} %get-tuple-element.144, bf16[1,2048,512]{2,1,0:T(8,128)(2,1)} %param.33), kind=kOutput, calls=%fused_computation.107 | convolution fusion | flops 8589934592 | bytes 39845888 | tf_op jit(solution)/shard_map/dot_general | solution.py:29
  616.6 20.3 %add_convert_fusion = bf16[4096,2048]{1,0:T(8,128)(2,1)} fusion(f32[4096,2048]{1,0:T(8,128)} %fusion.41, bf16[4096,512]{0,1:T(8,128)(2,1)} %get-tuple-element.161, bf16[1,2048,512]{2,1,0:T(8,128)(2,1)S(1)} %copy-done), kind=kOutput, calls=%fused_computation.26 | convolution fusion | flops 8606711808 | bytes 56623104 | tf_op jit(solution)/shard_map/dot_general | solution.py:29
  645.0 13.9 %convolution_bitcast_fusion = f32[1,2048,512]{2,1,0:T(8,128)} fusion(bf16[4096,2048]{1,0:T(8,128)(2,1)} %bitcast.612, bf16[4096,512]{0,1:T(8,128)(2,1)S(1)} %copy-done.115), kind=kOutput, calls=%fused_computation.56 | convolution fusion | flops 8589934592 | bytes 25165824 | tf_op jit(solution)/shard_map/dot_general | solution.py:25
  661.1 8.1 fusion.28
  718.4 8.3 collective-permute-done.61
  751.0 9.4 collective-permute-done.81
  763.1 8.5 collective-permute-done.88
  811.4 19.2 %collective-permute-done.69 = bf16[128,2048]{1,0:T(8,128)(2,1)S(1)} collective-permute-done((bf16[128,2048]{1,0:T(8,128)(2,1)S(1)}, bf16[128,2048]{1,0:T(8,128)(2,1)S(1)}, u32[]{:S(2)}, u32[]{:S(2)}) %collective-permute-start.69) | collective-permute-done | bytes 524320 | tf_op jit(solution)/shard_map/ppermute | solution.py:103
  835.0 11.5 %collective-permute-done.76 = bf16[128,2048]{1,0:T(8,128)(2,1)S(1)} collective-permute-done((bf16[128,2048]{1,0:T(8,128)(2,1)S(1)}, bf16[128,2048]{1,0:T(8,128)(2,1)S(1)}, u32[]{:S(2)}, u32[]{:S(2)}) %collective-permute-start.76) | collective-permute-done | bytes 524320 | tf_op jit(solution)/shard_map/ppermute | solution.py:103
  847.3 10.4 collective-permute-done.49
  858.5 10.5 collective-permute-done.83
  944.3 8.5 all_gather.19
  972.0 14.8 %collective-permute-done.96 = bf16[512,768]{1,0:T(8,128)(2,1)S(1)} collective-permute-done((bf16[512,768]{1,0:T(8,128)(2,1)S(1)}, bf16[512,768]{1,0:T(8,128)(2,1)S(1)}, u32[]{:S(2)}, u32[]{:S(2)}) %collective-permute-start.96) | collective-permute-done | bytes 786464 | tf_op jit(solution)/shard_map/ppermute | solution.py:103
  993.0 14.0 %collective-permute-done.97 = bf16[512,768]{1,0:T(8,128)(2,1)S(1)} collective-permute-done((bf16[512,768]{1,0:T(8,128)(2,1)S(1)}, bf16[512,768]{1,0:T(8,128)(2,1)S(1)}, u32[]{:S(2)}, u32[]{:S(2)}) %collective-permute-start.97) | collective-permute-done | bytes 786464 | tf_op jit(solution)/shard_map/ppermute | solution.py:103
  (868 shorter events, 598.6 us)
Async XLA Ops:
  7.2 276.9 %all-gather.4.cloned.1.call-start = ((), (), s32[]{:S(2)}) async-start(), calls=%async_computation.7 | async-start | bytes 8650752 | tf_op jit(solution)/shard_map/all_gather | solution.py:341
  16.0 77.8 %all-to-all-start = ((bf16[8,64,768]{2,1,0:T(8,128)(2,1)}), bf16[8,64,768]{2,1,0:T(8,128)(2,1)}, u32[]{:S(2)}, u32[]{:S(2)}) async-start(bf16[8,64,768]{2,1,0:T(8,128)(2,1)} %pad_maximum_fusion.16), calls=%async_computation | async-start | bytes 1572864 | tf_op jit(solution)/shard_map/all_to_all | solution.py:171
  21.3 406.3 %all-gather.6.cloned.1.call-start = ((), (), s32[]{:S(2)}) async-start(), calls=%async_computation.8 | async-start | bytes 17301504 | tf_op jit(solution)/shard_map/all_gather | solution.py:342
  41.3 45.4 %collective-permute-start.1 = (bf16[2,64,2048]{2,1,0:T(8,128)(2,1)}, bf16[2,64,2048]{2,1,0:T(8,128)(2,1)}, u32[]{:S(2)}, u32[]{:S(2)}) collective-permute-start(bf16[2,64,2048]{2,1,0:T(8,128)(2,1)} %pad_maximum_fusion.19), channel_id=1, source_target_pairs={{0,4},{1,5},{2,6},{3,7},{4,0},{5,1},{6,2},{7,3},{8,12},{9,13},{10,... | collective-permute-start | bytes 1572872 | tf_op jit(solution)/shard_map/ppermute | solution.py:100
  116.3 31.5 %collective-permute-start.7 = (bf16[512,768]{1,0:T(8,128)(2,1)}, bf16[512,768]{1,0:T(8,128)(2,1)}, u32[]{:S(2)}, u32[]{:S(2)}) collective-permute-start(bf16[512,768]{1,0:T(8,128)(2,1)} %collective-permute-done.6), channel_id=1, source_target_pairs={{0,8},{8,24},{24,16},{16,0},{1,9},{9,25},{25,17},{17,1},{2,10},{10... | collective-permute-start | bytes 2359304 | tf_op jit(solution)/shard_map/ppermute | solution.py:103
  128.1 64.5 %collective-permute-start.5 = (bf16[4,64,2048]{2,1,0:T(8,128)(2,1)}, bf16[4,64,2048]{2,1,0:T(8,128)(2,1)}, u32[]{:S(2)}, u32[]{:S(2)}) collective-permute-start(bf16[4,64,2048]{2,1,0:T(8,128)(2,1)} %pad_maximum_fusion.3), channel_id=1, source_target_pairs={{0,1},{1,0},{2,3},{3,2},{4,5},{5,4},{6,7},{7,6},{8,9},{9,8},{10,11... | collective-permute-start | bytes 3145736 | tf_op jit(solution)/shard_map/ppermute | solution.py:100
  147.8 42.9 %collective-permute-start.8 = (bf16[512,768]{1,0:T(8,128)(2,1)}, bf16[512,768]{1,0:T(8,128)(2,1)S(1)}, u32[]{:S(2)}, u32[]{:S(2)}) collective-permute-start(bf16[512,768]{1,0:T(8,128)(2,1)} %collective-permute-done.7), channel_id=1, source_target_pairs={{0,8},{8,24},{24,16},{16,0},{1,9},{9,25},{25,17},{17,1},{2,10},{10... | collective-permute-start | bytes 2359304 | tf_op jit(solution)/shard_map/ppermute | solution.py:103
  321.1 28.8 %collective-permute-start.20 = (bf16[2,64,2048]{2,1,0:T(8,128)(2,1)S(1)}, bf16[2,64,2048]{2,1,0:T(8,128)(2,1)S(1)}, u32[]{:S(2)}, u32[]{:S(2)}) collective-permute-start(bf16[2,64,2048]{2,1,0:T(8,128)(2,1)S(1)} %pad_maximum_fusion.26), channel_id=1, source_target_pairs={{0,2},{1,3},{2,0},{3,1},{4,6},{5,7},{6,4},{7,5},{8,10},{9,11},{10,... | collective-permute-start | bytes 1572872 | tf_op jit(solution)/shard_map/ppermute | solution.py:100
  332.8 39.1 %collective-permute-start.14 = (bf16[4,64,2048]{2,1,0:T(8,128)(2,1)S(1)}, bf16[4,64,2048]{2,1,0:T(8,128)(2,1)S(1)}, u32[]{:S(2)}, u32[]{:S(2)}) collective-permute-start(bf16[4,64,2048]{2,1,0:T(8,128)(2,1)S(1)} %pad_maximum_fusion.5), channel_id=1, source_target_pairs={{0,1},{1,0},{2,3},{3,2},{4,5},{5,4},{6,7},{7,6},{8,9},{9,8},{10,11... | collective-permute-start | bytes 3145736 | tf_op jit(solution)/shard_map/ppermute | solution.py:100
  348.4 32.3 %collective-permute-start.27 = (bf16[2,64,2048]{2,1,0:T(8,128)(2,1)S(1)}, bf16[2,64,2048]{2,1,0:T(8,128)(2,1)S(1)}, u32[]{:S(2)}, u32[]{:S(2)}) collective-permute-start(bf16[2,64,2048]{2,1,0:T(8,128)(2,1)S(1)} %pad_maximum_fusion.28), channel_id=1, source_target_pairs={{0,2},{1,3},{2,0},{3,1},{4,6},{5,7},{6,4},{7,5},{8,10},{9,11},{10,... | collective-permute-start | bytes 1572872 | tf_op jit(solution)/shard_map/ppermute | solution.py:100
  349.9 33.5 %collective-permute-start.24 = (bf16[2,64,2048]{2,1,0:T(8,128)(2,1)S(1)}, bf16[2,64,2048]{2,1,0:T(8,128)(2,1)S(1)}, u32[]{:S(2)}, u32[]{:S(2)}) collective-permute-start(bf16[2,64,2048]{2,1,0:T(8,128)(2,1)S(1)} %pad_maximum_fusion.27), channel_id=1, source_target_pairs={{0,4},{1,5},{2,6},{3,7},{4,0},{5,1},{6,2},{7,3},{8,12},{9,13},{10,... | collective-permute-start | bytes 1572872 | tf_op jit(solution)/shard_map/ppermute | solution.py:100
  361.5 36.6 %collective-permute-start.21 = (bf16[4,64,2048]{2,1,0:T(8,128)(2,1)S(1)}, bf16[4,64,2048]{2,1,0:T(8,128)(2,1)S(1)}, u32[]{:S(2)}, u32[]{:S(2)}) collective-permute-start(bf16[4,64,2048]{2,1,0:T(8,128)(2,1)S(1)} %pad_maximum_fusion.7), channel_id=1, source_target_pairs={{0,1},{1,0},{2,3},{3,2},{4,5},{5,4},{6,7},{7,6},{8,9},{9,8},{10,11... | collective-permute-start | bytes 3145736 | tf_op jit(solution)/shard_map/ppermute | solution.py:100
  612.2 46.7 %all-to-all-start.3 = ((f32[32,1,128]{2,1,0:T(1,128)}), f32[32,1,128]{2,1,0:T(1,128)S(1)}, u32[]{:S(2)}, u32[]{:S(2)}) async-start(f32[32,1,128]{2,1,0:T(1,128)} %bitcast.135), calls=%async_computation.3 | async-start | bytes 32768 | tf_op jit(solution)/shard_map/all_to_all | solution.py:171
  615.1 28.3 %collective-permute-start.60 = (bf16[4,64,2048]{2,1,0:T(8,128)(2,1)}, bf16[4,64,2048]{2,1,0:T(8,128)(2,1)}, u32[]{:S(2)}, u32[]{:S(2)}) collective-permute-start(bf16[4,64,2048]{2,1,0:T(8,128)(2,1)} %get-tuple-element.171), channel_id=1, source_target_pairs={{0,1},{1,0},{2,3},{3,2},{4,5},{5,4},{6,7},{7,6},{8,9},{9,8},{10,11... | collective-permute-start | bytes 3145736 | tf_op jit(solution)/shard_map/ppermute | solution.py:100
  615.6 28.3 %collective-permute-start.53 = (bf16[4,64,2048]{2,1,0:T(8,128)(2,1)}, bf16[4,64,2048]{2,1,0:T(8,128)(2,1)}, u32[]{:S(2)}, u32[]{:S(2)}) collective-permute-start(bf16[4,64,2048]{2,1,0:T(8,128)(2,1)} %get-tuple-element.172), channel_id=1, source_target_pairs={{0,1},{1,0},{2,3},{3,2},{4,5},{5,4},{6,7},{7,6},{8,9},{9,8},{10,11... | collective-permute-start | bytes 3145736 | tf_op jit(solution)/shard_map/ppermute | solution.py:100
  615.7 28.3 %collective-permute-start.50 = (bf16[4,64,2048]{2,1,0:T(8,128)(2,1)}, bf16[4,64,2048]{2,1,0:T(8,128)(2,1)}, u32[]{:S(2)}, u32[]{:S(2)}) collective-permute-start(bf16[4,64,2048]{2,1,0:T(8,128)(2,1)} %get-tuple-element.173), channel_id=1, source_target_pairs={{0,1},{1,0},{2,3},{3,2},{4,5},{5,4},{6,7},{7,6},{8,9},{9,8},{10,11... | collective-permute-start | bytes 3145736 | tf_op jit(solution)/shard_map/ppermute | solution.py:100
  616.1 28.3 %collective-permute-start.46 = (bf16[4,64,2048]{2,1,0:T(8,128)(2,1)}, bf16[4,64,2048]{2,1,0:T(8,128)(2,1)}, u32[]{:S(2)}, u32[]{:S(2)}) collective-permute-start(bf16[4,64,2048]{2,1,0:T(8,128)(2,1)} %get-tuple-element.174), channel_id=1, source_target_pairs={{0,1},{1,0},{2,3},{3,2},{4,5},{5,4},{6,7},{7,6},{8,9},{9,8},{10,11... | collective-permute-start | bytes 3145736 | tf_op jit(solution)/shard_map/ppermute | solution.py:100
  616.2 28.3 %collective-permute-start.43 = (bf16[4,64,2048]{2,1,0:T(8,128)(2,1)}, bf16[4,64,2048]{2,1,0:T(8,128)(2,1)}, u32[]{:S(2)}, u32[]{:S(2)}) collective-permute-start(bf16[4,64,2048]{2,1,0:T(8,128)(2,1)} %get-tuple-element.175), channel_id=1, source_target_pairs={{0,1},{1,0},{2,3},{3,2},{4,5},{5,4},{6,7},{7,6},{8,9},{9,8},{10,11... | collective-permute-start | bytes 3145736 | tf_op jit(solution)/shard_map/ppermute | solution.py:100
  680.2 33.4 %collective-permute-start.51 = (bf16[2,64,2048]{2,1,0:T(8,128)(2,1)}, bf16[2,64,2048]{2,1,0:T(8,128)(2,1)}, u32[]{:S(2)}, u32[]{:S(2)}) collective-permute-start(bf16[2,64,2048]{2,1,0:T(8,128)(2,1)} %slice.914), channel_id=1, source_target_pairs={{0,4},{1,5},{2,6},{3,7},{4,0},{5,1},{6,2},{7,3},{8,12},{9,13},{10,... | collective-permute-start | bytes 1572872 | tf_op jit(solution)/shard_map/ppermute | solution.py:100
  694.3 32.5 %collective-permute-start.61 = (bf16[2,64,2048]{2,1,0:T(8,128)(2,1)S(1)}, bf16[2,64,2048]{2,1,0:T(8,128)(2,1)S(1)}, u32[]{:S(2)}, u32[]{:S(2)}) collective-permute-start(bf16[2,64,2048]{2,1,0:T(8,128)(2,1)S(1)} %copy-done.63), channel_id=1, source_target_pairs={{0,2},{1,3},{2,0},{3,1},{4,6},{5,7},{6,4},{7,5},{8,10},{9,11},{10,... | collective-permute-start | bytes 1572872 | tf_op jit(solution)/shard_map/ppermute | solution.py:100
  702.4 25.9 %collective-permute-start.58 = (bf16[2,64,2048]{2,1,0:T(8,128)(2,1)S(1)}, bf16[2,64,2048]{2,1,0:T(8,128)(2,1)S(1)}, u32[]{:S(2)}, u32[]{:S(2)}) collective-permute-start(bf16[2,64,2048]{2,1,0:T(8,128)(2,1)S(1)} %copy-done.62), channel_id=1, source_target_pairs={{0,4},{1,5},{2,6},{3,7},{4,0},{5,1},{6,2},{7,3},{8,12},{9,13},{10,... | collective-permute-start | bytes 1572872 | tf_op jit(solution)/shard_map/ppermute | solution.py:100
  705.5 30.5 %collective-permute-start.64 = (bf16[2,64,2048]{2,1,0:T(8,128)(2,1)S(1)}, bf16[2,64,2048]{2,1,0:T(8,128)(2,1)S(1)}, u32[]{:S(2)}, u32[]{:S(2)}) collective-permute-start(bf16[2,64,2048]{2,1,0:T(8,128)(2,1)S(1)} %slice.938), channel_id=1, source_target_pairs={{0,4},{1,5},{2,6},{3,7},{4,0},{5,1},{6,2},{7,3},{8,12},{9,13},{10,... | collective-permute-start | bytes 1572872 | tf_op jit(solution)/shard_map/ppermute | solution.py:100
  716.8 30.5 %collective-permute-start.71 = (bf16[2,64,2048]{2,1,0:T(8,128)(2,1)S(1)}, bf16[2,64,2048]{2,1,0:T(8,128)(2,1)S(1)}, u32[]{:S(2)}, u32[]{:S(2)}) collective-permute-start(bf16[2,64,2048]{2,1,0:T(8,128)(2,1)S(1)} %slice.950), channel_id=1, source_target_pairs={{0,4},{1,5},{2,6},{3,7},{4,0},{5,1},{6,2},{7,3},{8,12},{9,13},{10,... | collective-permute-start | bytes 1572872 | tf_op jit(solution)/shard_map/ppermute | solution.py:100
  728.4 32.1 %collective-permute-start.81 = (bf16[2,64,2048]{2,1,0:T(8,128)(2,1)S(1)}, bf16[2,64,2048]{2,1,0:T(8,128)(2,1)S(1)}, u32[]{:S(2)}, u32[]{:S(2)}) collective-permute-start(bf16[2,64,2048]{2,1,0:T(8,128)(2,1)S(1)} %slice.968), channel_id=1, source_target_pairs={{0,2},{1,3},{2,0},{3,1},{4,6},{5,7},{6,4},{7,5},{8,10},{9,11},{10,... | collective-permute-start | bytes 1572872 | tf_op jit(solution)/shard_map/ppermute | solution.py:100
  738.1 33.6 %collective-permute-start.88 = (bf16[2,64,2048]{2,1,0:T(8,128)(2,1)S(1)}, bf16[2,64,2048]{2,1,0:T(8,128)(2,1)S(1)}, u32[]{:S(2)}, u32[]{:S(2)}) collective-permute-start(bf16[2,64,2048]{2,1,0:T(8,128)(2,1)S(1)} %slice.980), channel_id=1, source_target_pairs={{0,2},{1,3},{2,0},{3,1},{4,6},{5,7},{6,4},{7,5},{8,10},{9,11},{10,... | collective-permute-start | bytes 1572872 | tf_op jit(solution)/shard_map/ppermute | solution.py:100
  749.3 28.0 %collective-permute-start.38 = (bf16[1,64,2048]{2,1,0:T(8,128)(2,1)S(1)}, bf16[1,64,2048]{2,1,0:T(8,128)(2,1)S(1)}, u32[]{:S(2)}, u32[]{:S(2)}) collective-permute-start(bf16[1,64,2048]{2,1,0:T(8,128)(2,1)S(1)} %slice.892), channel_id=1, source_target_pairs={{0,2},{1,3},{2,0},{3,1},{4,6},{5,7},{6,4},{7,5},{8,10},{9,11},{10,... | collective-permute-start | bytes 786440 | tf_op jit(solution)/shard_map/ppermute | solution.py:100
  801.3 45.9 %collective-permute-start.89 = (bf16[1,64,2048]{2,1,0:T(8,128)(2,1)S(1)}, bf16[1,64,2048]{2,1,0:T(8,128)(2,1)S(1)}, u32[]{:S(2)}, u32[]{:S(2)}) collective-permute-start(bf16[1,64,2048]{2,1,0:T(8,128)(2,1)S(1)} %slice.982), channel_id=1, source_target_pairs={{0,4},{1,5},{2,6},{3,7},{4,0},{5,1},{6,2},{7,3},{8,12},{9,13},{10,... | collective-permute-start | bytes 786440 | tf_op jit(solution)/shard_map/ppermute | solution.py:100
  805.4 26.4 %collective-permute-start.79 = (bf16[1,64,2048]{2,1,0:T(8,128)(2,1)S(1)}, bf16[1,64,2048]{2,1,0:T(8,128)(2,1)S(1)}, u32[]{:S(2)}, u32[]{:S(2)}) collective-permute-start(bf16[1,64,2048]{2,1,0:T(8,128)(2,1)S(1)} %slice.964), channel_id=1, source_target_pairs={{0,2},{1,3},{2,0},{3,1},{4,6},{5,7},{6,4},{7,5},{8,10},{9,11},{10,... | collective-permute-start | bytes 786440 | tf_op jit(solution)/shard_map/ppermute | solution.py:100
  832.1 25.7 %collective-permute-start.49 = (bf16[128,2048]{1,0:T(8,128)(2,1)S(1)}, bf16[128,2048]{1,0:T(8,128)(2,1)S(1)}, u32[]{:S(2)}, u32[]{:S(2)}) collective-permute-start(bf16[128,2048]{1,0:T(8,128)(2,1)S(1)} %add_convert_fusion.24), channel_id=1, source_target_pairs={{0,8},{8,24},{24,16},{16,0},{1,9},{9,25},{25,17},{17,1},{2,10},{10... | collective-permute-start | bytes 1572872 | tf_op jit(solution)/shard_map/ppermute | solution.py:103
  893.7 74.2 %collective-permute-start.103 = (bf16[2,64,2048]{2,1,0:T(8,128)(2,1)}, bf16[2,64,2048]{2,1,0:T(8,128)(2,1)}, u32[]{:S(2)}, u32[]{:S(2)}) collective-permute-start(bf16[2,64,2048]{2,1,0:T(8,128)(2,1)} %pad_maximum_fusion.36), channel_id=1, source_target_pairs={{0,2},{1,3},{2,0},{3,1},{4,6},{5,7},{6,4},{7,5},{8,10},{9,11},{10,... | collective-permute-start | bytes 1572872 | tf_op jit(solution)/shard_map/ppermute | solution.py:100
  896.6 73.0 %collective-permute-start.100 = (bf16[2,64,2048]{2,1,0:T(8,128)(2,1)}, bf16[2,64,2048]{2,1,0:T(8,128)(2,1)}, u32[]{:S(2)}, u32[]{:S(2)}) collective-permute-start(bf16[2,64,2048]{2,1,0:T(8,128)(2,1)} %pad_maximum_fusion.35), channel_id=1, source_target_pairs={{0,4},{1,5},{2,6},{3,7},{4,0},{5,1},{6,2},{7,3},{8,12},{9,13},{10,... | collective-permute-start | bytes 1572872 | tf_op jit(solution)/shard_map/ppermute | solution.py:100
  1008.1 28.6 %collective-permute-start.98 = (bf16[512,768]{1,0:T(8,128)(2,1)}, bf16[512,768]{1,0:T(8,128)(2,1)}, u32[]{:S(2)}, u32[]{:S(2)}) collective-permute-start(bf16[512,768]{1,0:T(8,128)(2,1)} %add_convert_fusion.2), channel_id=1, source_target_pairs={{0,8},{8,24},{24,16},{16,0},{1,9},{9,25},{25,17},{17,1},{2,10},{10... | collective-permute-start | bytes 2359304 | tf_op jit(solution)/shard_map/ppermute | solution.py:103
  (209 other events, 5075.1 us)
Sparse Core Ops, SparseCore 0:
  10.9 86.6 all-gather.3
  100.4 145.0 all-gather.5

commit v2 on v1

v2 whole, which is shorter than its diff:
```python
import functools
import math

import jax
import jax.numpy as jnp
import numpy as np
from jax import lax
from jax.experimental import pallas as pl
from jax.experimental.pallas import tpu as pltpu
from jax.sharding import PartitionSpec as P

HEADS = 16
HEAD_DIM = 128
TOP = 8

EPSILON = 1e-05
NEG_LARGE = -1e30
NOTES = 128
BF = jnp.bfloat16
F32 = jnp.float32
ALL = ("dp", "ctx")


def dot(left, right):
    return jnp.dot(left, right, preferred_element_type=F32)


def contract_rows(left, right):
    return lax.dot_general(left, right, (((0,), (0,)), ((), ())), preferred_element_type=F32)


def times_transposed(left, right):
    return lax.dot_general(left, right, (((1,), (1,)), ((), ())), preferred_element_type=F32)


def inverse_rms(tensor):
    return lax.rsqrt(jnp.mean(tensor * tensor, axis=-1, keepdims=True) + EPSILON)


def norm_backward(tensor, inverse, gain_vec, grad_in):
    scaled = grad_in * gain_vec
    grad_gain = jnp.sum(grad_in * tensor * inverse, axis=0)
    grad_tensor = inverse * scaled - tensor * (inverse * inverse * inverse) * jnp.mean(
        scaled * tensor, axis=-1, keepdims=True
    )
    return (grad_tensor, grad_gain)


class Layout:
    def __init__(self, rb):
        self.nz = lax.axis_size("dp")
        self.nc = lax.axis_size("ctx")
        self.dz = lax.axis_index("dp")
        self.cx = lax.axis_index("ctx")
        nz, nc = self.nz, self.nc
        order = [0] + list(range(1, nz, 2)) + list(range(nz - 2 + nz % 2, 0, -2))
        self.ring = [(order[i], order[(i + 1) % nz]) for i in range(nz)]
        odd = self.dz % 2 == 1
        self.pos = jnp.where(odd, (self.dz + 1) // 2, jnp.where(self.dz == 0, 0, nz - self.dz // 2))
        self.bits = [1 << b for b in range(1, (nc - 1).bit_length())]
        self.flips = list(range(2, nc, 2))
        self.hpd = HEADS // nc
        self.cols = self.hpd * HEAD_DIM
        self.group = HEAD_DIM // rb
        self.rb = rb

    def swap(self, value, bit):
        return lax.ppermute(value, "ctx", [(i, i ^ bit) for i in range(self.nc)])

    def ring_step(self, value):
        return lax.ppermute(value, "dp", self.ring)

    def layer_at(self, step):
        place = (self.pos - step) % self.nz
        back = jnp.where(place == 0, 0, 2 * (self.nz - place))
        return jnp.where((place > 0) & (place <= self.nz // 2), 2 * place - 1, back)

    def gather_ring(self, block):
        blocks = [block]
        for _ in range(self.nz - 1):
            blocks.append(self.ring_step(blocks[-1]))
        return blocks

    def gather_near(self, value):
        return jnp.concatenate([value] + [self.swap(value, flip) for flip in self.flips], axis=0)

    def gather_ctx(self, value):
        near = self.gather_near(value)
        return (near, self.swap(near, 1))

    def reduce_ctx(self, near, far):
        total = (near.astype(F32) + self.swap(far, 1).astype(F32)).astype(BF)
        return self.reduce_chips(total)

    def reduce_chips(self, total):
        blocks = total.reshape((self.nc // 2, -1) + total.shape[1:])
        half = blocks.shape[1] // 2
        outs = []
        for color in (0, 1):
            part = blocks[:, color * half : (color + 1) * half]
            held = list(range(self.nc // 2))
            for bit in self.bits[::-1] if color == 0 else self.bits:
                keep = np.array([n for n, h in enumerate(held) if not 2 * h & bit])
                send = np.array([n for n, h in enumerate(held) if 2 * h & bit])
                other = self.swap(jnp.stack([part[n] for n in send]), bit)
                part = (jnp.stack([part[n] for n in keep]).astype(F32) + other.astype(F32)).astype(BF)
                held = [held[n] for n in keep]
            outs.append(part[0])
        return jnp.concatenate(outs, axis=0)

    def reduce_ring(self, parts):
        total = parts(1)
        for step in list(range(2, self.nz)) + [0]:
            total = (self.ring_step(total).astype(F32) + parts(step).astype(F32)).astype(BF)
        return total

    def arrival(self):
        flips = np.array([2 * n + core for core in (0, 1) for n in range(self.nc // 2)], np.int32)
        return jnp.asarray(flips) ^ self.cx

    def arrival_place(self):
        flips = jnp.arange(self.nc) ^ self.cx
        return (flips % 2) * (self.nc // 2) + flips // 2

    def head_blocks(self, value):
        rows = value.shape[0]
        split = value.reshape(rows, self.group, self.hpd, self.nc // self.group, HEAD_DIM)
        return split.transpose(3, 1, 0, 2, 4).reshape(self.nc, rows, self.cols)

    def head_rows(self, value):
        rows = value.shape[1]
        split = value.reshape(self.nc // self.group, self.group, rows, self.hpd, HEAD_DIM)
        return split.transpose(2, 1, 3, 0, 4).reshape(rows, self.nc * self.cols)

    def head_at(self, device, n):
        return ((device % self.group) * self.hpd + n) * (self.nc // self.group) + device // self.group

    def weight_rows(self, grads, weights):
        count, rows = len(weights), weights[0].shape[0]
        width = weights[0].shape[1]

        def kernel(grads, *refs):
            sums = 0.0
            for device in range(self.nc):
                for w in range(count):
                    for n in range(self.hpd):
                        head = slice(self.head_at(device, n) * HEAD_DIM, (self.head_at(device, n) + 1) * HEAD_DIM)
                        start = w * self.cols + n * HEAD_DIM
                        part = grads[device, :, start : start + HEAD_DIM].astype(F32)
                        refs[count + w][:, head] = part
                        sums += part * refs[w][:, head].astype(F32)
            refs[-1][...] = as_row(jnp.sum(sums, axis=-1, keepdims=True))

        shape = jax.ShapeDtypeStruct((rows, width), F32)
        return pl.pallas_call(
            kernel,
            out_shape=[shape] * count + [jax.ShapeDtypeStruct((1, rows), F32)],
            compiler_params=pltpu.CompilerParams(vmem_limit_bytes=24 * 2**20),
        )(grads, *weights)

    def own_heads(self, vector):
        return self.head_blocks(vector[None])[self.cx, 0]

    def all_heads(self, vector):
        whole = jnp.zeros((self.nc, 1, self.cols), vector.dtype)
        whole = lax.dynamic_update_slice(whole, vector[None, None], (self.cx, 0, 0))
        return self.head_rows(whole)[0]


def sync(*values):
    return lax.optimization_barrier(values)


def after(value, *deps):
    return lax.optimization_barrier((value,) + deps)[0]


def a2a(value, axes):
    return lax.all_to_all(value, axes, split_axis=0, concat_axis=0, tiled=True)


def column(row):
    return jnp.broadcast_to(row, (row.shape[1], row.shape[1])).T[:, :1]


def as_row(col):
    return jnp.broadcast_to(col, (col.shape[0], col.shape[0])).T[:1]


def lane_pick(notes, *lanes):
    lane = lax.broadcasted_iota(jnp.int32, notes.shape, 1)
    keep = functools.reduce(jnp.logical_or, [lane == n for n in lanes])
    return jnp.sum(jnp.where(keep, notes.astype(F32), 0.0), axis=-1, keepdims=True)


def pick_kernel(capacity, count, expert_ref, block, *outs):
    rows = block.shape[0]
    width = outs[0].shape[1]
    start = block.shape[1] - NOTES
    before = lax.broadcasted_iota(jnp.int32, (rows, rows), 0) < lax.broadcasted_iota(jnp.int32, (rows, rows), 1)
    before = jnp.where(before, 1.0, 0.0).astype(BF)
    for n in range(count):
        named = lane_pick(block[:, start:], expert_ref[n])
        named = jnp.broadcast_to(named, (rows, rows)).T[:capacity]
        slot = dot(named.astype(BF), before)
        mine = lax.broadcasted_iota(jnp.int32, slot.shape, 0).astype(F32)
        choose = jnp.where((slot == mine) & (named > 0.5), 1.0, 0.0).astype(BF)
        picked = dot(choose, block[:, :width]).astype(BF)
        if len(outs) == 1:
            outs[0][n * capacity : (n + 1) * capacity] = picked
        else:
            outs[n][...] = picked


def pick_rows(block, experts, capacity, width, joined):
    rows, wide = block.shape
    count = experts.shape[0]
    shapes = [(count * capacity, width)] if joined else [(capacity, width)] * count
    return pl.pallas_call(
        functools.partial(pick_kernel, capacity, count),
        grid_spec=pltpu.PrefetchScalarGridSpec(
            num_scalar_prefetch=1,
            grid=(1,),
            in_specs=[pl.BlockSpec((rows, wide), lambda n, experts: (0, 0))],
            out_specs=[pl.BlockSpec(shape, lambda n, experts: (0, 0)) for shape in shapes],
        ),
        out_shape=[jax.ShapeDtypeStruct(shape, BF) for shape in shapes],
        compiler_params=pltpu.CompilerParams(vmem_limit_bytes=24 * 2**20),
        cost_estimate=pl.CostEstimate(
            flops=2 * count * rows * capacity * width, bytes_accessed=4 * count * rows * width, transcendentals=0
        ),
    )(experts, block)


def spread_kernel(capacity, has_sum, expert_ref, notes, *refs):
    out = refs[-1]
    parts = refs[: -2 if has_sum else -1]
    rows = notes.shape[0]
    after_it = lax.broadcasted_iota(jnp.int32, (rows, rows), 1) < lax.broadcasted_iota(jnp.int32, (rows, rows), 0)
    after_it = jnp.where(after_it, 1.0, 0.0).astype(BF)
    total = refs[-2][...].astype(F32) if has_sum else 0.0
    n = 0
    for part in parts:
        for place in range(0, part.shape[0], capacity):
            named = jnp.broadcast_to(lane_pick(notes[...], expert_ref[n]), (rows, capacity))
            slot = dot(after_it, named.astype(BF))
            mine = lax.broadcasted_iota(jnp.int32, slot.shape, 1).astype(F32)
            choose = jnp.where((slot == mine) & (named > 0.5), 1.0, 0.0).astype(BF)
            total += dot(choose, part[place : place + capacity])
            n += 1
    out[...] = total.astype(BF)


def spread_rows(block, experts, parts, total, capacity):
    rows = block.shape[0]
    width = parts[0].shape[1]
    place = block.shape[1] // NOTES - 1
    row = pl.BlockSpec((rows, width), lambda n, experts: (0, 0))
    return pl.pallas_call(
        functools.partial(spread_kernel, capacity, total is not None),
        grid_spec=pltpu.PrefetchScalarGridSpec(
            num_scalar_prefetch=1,
            grid=(1,),
            in_specs=[pl.BlockSpec((rows, NOTES), lambda n, experts: (0, place))]
            + [pl.BlockSpec(p.shape, lambda n, experts: (0, 0)) for p in parts]
            + ([row] if total is not None else []),
            out_specs=row,
        ),
        out_shape=jax.ShapeDtypeStruct((rows, width), BF),
        compiler_params=pltpu.CompilerParams(vmem_limit_bytes=24 * 2**20),
        cost_estimate=pl.CostEstimate(
            flops=8 * rows * rows * width, bytes_accessed=16 * rows * width, transcendentals=0
        ),
    )(experts, block, *parts, *([total] if total is not None else []))


def expert_kernel(
    kinds, expert_ref, near, far, dy_near, dy_far, gate_w, up_w, down_w,
    out_near, out_far, grad_near, grad_far, hidden_near, hidden_far, gate_near, gate_far, up_near, up_far,
):
    tile = near.shape[0]
    width = dy_near.shape[1]
    expert = expert_ref[0]
    rows = jnp.concatenate([near[:, :width], far[:, :width]], axis=0)
    notes = jnp.concatenate([near[:, width:], far[:, width:]], axis=0)
    dy = jnp.concatenate([dy_near[...], dy_far[...]], axis=0)
    gate_col = lane_pick(notes, expert + kinds, expert + 2 * kinds)
    gate_pre = dot(rows, gate_w[...])
    up_pre = dot(rows, up_w[...])
    sigmoid_val = jax.nn.sigmoid(gate_pre)
    silu = gate_pre * sigmoid_val
    hidden_f = silu * up_pre
    out = (dot(hidden_f.astype(BF), down_w[...]) * gate_col).astype(BF)
    out_near[...] = out[:tile]
    out_far[...] = out[tile:]
    grad_hidden = times_transposed(dy, down_w[...])
    weighted = jnp.sum(grad_hidden * hidden_f, axis=-1, keepdims=True) * gate_col
    lane = lax.broadcasted_iota(jnp.int32, (2 * tile, NOTES), 1)
    weighted = jnp.where(lane == expert, weighted, 0.0).astype(BF)
    grad_near[:, width:] = weighted[:tile]
    grad_far[:, width:] = weighted[tile:]
    grad_hidden = grad_hidden * gate_col
    grad_gate_pre = (
        grad_hidden * up_pre * (sigmoid_val * (1.0 + gate_pre * (1.0 - sigmoid_val)))
    ).astype(BF)
    grad_up_pre = (grad_hidden * silu).astype(BF)
    hidden = (hidden_f * gate_col).astype(BF)
    hidden_near[...] = hidden[:tile]
    hidden_far[...] = hidden[tile:]
    gate_near[...] = grad_gate_pre[:tile]
    gate_far[...] = grad_gate_pre[tile:]
    up_near[...] = grad_up_pre[:tile]
    up_far[...] = grad_up_pre[tile:]
    grad = (
        times_transposed(grad_gate_pre, gate_w[...]) + times_transposed(grad_up_pre, up_w[...])
    ).astype(BF)
    grad_near[:, :width] = grad[:tile]
    grad_far[:, :width] = grad[tile:]


def expert_chunk(kinds, expert, near, far, dy_near, dy_far, gate_w, up_w, down_w, tile=128):
    rows, width = dy_near.shape
    units = gate_w.shape[1]

    def row(cols):
        return pl.BlockSpec((tile, cols), lambda i, expert: (i, 0))

    def whole(array):
        return pl.BlockSpec(array.shape, lambda i, expert: (0, 0), pipeline_mode=pl.Buffered(1))

    def shape(cols):
        return jax.ShapeDtypeStruct((rows, cols), BF)

    wide = near.shape[1]
    outs = [width, width, wide, wide] + [units] * 6
    return pl.pallas_call(
        functools.partial(expert_kernel, kinds),
        grid_spec=pltpu.PrefetchScalarGridSpec(
            num_scalar_prefetch=1,
            grid=(rows // tile,),
            in_specs=[row(wide), row(wide), row(width), row(width), whole(gate_w), whole(up_w), whole(down_w)],
            out_specs=[row(cols) for cols in outs],
        ),
        out_shape=[shape(cols) for cols in outs],
        compiler_params=pltpu.CompilerParams(vmem_limit_bytes=56 * 2**20),
        cost_estimate=pl.CostEstimate(
            flops=24 * rows * width * units,
            bytes_accessed=16 * rows * width,
            transcendentals=2 * rows * units,
        ),
    )(expert, near, far, dy_near, dy_far, gate_w, up_w, down_w)


def contract_kernel(count, *refs):
    total = 0.0
    for left, right in zip(refs[:count], refs[count:-1]):
        total += contract_rows(left[...], right[...])
    refs[-1][...] = total


def contract_many(lefts, rights, rows, cols, tile=256):
    count = len(lefts)
    depth = lefts[0].shape[0]
    tall = rows >= cols
    strip = pl.BlockSpec((depth, tile), lambda i: (0, i))
    held = pl.BlockSpec((depth, min(rows, cols)), lambda i: (0, 0), pipeline_mode=pl.Buffered(1))
    return pl.pallas_call(
        functools.partial(contract_kernel, count),
        grid=(max(rows, cols) // tile,),
        in_specs=[strip if tall else held] * count + [held if tall else strip] * count,
        out_specs=pl.BlockSpec((tile, cols), lambda i: (i, 0)) if tall else pl.BlockSpec((rows, tile), lambda i: (0, i)),
        out_shape=jax.ShapeDtypeStruct((rows, cols), F32),
        compiler_params=pltpu.CompilerParams(vmem_limit_bytes=56 * 2**20),
        cost_estimate=pl.CostEstimate(
            flops=2 * depth * count * rows * cols,
            bytes_accessed=2 * depth * count * (rows + cols) + 4 * rows * cols,
            transcendentals=0,
        ),
    )(*lefts, *rights)


def columns(rows):
    count = rows.shape[1] // 128
    return jnp.concatenate([column(rows[:, n * 128 : (n + 1) * 128]) for n in range(count)], axis=0)


def as_rows(cols):
    count = cols.shape[0] // 128
    return jnp.concatenate([as_row(cols[n * 128 : (n + 1) * 128]) for n in range(count)], axis=1)


def norm_kernel(place_ref, near, far, gain, out):
    n = pl.program_id(0)
    steps = pl.num_programs(0)
    rows = jnp.where(place_ref[n] < steps // 2, near[...], far[...]).astype(F32)
    out[...] = (rows * inverse_rms(rows) * gain[...]).astype(BF)


def norm_in_order(place, near, far, gain, half):
    steps = place.shape[0]
    width = near.shape[1]
    return pl.pallas_call(
        norm_kernel,
        grid_spec=pltpu.PrefetchScalarGridSpec(
            num_scalar_prefetch=1,
            grid=(steps,),
            in_specs=[
                pl.BlockSpec((half, width), lambda n, place: (jnp.minimum(place[n], steps // 2 - 1), 0)),
                pl.BlockSpec((half, width), lambda n, place: (jnp.maximum(place[n] - steps // 2, 0), 0)),
                pl.BlockSpec((1, width), lambda n, place: (0, 0)),
            ],
            out_specs=pl.BlockSpec((half, width), lambda n, place: (n, 0)),
        ),
        out_shape=jax.ShapeDtypeStruct((steps * half, width), BF),
        compiler_params=pltpu.CompilerParams(vmem_limit_bytes=16 * 2**20),
        cost_estimate=pl.CostEstimate(
            flops=4 * steps * half * width, bytes_accessed=6 * steps * half * width, transcendentals=0
        ),
    )(place, near, far, gain)


def project_kernel(count, cols, layer_ref, rows, *refs):
    total = 0.0
    for n in range(count):
        depth = refs[n].shape[0]
        start = pl.multiple_of(layer_ref[n] * depth, depth)
        total += dot(rows[:, pl.ds(start, depth)], refs[n][...])
    out, squares = refs[count:]
    out[...] = total
    for n in range(2):
        part = total[:, n * cols : (n + 1) * cols]
        squares[n : n + 1] = as_rows(jnp.sum(part * part, axis=-1, keepdims=True))


def project(layers, rows, weights, cols, tile=256):
    count = len(weights)
    total, width = rows.shape
    wide = weights[0].shape[1]
    held = pl.BlockSpec(weights[0].shape, lambda n, layers: (0, 0), pipeline_mode=pl.Buffered(1))
    return pl.pallas_call(
        functools.partial(project_kernel, count, cols),
        grid_spec=pltpu.PrefetchScalarGridSpec(
            num_scalar_prefetch=1,
            grid=(total // tile,),
            in_specs=[pl.BlockSpec((tile, width), lambda n, layers: (n, 0))] + [held] * count,
            out_specs=[
                pl.BlockSpec((tile, wide), lambda n, layers: (n, 0)),
                pl.BlockSpec((2, tile), lambda n, layers: (0, n)),
            ],
        ),
        out_shape=[jax.ShapeDtypeStruct((total, wide), F32), jax.ShapeDtypeStruct((2, total), F32)],
        compiler_params=pltpu.CompilerParams(vmem_limit_bytes=40 * 2**20),
        cost_estimate=pl.CostEstimate(
            flops=2 * total * width * wide, bytes_accessed=2 * total * width + 6 * total * wide, transcendentals=0
        ),
    )(layers, rows, *weights)


def project_back_kernel(count, half, layer_ref, block_ref, grads, *refs):
    near, far = refs[count:]
    step = pl.program_id(0)
    blocks = near.shape[0] // half
    for side, out in enumerate((near, far)):
        first = (side * pl.num_programs(0) + step) * blocks
        rows = jnp.concatenate(
            [grads[pl.ds(pl.multiple_of(block_ref[first + n] * half, half), half)] for n in range(blocks)], axis=0
        )
        for n in range(count):
            depth = refs[n].shape[0]
            start = pl.multiple_of(layer_ref[n] * depth, depth)
            out[:, pl.ds(start, depth)] = times_transposed(rows, refs[n][...]).astype(BF)


def project_back(layers, blocks, grads, weights, half, tile=256):
    count = len(weights)
    total, wide = grads.shape
    width = count * weights[0].shape[0]
    held = pl.BlockSpec(weights[0].shape, lambda n, *refs: (0, 0), pipeline_mode=pl.Buffered(1))
    out = jax.ShapeDtypeStruct((total // 2, width), BF)
    return pl.pallas_call(
        functools.partial(project_back_kernel, count, half),
        grid_spec=pltpu.PrefetchScalarGridSpec(
            num_scalar_prefetch=2,
            grid=(total // 2 // tile,),
            in_specs=[pl.BlockSpec((total, wide), lambda n, *refs: (0, 0), pipeline_mode=pl.Buffered(1))]
            + [held] * count,
            out_specs=[pl.BlockSpec((tile, width), lambda n, *refs: (n, 0))] * 2,
        ),
        out_shape=[out, out],
        compiler_params=pltpu.CompilerParams(vmem_limit_bytes=40 * 2**20),
        cost_estimate=pl.CostEstimate(
            flops=2 * total * width * wide, bytes_accessed=2 * total * (width + wide), transcendentals=0
        ),
    )(layers, blocks, grads, *weights)


def turn(value, cosine, sine):
    return value * cosine + pltpu.roll(value, HEAD_DIM // 2, 1) * sine


def half_blocks(rows, half):
    count = rows // half
    return [(2 * n if n < count // 2 else 2 * (count - 1 - n) + 1) * half for n in range(count)]


def masked_scores(queries, keys, first, score_scale):
    scores = times_transposed(queries, keys) * score_scale
    row = lax.broadcasted_iota(jnp.int32, scores.shape, 0) + first
    col = lax.broadcasted_iota(jnp.int32, scores.shape, 1)
    return scores, col <= row


def attention_kernel(
    half, tile, score_scale, q_pre, k_pre, v_pre, inv, gains, cosine, sine,
    sent, attended, lse, query_rot, key_rot, value,
):
    rows = q_pre.shape[0]
    cos, sin = cosine[...], sine[...]
    query_rot[...] = turn(q_pre[...] * columns(inv[0:1]) * gains[0:1], cos, sin).astype(BF)
    key_rot[...] = turn(k_pre[...] * columns(inv[1:2]) * gains[1:2], cos, sin).astype(BF)
    value[...] = v_pre[...].astype(BF)
    for n in range(rows // tile):
        first = n * tile
        end = first + tile
        scores, allowed = masked_scores(query_rot[first:end], key_rot[:end], first, score_scale)
        scores = jnp.where(allowed, scores, NEG_LARGE)
        top = jnp.max(scores, axis=-1, keepdims=True)
        probs = jnp.exp(scores - top)
        total = jnp.sum(probs, axis=-1, keepdims=True)
        lse[first:end] = jnp.broadcast_to(top + jnp.log(total), (tile, HEAD_DIM))
        attended[first:end] = dot((probs / total).astype(BF), value[:end])
    for n, place in enumerate(half_blocks(rows, half)):
        sent[place : place + half] = attended[n * half : (n + 1) * half].astype(BF)


def attention_grad_kernel(
    half, tile, score_scale, sent_grad, attended, lse, query_rot, key_rot, value, q_pre, k_pre, inv, gains,
    cosine, sine, scaled_q, scaled_k, grad_value, dots, grad_gains, grad_heads, key_sum, value_sum, query_sum,
):
    rows = q_pre.shape[0]
    for n, place in enumerate(half_blocks(rows, half)):
        grad_heads[n * half : (n + 1) * half] = sent_grad[place : place + half]
    key_sum[...] = jnp.zeros_like(key_sum)
    value_sum[...] = jnp.zeros_like(value_sum)
    for n in range(rows // tile):
        first = n * tile
        end = first + tile
        grads = grad_heads[first:end]
        queries = query_rot[first:end]
        delta = jnp.sum(grads.astype(F32) * attended[first:end], axis=-1, keepdims=True)
        scores, allowed = masked_scores(queries, key_rot[:end], first, score_scale)
        probs = jnp.where(allowed, jnp.exp(scores - lse[first:end][:, :1]), 0.0)
        grad_scores = (probs * (times_transposed(grads, value[:end]) - delta)).astype(BF)
        query_sum[first:end] = dot(grad_scores, key_rot[:end])
        key_sum[:end] += contract_rows(grad_scores, queries)
        value_sum[:end] += contract_rows(probs.astype(BF), grads)
    grad_value[...] = value_sum[...].astype(BF)
    cos, sin = cosine[...], -sine[...]
    for n, (total, pre, scaled) in enumerate(((query_sum, q_pre, scaled_q), (key_sum, k_pre, scaled_k))):
        grad = turn(total[...] * score_scale, cos, sin)
        grad_gains[n : n + 1] = jnp.sum(grad * pre[...] * columns(inv[n : n + 1]), axis=0, keepdims=True)
        grad = grad * gains[n : n + 1]
        scaled[...] = grad
        dots[n : n + 1] = as_rows(jnp.sum(grad * pre[...], axis=-1, keepdims=True))


class Attention:
    def __init__(self, rows, half, hpd):
        self.rows, self.half, self.hpd = rows, half, hpd
        self.tile = min(256, rows)
        position = np.arange(rows, dtype=np.float32)
        freq = np.exp(np.arange(HEAD_DIM // 2, dtype=np.float32) * np.float32(-2.0 * math.log(10000.0) / HEAD_DIM))
        angles = position[:, None] * freq[None, :].astype(np.float32)
        self.cosine = jnp.asarray(np.concatenate([np.cos(angles)] * 2, axis=1), F32)
        self.sine = jnp.asarray(np.concatenate([-np.sin(angles), np.sin(angles)], axis=1), F32)
        self.head = pl.BlockSpec((rows, HEAD_DIM), lambda h: (0, h))
        self.keys = pl.BlockSpec((rows, HEAD_DIM), lambda h: (0, h + hpd))
        self.values = pl.BlockSpec((rows, HEAD_DIM), lambda h: (0, h + 2 * hpd))
        self.stat = pl.BlockSpec((2, rows), lambda h: (0, 0))
        self.gain = pl.BlockSpec((2, HEAD_DIM), lambda h: (0, h))
        self.table = pl.BlockSpec((rows, HEAD_DIM), lambda h: (0, 0))
        self.args = (half, self.tile, 1.0 / math.sqrt(HEAD_DIM))
        self.params = pltpu.CompilerParams(vmem_limit_bytes=48 * 2**20)

    def shape(self, dtype):
        return jax.ShapeDtypeStruct((self.rows, self.hpd * HEAD_DIM), dtype)

    def cost(self, products):
        area = self.hpd * self.rows * self.rows
        return pl.CostEstimate(
            flops=products * area * HEAD_DIM, bytes_accessed=self.hpd * self.rows * HEAD_DIM * 24, transcendentals=area
        )

    def forward(self, qkv, inv, gains):
        return pl.pallas_call(
            functools.partial(attention_kernel, *self.args),
            grid=(self.hpd,),
            in_specs=[self.head, self.keys, self.values, self.stat, self.gain, self.table, self.table],
            out_specs=[self.head] * 6,
            out_shape=[self.shape(t) for t in (BF, F32, F32, BF, BF, BF)],
            compiler_params=self.params,
            cost_estimate=self.cost(3),
        )(qkv, qkv, qkv, inv, gains, self.cosine, self.sine)

    def backward(self, sent_grad, kept, qkv, inv, gains):
        rows, hpd = self.rows, self.hpd
        line = pl.BlockSpec((None, 2, rows), lambda h: (h, 0, 0))
        return pl.pallas_call(
            functools.partial(attention_grad_kernel, *self.args),
            grid=(hpd,),
            in_specs=[self.head] * 6 + [self.head, self.keys, self.stat, self.gain, self.table, self.table],
            out_specs=[self.head] * 3 + [line, self.gain],
            out_shape=[self.shape(F32), self.shape(F32), self.shape(BF)]
            + [jax.ShapeDtypeStruct((hpd, 2, rows), F32), jax.ShapeDtypeStruct((2, hpd * HEAD_DIM), F32)],
            scratch_shapes=[pltpu.VMEM((rows, HEAD_DIM), BF)] + [pltpu.VMEM((rows, HEAD_DIM), F32)] * 3,
            compiler_params=self.params,
            cost_estimate=self.cost(6),
        )(sent_grad, *kept, qkv, qkv, inv, gains, self.cosine, self.sine)


class Gathered:
    def __init__(self, lay, routes, expert_count, capacity, width):
        self.lay, self.kinds, self.capacity, self.width = lay, expert_count, capacity, width
        self.tok_rows = routes.shape[0]
        chosen = routes[:, :, None] == jnp.arange(expert_count, dtype=jnp.int32)
        self.chosen = jnp.any(chosen, axis=1)
        first = lay.dz * (lay.nc // 2)
        flipped = first + (lay.cx ^ jnp.array([0] + lay.flips, jnp.int32)) // 2
        self.flipped = flipped.astype(jnp.int32)
        self.own = self.flipped[:1]
        self.straight = (first + jnp.arange(lay.nc // 2)).astype(jnp.int32)

    def experts(self, step):
        return self.straight if step else self.flipped

    def noted(self, rows, *notes):
        notes = [self.chosen.astype(BF)] + list(notes)
        rest = NOTES - self.kinds * len(notes)
        return jnp.concatenate([rows] + notes + [jnp.zeros((self.tok_rows, rest), BF)], axis=1)

    def offer(self, step, block, width=None):
        return pick_rows(block, self.experts(step), self.capacity, width or block.shape[1], step > 0)

    def exchange(self, parts):
        if len(parts) > 1:
            return [parts[0]] + [self.lay.swap(p, flip) for p, flip in zip(parts[1:], self.lay.flips)]
        groups = [list(range(core, self.lay.nc, 2)) for core in (0, 1)]
        return [
            lax.all_to_all(parts[0], "ctx", split_axis=0, concat_axis=0, tiled=True, axis_index_groups=groups)
        ]

    def joined(self, parts):
        return jnp.concatenate(parts, axis=0) if len(parts) > 1 else parts[0]

    def give_back(self, step, near, far):
        sums = (near.astype(F32) + far.astype(F32)).astype(BF)
        if step:
            return self.exchange([sums])
        count = len(self.lay.flips) + 1
        return self.exchange([sums[n * self.capacity : (n + 1) * self.capacity] for n in range(count)])

    def spread(self, step, parts, total):
        return spread_rows(self.blocks[step], self.experts(step), parts, total, self.capacity)

    def run(self, block, dy, gate_w, up_w, down_w):
        lay, nz = self.lay, self.lay.nz
        self.blocks = blocks = [block]
        self.rows, self.done, self.dy = rows, done, dy = [], [], dy
        back, far_grads = {}, {}
        parts = self.exchange(self.offer(0, block))
        coming = lay.ring_step(block)
        coming, *parts = sync(coming, *parts)
        for step in range(nz):
            near = self.joined(parts)
            far = lay.swap(near, 1)
            if step:
                far_grads[step - 1] = lay.swap(done[-1][3], 1)
            if step + 1 < nz:
                blocks.append(coming)
                parts = self.exchange(self.offer(step + 1, coming))
                if step + 2 < nz:
                    coming = lay.ring_step(coming)
            for pair in dy[step + 1 : step + 2]:
                if len(pair) == 1:
                    pair.append(lay.swap(pair[0], 1))
            if step > 1:
                far, far_grads[step - 2] = sync(far, far_grads[step - 2])
                back[step - 2] = self.give_back(step - 2, done[step - 2][2], far_grads[step - 2])
            rows += [near, far]
            made = list(expert_chunk(self.kinds, self.own, near, far, *dy[step], gate_w, up_w, down_w))
            held = [made[3], coming] + (list(parts) if step + 1 < nz else [])
            if step:
                held.append(far_grads[step - 1])
            held = list(sync(*held))
            made[3], coming = held[:2]
            if step + 1 < nz:
                parts = held[2 : 2 + len(parts)]
            if step:
                far_grads[step - 1] = held[-1]
            done.append(made)
        last = nz - 1
        far_grads[last] = lay.swap(done[last][3], 1)
        back[last - 1] = self.give_back(last - 1, done[last - 1][2], far_grads[last - 1])
        far_outs = [lay.swap(after(d[1], done[last][3]), 1) for d in done]
        self.outs = [(d[0], other) for d, other in zip(done, far_outs)]
        total = None
        for step in list(range(1, nz)) + [0]:
            if total is not None:
                total = lay.ring_step(total)
            if step == last - 1:
                total, far_grads[last], *back[step] = sync(total, far_grads[last], *back[step])
                back[last] = self.give_back(last, done[last][2], far_grads[last])
            elif step == last:
                total, *back[step] = sync(total, *back[step])
            total = self.spread(step, back[step], total)
        total = total.astype(F32)
        self.tail = back[last][-1]
        return total[:, : self.width], total[:, self.width : self.width + self.kinds]

    def mixture_parts(self, step, dep):
        near, far = self.outs[step]
        return self.give_back(step, near, after(far, dep))

    def weight_grads(self, which, dep):
        near = 4 + 2 * which
        mids = [after(d[k], dep) for d in self.done for k in (near, near + 1)]
        units = mids[0].shape[1]
        if which == 0:
            return contract_many(mids, [d for pair in self.dy for d in pair], units, self.width)
        return contract_many(self.rows, mids, self.width, units)


def experts_sent(lay, mlp_normed, routes, router_probs, grad_result, gate_w, up_w, down_w):
    tok_rows, width = mlp_normed.shape
    expert_count = router_probs.shape[1]
    capacity = 3 * tok_rows * TOP // (2 * expert_count)
    flat_routes = routes.reshape(tok_rows * TOP)
    onehot = (flat_routes[:, None] == jnp.arange(expert_count, dtype=jnp.int32)[None, :]).astype(
        jnp.int32
    )
    slot_index = jnp.sum((jnp.cumsum(onehot, axis=0) - onehot) * onehot, axis=1)
    chosen = onehot.reshape(tok_rows, TOP, expert_count).astype(F32)
    gate_values = jnp.einsum("tke,te->tk", chosen, router_probs)

    def dispatch(rows_in):
        sent = jnp.zeros((expert_count, capacity, width), BF).at[flat_routes, slot_index].set(rows_in)
        return a2a(jnp.repeat(sent, 2, axis=0), ALL)

    def collect(buffer):
        even_rows = buffer[2 * flat_routes, slot_index].astype(F32)
        odd_rows = buffer[2 * flat_routes + 1, slot_index].astype(F32)
        return (even_rows + odd_rows).reshape(tok_rows, TOP, width)

    received = dispatch(jnp.repeat(mlp_normed, TOP, axis=0))
    flat_in = received.reshape(-1, width)
    gate_pre = dot(flat_in, gate_w)
    up_pre = dot(flat_in, up_w)
    hidden = (jax.nn.silu(gate_pre) * up_pre).astype(BF)
    half_out = dot(hidden, down_w).astype(BF).reshape(received.shape)
    expert_rows = collect(a2a(half_out, ALL))
    mixture = jnp.einsum("tk,tkd->td", gate_values, expert_rows)
    grad_gates = jnp.einsum("td,tkd->tk", grad_result, expert_rows)
    grad_rows = (
        (gate_values[:, :, None] * grad_result[:, None, :])
        .astype(BF)
        .reshape(tok_rows * TOP, width)
    )
    grad_flat = dispatch(grad_rows).reshape(-1, width)
    grad_down_w = contract_rows(hidden, grad_flat)
    grad_hidden = times_transposed(grad_flat, down_w)
    sigmoid_val = jax.nn.sigmoid(gate_pre)
    grad_gate_pre = (
        grad_hidden * up_pre * sigmoid_val * (1.0 + gate_pre * (1.0 - sigmoid_val))
    ).astype(BF)
    grad_up_pre = (grad_hidden * jax.nn.silu(gate_pre)).astype(BF)
    grad_gate_w = contract_rows(flat_in, grad_gate_pre)
    grad_up_w = contract_rows(flat_in, grad_up_pre)
    grad_copy = (
        (times_transposed(grad_gate_pre, gate_w) + times_transposed(grad_up_pre, up_w))
        .astype(BF)
        .reshape(received.shape)
    )
    grad_sum = jnp.sum(collect(a2a(grad_copy, ALL)), axis=1)
    weighted = router_probs * jnp.einsum("tk,tke->te", grad_gates, chosen)
    return (mixture, grad_sum, weighted, lambda which, dep: (grad_down_w, grad_gate_w, grad_up_w)[which])


def body(
    tokens,
    routes,
    cotangent,
    attn_gain,
    query_weight,
    key_weight,
    value_weight,
    query_gain,
    key_gain,
    out_weight,
    mlp_gain,
    router_weight,
    gate_weight,
    up_weight,
    down_weight,
):
    rb = query_weight.shape[0]
    lay = Layout(rb)
    nz, nc, cx = lay.nz, lay.nc, lay.cx
    tok_rows = tokens.shape[1]
    width = tokens.shape[2]
    half = tok_rows // 2
    seq_rows = tok_rows * nc
    expert_count = router_weight.shape[1]
    hpd, cols = lay.hpd, lay.cols
    devices = nz * nc
    capacity = 3 * tok_rows * TOP // (2 * expert_count)
    gathered = (
        devices * tok_rows <= 4 * expert_count * capacity and 3 * expert_count <= NOTES and capacity % 16 == 0
    )

    sent = jnp.concatenate(
        [lay.head_blocks(w) for w in (query_weight, key_weight, value_weight)], axis=-1
    )
    kinds = expert_count + 4
    small = jnp.concatenate(
        [router_weight] + [g[:, None] for g in (attn_gain, query_gain, key_gain, mlp_gain)], axis=1
    )
    small = jnp.broadcast_to(small.T.reshape(1, kinds * rb), (devices, kinds * rb))
    block = a2a(sent, "ctx").reshape(nc * rb, 3 * cols)
    parts = [tokens[0]] + [lay.swap(tokens[0], flip) for flip in lay.flips]
    if gathered:
        moe = Gathered(lay, routes[0], expert_count, capacity, width)
        dy_blocks = [moe.noted(cotangent[0])]
        dy_blocks.append(lay.ring_step(dy_blocks[0]))
        block, dy_blocks[1] = sync(block, dy_blocks[1])
    ring = [block]
    for step in range(1, nz):
        block = lay.ring_step(block)
        beside = []
        if step == 1:
            small = a2a(small, ALL)
            beside = [small] + parts[1:]
        elif step == 2:
            seq_near = jnp.concatenate(parts, axis=0)
            seq_far = lay.swap(seq_near, 1)
            beside = [seq_far]
            if gathered:
                dy0 = moe.exchange(moe.offer(0, after(dy_blocks[0], ring[-1]), width))
                beside += dy0[1:]
        elif step == 3:
            small = small.reshape(devices, kinds, rb).transpose(1, 0, 2).reshape(kinds, width)
            router_t = small[:expert_count]
            attn_gain_f, qgain_f, kgain_f, mlp_gain_f = (
                small[expert_count + k].astype(F32) for k in range(4)
            )
            places = lay.arrival_place()
            places = jnp.concatenate([places * 2, (places * 2 + 1)[::-1]]).astype(jnp.int32)
            normed = norm_in_order(places, seq_near, seq_far, attn_gain_f[None], half)
            beside = [normed]
            if gathered:
                dy = [[moe.joined(dy0)]]
                dy[0].append(lay.swap(dy[0][0], 1))
                dy1 = moe.exchange(moe.offer(1, after(dy_blocks[1], ring[-1]), width))
                beside += [dy[0][1]] + dy1
        block, *beside = sync(block, *beside)
        if step == 1:
            small, parts[1:] = beside[0], beside[1:]
        elif step == 2:
            seq_far = beside[0]
            if gathered:
                dy0[1:] = beside[1:]
        elif step == 3:
            normed = beside[0]
            if gathered:
                dy[0][1], dy1 = beside[1], beside[2:]
        ring.append(block)
    out_w = lax.all_gather(after(out_weight, ring[2]), ALL, axis=0, tiled=True)
    if gathered:
        dy_blocks.append(lay.ring_step(after(dy_blocks[1], ring[-1])))
    layers = jnp.stack([lay.layer_at(step) for step in range(nz)]).astype(jnp.int32)
    qkv, squares = project(layers, normed, ring, cols)
    query_pre, key_pre = qkv[:, :cols], qkv[:, cols : 2 * cols]

    def sum_heads(stats):
        stats = lax.all_gather(stats.reshape(2 * seq_rows // 128, 128), "ctx", axis=0).sum(0)
        return stats.reshape(2, seq_rows) / width

    inv = lax.rsqrt(sum_heads(squares) + EPSILON)
    own_gains = jnp.stack([lay.own_heads(qgain_f), lay.own_heads(kgain_f)])
    attention = Attention(seq_rows, half, hpd)
    if gathered:
        inv, dy_blocks[2] = sync(inv, dy_blocks[2])
        dy_blocks.append(lay.ring_step(dy_blocks[2]))
        dy.append([moe.joined(dy1)])
        dy.append(moe.exchange(moe.offer(2, dy_blocks[2], width)))
    attended_b, *kept = attention.forward(qkv, inv, own_gains)
    if gathered:
        attended_b, dy_blocks[3], *dy[2] = sync(attended_b, dy_blocks[3], *dy[2])
        for pair in dy[1:3]:
            pair.append(lay.swap(pair[0], 1))
        offered = moe.offer(3, dy_blocks[3], width)
    attended_own = a2a(attended_b.reshape(nc, tok_rows, cols), "ctx")
    if gathered:
        attended_own, dy[1][1], dy[2][1], *offered = sync(attended_own, dy[1][1], dy[2][1], *offered)
        dy.append(moe.exchange(offered))
    attended_own = lay.head_rows(attended_own)
    inputs_f = tokens[0].astype(F32)
    middle = inputs_f + dot(attended_own, out_w)
    mlp_inv = inverse_rms(middle)
    mlp_normed = (middle * mlp_inv * mlp_gain_f).astype(BF)
    router_probs = jax.nn.softmax(times_transposed(mlp_normed, router_t), axis=-1)
    grad_result = cotangent[0].astype(F32)
    if gathered:
        combine = jnp.where(moe.chosen, router_probs, 0.0)
        high = combine.astype(BF)
        mlp_normed, high, *dy[3] = sync(mlp_normed, high, *dy[3])
        block = moe.noted(mlp_normed, high, (combine - high.astype(F32)).astype(BF))
        grad_mlp_normed, weighted = moe.run(
            block, dy, gate_weight[0], up_weight[0], down_weight[0]
        )
        weight_grads = moe.weight_grads
    else:
        mixture, grad_mlp_normed, weighted, weight_grads = experts_sent(
            lay, mlp_normed, routes[0], router_probs, grad_result, gate_weight[0], up_weight[0], down_weight[0]
        )
    grad_logits = (weighted - router_probs * jnp.sum(weighted, axis=-1, keepdims=True)).astype(BF)
    grad_router_t = contract_rows(grad_logits, mlp_normed)
    grad_mlp_normed = grad_mlp_normed + dot(grad_logits, router_t)
    grad_middle_norm, grad_mlp_gain = norm_backward(middle, mlp_inv, mlp_gain_f, grad_mlp_normed)
    grad_middle = grad_result + grad_middle_norm
    grad_branch = grad_middle.astype(BF)
    grad_attended = times_transposed(grad_branch, out_w).astype(BF)
    grad_heads = a2a(lay.head_blocks(grad_attended), "ctx").reshape(seq_rows, cols)

    if gathered:
        mix = {1: moe.mixture_parts(1, moe.tail), 2: moe.mixture_parts(2, grad_heads)}
    scaled_q, scaled_k, grad_value, dots, grad_gains = attention.backward(grad_heads, kept, qkv, inv, own_gains)
    if gathered:
        dots, *mix[1] = sync(dots, *mix[1])
        mixture = lay.ring_step(moe.spread(1, mix[1], None))
    dots = sum_heads(dots.sum(0))

    def through_norm(scaled, pre, n):
        inverse = inv[n][:, None]
        return (inverse * scaled - pre * (inverse * inverse * inverse) * dots[n][:, None]).astype(BF)

    grad_pre = jnp.concatenate(
        [through_norm(scaled_q, query_pre, 0), through_norm(scaled_k, key_pre, 1), grad_value], axis=-1
    )
    grad_qkv = contract_rows(normed, grad_pre).astype(BF)
    layer_rows = nc * rb

    def qkv_part(step):
        return lax.dynamic_slice_in_dim(grad_qkv, lay.layer_at(step) * layer_rows, layer_rows, 0)

    packed = jnp.concatenate(
        [grad_router_t]
        + [g[None] for g in (lay.all_heads(grad_gains[0]), lay.all_heads(grad_gains[1]), grad_mlp_gain)],
        axis=0,
    )
    kinds = expert_count + 3
    packed = packed.reshape(kinds, devices, rb).transpose(1, 0, 2).reshape(devices, kinds * rb)
    packed = a2a(packed, ALL).sum(0).reshape(kinds, rb)
    halves = jnp.stack([lay.arrival(), 2 * nc - 1 - lay.arrival()], axis=1).reshape(-1).astype(jnp.int32)
    branch_all = jnp.concatenate(lay.gather_ctx(after(grad_branch, grad_pre)), axis=0)
    attended_arrival = attended_b.reshape(nc, tok_rows, cols)[lay.arrival()].reshape(seq_rows, cols)
    grad_out = contract_rows(attended_arrival, branch_all).astype(BF).reshape(hpd, lay.group, rb, width)
    share = cx % lay.group
    terms = []
    for k in range(lay.group):
        term = lax.dynamic_index_in_dim(grad_out, share ^ k, 1, keepdims=False)
        terms.append(lay.swap(term, k) if k else term)
    terms = jnp.stack(terms)

    def out_part(step):
        layer = lay.layer_at(step)
        return terms[(layer // hpd) ^ share, layer % hpd]

    total, out_total = qkv_part(1), out_part(1)
    expert_grads = []
    if gathered:
        mix.update({step: moe.mixture_parts(step, grad_pre) for step in (3, 0)})
    for n, step in enumerate(list(range(2, nz)) + [0]):
        total, out_total = lay.ring_step(total), lay.ring_step(out_total)
        beside = []
        if n < 3:
            expert_grads.append(weight_grads(n, total if n else grad_pre))
            beside.append(expert_grads[-1])
        if n == 0:
            near, far = project_back(layers, halves, grad_pre, ring, half)
            beside += [near, far]
            if gathered:
                mixture, *mix[2] = sync(mixture, *mix[2])
                mixture = moe.spread(2, mix[2], mixture)
                beside.append(mixture)
        elif n == 1:
            grad_normed = lay.reduce_ctx(near, far)
            if gathered:
                mixture = lay.ring_step(mixture)
                beside += [mixture] + mix[3]
        elif n == 2 and gathered:
            mixture = lay.ring_step(moe.spread(3, mix[3], mixture))
            beside.append(mixture)
        total, out_total, *beside = sync(total, out_total, *beside)
        if n < 3:
            expert_grads[-1] = beside.pop(0)
        if n == 0:
            near, far = beside[:2]
            if gathered:
                mixture = beside[2]
        elif n == 1 and gathered:
            mixture, mix[3] = beside[0], beside[1:]
        elif n == 2 and gathered:
            mixture = beside[0]
        total = (total.astype(F32) + qkv_part(step).astype(F32)).astype(BF)
        out_total = (out_total.astype(F32) + out_part(step).astype(F32)).astype(BF)
    grad_qkv = a2a(total.reshape(nc, rb, 3 * cols), "ctx")
    grad_out_w = out_total.astype(F32)
    grad_down_w, grad_gate_w, grad_up_w = expert_grads
    if gathered:
        mixture = moe.spread(0, mix[0], mixture).astype(F32)
    result = middle + mixture
    grad_query_w, grad_key_w, grad_value_w, grad_attn_gain = lay.weight_rows(
        grad_qkv, (query_weight, key_weight, value_weight)
    )
    grad_attn_gain = grad_attn_gain[0] / attn_gain.astype(F32)
    attn_inv = inverse_rms(inputs_f)
    grad_inputs_norm, _ = norm_backward(inputs_f, attn_inv, attn_gain_f, grad_normed.astype(F32))
    grad_inputs = grad_middle + grad_inputs_norm
    gains = [grad_attn_gain] + [packed[expert_count + k] for k in range(3)]
    return (
        result.astype(BF)[None],
        grad_inputs.astype(BF)[None],
        gains[0],
        grad_query_w,
        grad_key_w,
        grad_value_w,
        gains[1],
        gains[2],
        grad_out_w,
        gains[3],
        packed[:expert_count].T,
        grad_gate_w[None],
        grad_up_w[None],
        grad_down_w[None],
    )


def solution(mesh):
    both = ("dp", "ctx")
    in_specs = (
        P("dp", "ctx", None),
        P("dp", "ctx", None),
        P("dp", "ctx", None),
        P(both),
        P(both, None),
        P(both, None),
        P(both, None),
        P(both),
        P(both),
        P(both, None),
        P(both),
        P(both, None),
        P(both, None, None),
        P(both, None, None),
        P(both, None, None),
    )
    out_specs = (
        P("dp", "ctx", None),
        P("dp", "ctx", None),
        P(both),
        P(both, None),
        P(both, None),
        P(both, None),
        P(both),
        P(both),
        P(both, None),
        P(both),
        P(both, None),
        P(both, None, None),
        P(both, None, None),
        P(both, None, None),
    )
    return jax.shard_map(body, mesh=mesh, in_specs=in_specs, out_specs=out_specs, check_vma=False)
```

time: 1090 us -> 759 us (0.70)
  Pallas kernels: 0 us -> 196 us
  matrix products: 190 us -> 20.3 us
  local copies, waits for them, and re-layouts: 241 us -> 74.1 us
  waiting for transfers between devices: 325 us -> 203 us
  other arithmetic: 110 us -> 62.3 us
  blocking collectives: 59.6 us -> 40.2 us
  between operations: 34 us -> 16.6 us
  starting transfers between devices: 120 us -> 135 us
    pallas_call x0 -> x29, Pallas kernels: none -> 196 us  [the longest x4 66.9 us: expert_chunk(): pl.pallas_call(functools.partial(expert_kernel, kinds), grid_spec=pltpu.P...]
    ppermute x18 -> x21, waiting for transfers between devices: 152 us -> 70.4 us  [ring_step(): return lax.ppermute(value, 'dp', self.ring)]
    ppermute x91 -> x42, waiting for transfers between devices: 149 us -> 78.2 us  [swap(): return lax.ppermute(value, 'ctx', [(i, i ^ bit) for i in range(self.nc)])]
    gather x30 -> x1, local copies, waits for them, and re-layouts: 70 us -> 1.49 us  [body(): attended_b.reshape(nc, tok_rows, cols)[lay.arrival()]]
    dot_general x6 -> x2, matrix products: 58.2 us -> 5.34 us  [dot(): return jnp.dot(left, right, preferred_element_type=F32)]
    dot_general x6 -> x2, matrix products: 57.8 us -> 6.55 us  [times_transposed(): lax.dot_general(left, right, (((1,), (1,)), ((), ())), preferred_element_...]
    all_to_all x0 -> x12, starting transfers between devices: none -> 49.6 us  [exchange(): lax.all_to_all(parts[0], 'ctx', split_axis=0, concat_axis=0, tiled=True,...]
    ppermute x91 -> x42, starting transfers between devices: 76.2 us -> 31.7 us  [swap(): return lax.ppermute(value, 'ctx', [(i, i ^ bit) for i in range(self.nc)])]
  transfers between devices with their start and end apart: 118 -> 81, of which waited for: 44 -> 29; matrix products, arithmetic and copies ran while one was open for 33% -> 14% of each run, Pallas kernels for 0% -> 26%
where the time goes in v2:
time: 759 us; the launch traced here: 747 us
  waiting for transfers between devices  203 us (27%)
  Pallas kernels  196 us (26%)
  starting transfers between devices  135 us (18%)
  local copies, waits for them, and re-layouts  74.1 us (10%)
  other arithmetic  62.3 us (8%)
  blocking collectives  40.2 us (5%)
  matrix products  20.3 us (3%)
  between operations  16.6 us (2%)
    ppermute x42, waiting for transfers between devices, swap(): return lax.ppermute(value, 'ctx', [(i, i ^ bit) for i in range(self.nc)])  78.2 us
    ppermute x21, waiting for transfers between devices, ring_step(): return lax.ppermute(value, 'dp', self.ring)  70.4 us
    pallas_call x4, Pallas kernels, expert_chunk(): pl.pallas_call(functools.partial(expert_kernel, kinds), grid_spec=pltpu.P...  66.9 us
    unnamed x277, local copies, waits for them, and re-layouts  52.2 us
    all_to_all x12, starting transfers between devices, exchange(): lax.all_to_all(parts[0], 'ctx', split_axis=0, concat_axis=0, tiled=True,...  49.6 us
    pallas_call x3, Pallas kernels, contract_many(): pl.pallas_call(functools.partial(contract_kernel, count), grid=(max(rows,...  44.3 us
    all_to_all x12, waiting for transfers between devices, exchange(): lax.all_to_all(parts[0], 'ctx', split_axis=0, concat_axis=0, tiled=True,...  41.2 us
    ppermute x21, starting transfers between devices, ring_step(): return lax.ppermute(value, 'dp', self.ring)  33 us
  transfers between devices with their start and end apart: 81, of which 29 were waited for; matrix products, arithmetic and copies ran while one was open for 14% of the time, Pallas kernels for 26%

profile of v2, /device:TPU:0, one launch (start us, length us, event | category | flops | bytes accessed | tf_op | source)
XLA Modules:
  0.0 747.0 jit_solution(14105522692806666404)
XLA Ops:
  18.4 14.3 %collective-permute-done.block = bf16[128,2176]{1,0:T(8,128)(2,1)S(1)} collective-permute-done((bf16[128,2176]{1,0:T(8,128)(2,1)S(1)}, bf16[128,2176]{1,0:T(8,128)(2,1)S(1)}, u32[]{:S(2)}, u32[]{:S(2)}) %collective-permute-start) | collective-permute-done | bytes 557088 | tf_op jit(solution)/shard_map/ppermute | solution.py:71
  38.9 20.9 %all_to_all.182 = bf16[32,2,640]{2,1,0:T(2,128)(2,1)S(1)} all-to-all(bf16[32,2,640]{2,1,0:T(2,128)(2,1)S(1)} %reshape.394), channel_id=1, replica_groups=mesh['dp'=4,'ctx'=8] {'dp','ctx'}, dimensions={0} | all-to-all | bytes 163840 | tf_op jit(solution)/shard_map/all_to_all | solution.py:179
  73.6 8.5 %collective-permute-done.7 = bf16[96,2048]{1,0:T(8,128)(2,1)S(1)} collective-permute-done((bf16[96,2048]{1,0:T(8,128)(2,1)S(1)}, bf16[96,2048]{1,0:T(8,128)(2,1)S(1)}, u32[]{:S(2)}, u32[]{:S(2)}) %collective-permute-start.7) | collective-permute-done | bytes 393248 | tf_op jit(solution)/shard_map/ppermute | solution.py:68
  82.1 8.7 %collective-permute-done.8 = bf16[96,2048]{1,0:T(8,128)(2,1)S(1)} collective-permute-done((bf16[96,2048]{1,0:T(8,128)(2,1)S(1)}, bf16[96,2048]{1,0:T(8,128)(2,1)S(1)}, u32[]{:S(2)}, u32[]{:S(2)}) %collective-permute-start.8) | collective-permute-done | bytes 393248 | tf_op jit(solution)/shard_map/ppermute | solution.py:68
  109.1 9.9 %shard_map.309.rows = bf16[1024,2048]{1,0:T(8,128)(2,1)S(1)} custom-call(s32[16]{0:T(128)S(1)} %pad_add_fusion.2.place_ref, bf16[512,2048]{1,0:T(8,128)(2,1)S(1)} %pad_maximum_fusion.near, bf16[512,2048]{1,0:T(8,128)(2,1)} %collective-permute-done.6.far, f32[1,2048]{1,0:T(1,128)S(1)} %reshape.338.gain), custom_call_target="tpu_custom_call" | custom-call | flops 8388608 | bytes 12582912 | tf_op jit(solution)/shard_map/pallas_call | solution.py:402
  129.3 6.9 shard_map.311
  137.8 9.4 %all_gather.9 = f32[8,16,128]{2,1,0:T(8,128)S(1)} all-gather(f32[1,16,128]{2,1,0:T(8,128)S(1)} %all_gather_reshape.6), channel_id=1, replica_groups=mesh['dp'=4,'ctx'=8] {'ctx'}, dimensions={0}, use_global_device_ids=true | all-gather | bytes 73728 | tf_op jit(solution)/shard_map/all_gather | solution.py:884
  147.3 6.4 collective-permute-done.12.block
  162.7 9.9 %shard_map.312 = (bf16[1024,256]{1,0:T(8,128)(2,1)S(1)}, f32[1024,256]{1,0:T(8,128)S(1)}, f32[1024,256]{1,0:T(8,128)S(1)}, bf16[1024,256]{1,0:T(8,128)(2,1)S(1)}...) custom-call(f32[1024,768]{1,0:T(8,128)} %copy-done, f32[1024,768]{1,0:T(8,128)} %copy-done, ...), custom_call_target="tpu_custom_call" | custom-call | flops 805306368 | bytes 6291456 | tf_op jit(solution)/shard_map/pallas_call | solution.py:595
  177.0 6.8 collective-permute-done.13.block
  183.8 7.6 %all-to-all-done.3 = bf16[4,96,2048]{2,1,0:T(8,128)(2,1)} async-done(((bf16[4,96,2048]{2,1,0:T(8,128)(2,1)}), bf16[4,96,2048]{2,1,0:T(8,128)(2,1)}, u32[]{:S(2)}, u32[]{:S(2)}) %all-to-all-start.3) | async-done | bytes 1572896 | tf_op jit(solution)/shard_map/all_to_all | solution.py:649
  199.2 6.4 all-to-all-done.4
  216.9 11.9 %all-to-all-done.5 = bf16[4,96,2048]{2,1,0:T(8,128)(2,1)} async-done(((bf16[4,96,2048]{2,1,0:T(8,128)(2,1)}), bf16[4,96,2048]{2,1,0:T(8,128)(2,1)}, u32[]{:S(2)}, u32[]{:S(2)}) %all-to-all-start.5) | async-done | bytes 1572896 | tf_op jit(solution)/shard_map/all_to_all | solution.py:649
  235.5 9.1 %collective-permute-done.17 = bf16[96,2176]{1,0:T(8,128)(2,1)S(1)} collective-permute-done((bf16[96,2176]{1,0:T(8,128)(2,1)S(1)}, bf16[96,2176]{1,0:T(8,128)(2,1)S(1)}, u32[]{:S(2)}, u32[]{:S(2)}) %collective-permute-start.17) | collective-permute-done | bytes 417824 | tf_op jit(solution)/shard_map/ppermute | solution.py:68
  264.9 16.7 %shard_map.316 = (bf16[384,2048]{1,0:T(8,128)(2,1)}, bf16[384,2048]{1,0:T(8,128)(2,1)}, bf16[384,2176]{1,0:T(8,128)(2,1)}, bf16[384,2176]{1,0:T(8,128)(2,1)}, bf...) custom-call(s32[1]{0:T(128)} %bitcast.159, ...), custom_call_target="tpu_custom_call" | custom-call | flops 9663676416 | bytes 12582912 | tf_op jit(solution)/shard_map/pallas_call | solution.py:336
  292.7 16.7 %shard_map.318 = (bf16[384,2048]{1,0:T(8,128)(2,1)}, bf16[384,2048]{1,0:T(8,128)(2,1)}, bf16[384,2176]{1,0:T(8,128)(2,1)}, bf16[384,2176]{1,0:T(8,128)(2,1)}, bf...) custom-call(s32[1]{0:T(128)} %bitcast.160, ...), custom_call_target="tpu_custom_call" | custom-call | flops 9663676416 | bytes 12582912 | tf_op jit(solution)/shard_map/pallas_call | solution.py:336
  318.9 16.8 %shard_map.320 = (bf16[384,2048]{1,0:T(8,128)(2,1)}, bf16[384,2048]{1,0:T(8,128)(2,1)}, bf16[384,2176]{1,0:T(8,128)(2,1)}, bf16[384,2176]{1,0:T(8,128)(2,1)}, bf...) custom-call(s32[1]{0:T(128)} %bitcast.161, ...), custom_call_target="tpu_custom_call" | custom-call | flops 9663676416 | bytes 12582912 | tf_op jit(solution)/shard_map/pallas_call | solution.py:336
  353.5 16.8 %shard_map.322 = (bf16[384,2048]{1,0:T(8,128)(2,1)}, bf16[384,2048]{1,0:T(8,128)(2,1)}, bf16[384,2176]{1,0:T(8,128)(2,1)}, bf16[384,2176]{1,0:T(8,128)(2,1)}, bf...) custom-call(s32[1]{0:T(128)} %bitcast.162, ...), custom_call_target="tpu_custom_call" | custom-call | flops 9663676416 | bytes 12582912 | tf_op jit(solution)/shard_map/pallas_call | solution.py:336
  384.0 14.5 %all-to-all-done.10 = bf16[4,96,2176]{2,1,0:T(8,128)(2,1)S(1)} async-done(((bf16[4,96,2176]{2,1,0:T(8,128)(2,1)}), bf16[4,96,2176]{2,1,0:T(8,128)(2,1)S(1)}, u32[]{:S(2)}, u32[]{:S(2)}) %all-to-all-start.10) | async-done | bytes 1671200 | tf_op jit(solution)/shard_map/all_to_all | solution.py:649
  415.0 12.0 %collective-permute-done.36.refs_1_ = bf16[128,2176]{1,0:T(8,128)(2,1)S(1)} collective-permute-done((bf16[128,2176]{1,0:T(8,128)(2,1)S(1)}, bf16[128,2176]{1,0:T(8,128)(2,1)S(1)}, u32[]{:S(2)}, u32[]{:S(2)}) %collective-permute-start.36) | collective-permute-done | bytes 557088 | tf_op jit(solution)/shard_map/ppermute | solution.py:71
  436.3 9.2 %collective-permute-done.33.refs_3_ = bf16[96,2176]{1,0:T(8,128)(2,1)S(1)} collective-permute-done((bf16[96,2176]{1,0:T(8,128)(2,1)}, bf16[96,2176]{1,0:T(8,128)(2,1)S(1)}, u32[]{:S(2)}, u32[]{:S(2)}) %collective-permute-start.33) | collective-permute-done | bytes 417824 | tf_op jit(solution)/shard_map/ppermute | solution.py:68
  445.5 7.3 collective-permute-done.32.refs_2_
  474.4 6.5 all-to-all-done.12
  496.4 9.0 %shard_map.327 = (f32[1024,256]{1,0:T(8,128)S(1)}, f32[1024,256]{1,0:T(8,128)S(1)}, bf16[1024,256]{1,0:T(8,128)(2,1)S(1)}, f32[2,2,1024]{2,1,0:T(2,128)S(1)}, f32[2,256]{1,0:T(2,128)S(1)}) custom-call(bf16[1024,256]{1,0:T(8,128)(2,1)S(1)} %bitcast.153, f32[1024,256]{1,0:T(8,128)} %copy-done.36, f32[1024,256]{1,0:T(8,128)} %copy-done.37, ...), custom_call_target="tpu_custom_call" | custom-call | flops 1610612736 | bytes 6291456 | tf_op jit(solution)/shard_map/pallas_call | solution.py:608
  509.0 9.9 %all_gather.11 = f32[8,16,128]{2,1,0:T(8,128)S(1)} all-gather(f32[1,16,128]{2,1,0:T(8,128)S(1)} %all_gather_reshape.7), channel_id=1, replica_groups=mesh['dp'=4,'ctx'=8] {'ctx'}, dimensions={0}, use_global_device_ids=true | all-gather | bytes 73728 | tf_op jit(solution)/shard_map/all_gather | solution.py:884
  540.5 9.6 %collective-permute-done.44 = bf16[128,2048]{1,0:T(8,128)(2,1)} collective-permute-done((bf16[128,2048]{1,0:T(8,128)(2,1)S(1)}, bf16[128,2048]{1,0:T(8,128)(2,1)}, u32[]{:S(2)}, u32[]{:S(2)}) %collective-permute-start.44) | collective-permute-done | bytes 524320 | tf_op jit(solution)/shard_map/ppermute | solution.py:68
  561.3 15.0 %shard_map.328 = f32[512,2048]{1,0:T(8,128)} custom-call(bf16[384,512]{1,0:T(8,128)(2,1)} %get-tuple-element.288.refs_0_, bf16[384,512]{1,0:T(8,128)(2,1)} %get-tuple-element.290.refs_1_, bf16[384,512]{1,0:T(8,128)(2,1)} %get-tuple-element.292.refs_2_, bf16[384,512]{1,0:T(8,128)(2,1)} %get-tuple-element.294.refs_3_, ...), custom_call_target="tpu_custom_call" | custom-call | flops 6442450944 | bytes 19922944 | tf_op jit(solution)/shard_map/pallas_call | solution.py:367
  620.8 12.6 %collective-permute-done.51 = bf16[512,768]{1,0:T(8,128)(2,1)} collective-permute-done((bf16[512,768]{1,0:T(8,128)(2,1)S(1)}, bf16[512,768]{1,0:T(8,128)(2,1)}, u32[]{:S(2)}, u32[]{:S(2)}) %collective-permute-start.51) | collective-permute-done | bytes 786464 | tf_op jit(solution)/shard_map/ppermute | solution.py:71
  633.4 14.6 %shard_map.332 = f32[2048,512]{1,0:T(8,128)} custom-call(bf16[384,2176]{1,0:T(8,128)(2,1)} %constant_dynamic-update-slice_fusion.4.near.refs_0_, bf16[384,2176]{1,0:T(8,128)(2,1)} %copy-done.130, bf16[384,2176]{1,0:T(8,128)(2,1)} %bitcast.37.near.refs_2_, bf16[384,2176]{1,0:T(8,128)(2,1)} %collective-permute-done.22.far.refs_3_, ...), custom_call_target="tpu_custom_call" | custom-call | flops 6442450944 | bytes 19922944 | tf_op jit(solution)/shard_map/pallas_call | solution.py:367
  668.8 8.5 %collective-permute-done.55 = bf16[512,768]{1,0:T(8,128)(2,1)} collective-permute-done((bf16[512,768]{1,0:T(8,128)(2,1)}, bf16[512,768]{1,0:T(8,128)(2,1)}, u32[]{:S(2)}, u32[]{:S(2)}) %collective-permute-start.55) | collective-permute-done | bytes 786464 | tf_op jit(solution)/shard_map/ppermute | solution.py:71
  682.9 14.6 %shard_map.333 = f32[2048,512]{1,0:T(8,128)} custom-call(bf16[384,2176]{1,0:T(8,128)(2,1)} %constant_dynamic-update-slice_fusion.4.near.refs_0_, bf16[384,2176]{1,0:T(8,128)(2,1)} %copy-done.130, bf16[384,2176]{1,0:T(8,128)(2,1)} %bitcast.37.near.refs_2_, bf16[384,2176]{1,0:T(8,128)(2,1)} %collective-permute-done.22.far.refs_3_, ...), custom_call_target="tpu_custom_call" | custom-call | flops 6442450944 | bytes 19922944 | tf_op jit(solution)/shard_map/pallas_call | solution.py:367
  719.4 8.3 %collective-permute-done.59 = bf16[2,64,2048]{2,1,0:T(8,128)(2,1)S(1)} collective-permute-done((bf16[2,64,2048]{2,1,0:T(8,128)(2,1)}, bf16[2,64,2048]{2,1,0:T(8,128)(2,1)S(1)}, u32[]{:S(2)}, u32[]{:S(2)}) %collective-permute-start.59) | collective-permute-done | bytes 524320 | tf_op jit(solution)/shard_map/ppermute | solution.py:68
  (582 shorter events, 375.2 us)
Async XLA Ops:
  16.2 194.0 %all-gather.2.cloned.1.call-start = ((), (), s32[]{:S(2)}) async-start(), calls=%async_computation.18 | async-start | bytes 8650752 | tf_op jit(solution)/shard_map/all_gather | solution.py:876
  32.7 27.8 %collective-permute-start.1 = (bf16[512,768]{1,0:T(8,128)(2,1)S(1)}, bf16[512,768]{1,0:T(8,128)(2,1)}, u32[]{:S(2)}, u32[]{:S(2)}) collective-permute-start(bf16[512,768]{1,0:T(8,128)(2,1)S(1)} %bitcast.156), channel_id=1, source_target_pairs={{0,8},{8,24},{24,16},{16,0},{1,9},{9,25},{25,17},{17,1},{2,10},{10... | collective-permute-start | bytes 2359304 | tf_op jit(solution)/shard_map/ppermute | solution.py:71
  33.5 27.0 %collective-permute-start.4 = (bf16[128,2048]{1,0:T(8,128)(2,1)S(1)}, bf16[128,2048]{1,0:T(8,128)(2,1)S(1)}, u32[]{:S(2)}, u32[]{:S(2)}) collective-permute-start(bf16[128,2048]{1,0:T(8,128)(2,1)S(1)} %bitcast.171), channel_id=1, source_target_pairs={{0,6},{1,7},{2,4},{3,5},{4,2},{5,3},{6,0},{7,1},{8,14},{9,15},{10,... | collective-permute-start | bytes 1572872 | tf_op jit(solution)/shard_map/ppermute | solution.py:68
  62.9 28.7 %collective-permute-start.6 = (bf16[512,2048]{1,0:T(8,128)(2,1)S(1)}, bf16[512,2048]{1,0:T(8,128)(2,1)}, u32[]{:S(2)}, u32[]{:S(2)}) collective-permute-start(bf16[512,2048]{1,0:T(8,128)(2,1)S(1)} %pad_maximum_fusion.near), channel_id=1, source_target_pairs={{0,1},{1,0},{2,3},{3,2},{4,5},{5,4},{6,7},{7,6},{8,9},{9,8},{10,11... | collective-permute-start | bytes 6291464 | tf_op jit(solution)/shard_map/ppermute | solution.py:68
  63.1 27.7 %collective-permute-start.5 = (bf16[512,768]{1,0:T(8,128)(2,1)}, bf16[512,768]{1,0:T(8,128)(2,1)}, u32[]{:S(2)}, u32[]{:S(2)}) collective-permute-start(bf16[512,768]{1,0:T(8,128)(2,1)} %collective-permute-done.1.refs_1_), channel_id=1, source_target_pairs={{0,8},{8,24},{24,16},{16,0},{1,9},{9,25},{25,17},{17,1},{2,10},{10... | collective-permute-start | bytes 2359304 | tf_op jit(solution)/shard_map/ppermute | solution.py:71
  96.9 30.2 %collective-permute-start.11 = (bf16[384,2048]{1,0:T(8,128)(2,1)}, bf16[384,2048]{1,0:T(8,128)(2,1)}, u32[]{:S(2)}, u32[]{:S(2)}) collective-permute-start(bf16[384,2048]{1,0:T(8,128)(2,1)} %constant_dynamic-update-slice_fusion.dy_near.refs_8_), channel_id=1, source_target_pairs={{0,1},{1,0},{2,3},{3,2},{4,5},{5,4},{6,7},{7,6},{8,9},{9,8},{10,11... | collective-permute-start | bytes 4718600 | tf_op jit(solution)/shard_map/ppermute | solution.py:68
  99.9 27.2 %all-to-all-start.2 = ((bf16[4,96,2048]{2,1,0:T(8,128)(2,1)}), bf16[4,96,2048]{2,1,0:T(8,128)(2,1)}, u32[]{:S(2)}, u32[]{:S(2)}) async-start(bf16[4,96,2048]{2,1,0:T(8,128)(2,1)} %bitcast.150), calls=%async_computation.2 | async-start | bytes 3145728 | tf_op jit(solution)/shard_map/all_to_all | solution.py:649
  127.1 26.6 %collective-permute-start.12 = (bf16[128,2176]{1,0:T(8,128)(2,1)S(1)}, bf16[128,2176]{1,0:T(8,128)(2,1)}, u32[]{:S(2)}, u32[]{:S(2)}) collective-permute-start(bf16[128,2176]{1,0:T(8,128)(2,1)S(1)} %collective-permute-done.block), channel_id=1, source_target_pairs={{0,8},{8,24},{24,16},{16,0},{1,9},{9,25},{25,17},{17,1},{2,10},{10... | collective-permute-start | bytes 1671176 | tf_op jit(solution)/shard_map/ppermute | solution.py:71
  157.7 33.7 %all-to-all-start.3 = ((bf16[4,96,2048]{2,1,0:T(8,128)(2,1)}), bf16[4,96,2048]{2,1,0:T(8,128)(2,1)}, u32[]{:S(2)}, u32[]{:S(2)}) async-start(bf16[4,96,2048]{2,1,0:T(8,128)(2,1)} %bitcast.25), calls=%async_computation.3 | async-start | bytes 3145728 | tf_op jit(solution)/shard_map/all_to_all | solution.py:649
  162.6 36.6 %collective-permute-start.14 = (bf16[384,2048]{1,0:T(8,128)(2,1)}, bf16[384,2048]{1,0:T(8,128)(2,1)}, u32[]{:S(2)}, u32[]{:S(2)}) collective-permute-start(bf16[384,2048]{1,0:T(8,128)(2,1)} %bitcast.18.dy_near.refs_10_), channel_id=1, source_target_pairs={{0,1},{1,0},{2,3},{3,2},{4,5},{5,4},{6,7},{7,6},{8,9},{9,8},{10,11... | collective-permute-start | bytes 4718600 | tf_op jit(solution)/shard_map/ppermute | solution.py:68
  256.6 25.7 %all-to-all-start.6 = ((bf16[4,96,2176]{2,1,0:T(8,128)(2,1)}), bf16[4,96,2176]{2,1,0:T(8,128)(2,1)}, u32[]{:S(2)}, u32[]{:S(2)}) async-start(bf16[4,96,2176]{2,1,0:T(8,128)(2,1)} %bitcast.36), calls=%async_computation.6 | async-start | bytes 3342336 | tf_op jit(solution)/shard_map/all_to_all | solution.py:649
  282.3 28.7 %collective-permute-start.24 = (bf16[384,2176]{1,0:T(8,128)(2,1)}, bf16[384,2176]{1,0:T(8,128)(2,1)S(1)}, u32[]{:S(2)}, u32[]{:S(2)}) collective-permute-start(bf16[384,2176]{1,0:T(8,128)(2,1)} %get-tuple-element.243), channel_id=1, source_target_pairs={{0,1},{1,0},{2,3},{3,2},{4,5},{5,4},{6,7},{7,6},{8,9},{9,8},{10,11... | collective-permute-start | bytes 5013512 | tf_op jit(solution)/shard_map/ppermute | solution.py:68
  311.0 28.8 %collective-permute-start.26 = (bf16[384,2176]{1,0:T(8,128)(2,1)}, bf16[384,2176]{1,0:T(8,128)(2,1)}, u32[]{:S(2)}, u32[]{:S(2)}) collective-permute-start(bf16[384,2176]{1,0:T(8,128)(2,1)} %get-tuple-element.250), channel_id=1, source_target_pairs={{0,1},{1,0},{2,3},{3,2},{4,5},{5,4},{6,7},{7,6},{8,9},{9,8},{10,11... | collective-permute-start | bytes 5013512 | tf_op jit(solution)/shard_map/ppermute | solution.py:68
  340.3 30.0 %collective-permute-start.29 = (bf16[384,2176]{1,0:T(8,128)(2,1)}, bf16[384,2176]{1,0:T(8,128)(2,1)}, u32[]{:S(2)}, u32[]{:S(2)}) collective-permute-start(bf16[384,2176]{1,0:T(8,128)(2,1)} %get-tuple-element.256), channel_id=1, source_target_pairs={{0,1},{1,0},{2,3},{3,2},{4,5},{5,4},{6,7},{7,6},{8,9},{9,8},{10,11... | collective-permute-start | bytes 5013512 | tf_op jit(solution)/shard_map/ppermute | solution.py:68
  370.3 28.2 %collective-permute-start.35 = (bf16[384,2176]{1,0:T(8,128)(2,1)}, bf16[384,2176]{1,0:T(8,128)(2,1)}, u32[]{:S(2)}, u32[]{:S(2)}) collective-permute-start(bf16[384,2176]{1,0:T(8,128)(2,1)} %get-tuple-element.257), channel_id=1, source_target_pairs={{0,1},{1,0},{2,3},{3,2},{4,5},{5,4},{6,7},{7,6},{8,9},{9,8},{10,11... | collective-permute-start | bytes 5013512 | tf_op jit(solution)/shard_map/ppermute | solution.py:68
  407.0 29.2 %collective-permute-start.38 = (bf16[384,2048]{1,0:T(8,128)(2,1)}, bf16[384,2048]{1,0:T(8,128)(2,1)}, u32[]{:S(2)}, u32[]{:S(2)}) collective-permute-start(bf16[384,2048]{1,0:T(8,128)(2,1)} %get-tuple-element.280), channel_id=1, source_target_pairs={{0,1},{1,0},{2,3},{3,2},{4,5},{5,4},{6,7},{7,6},{8,9},{9,8},{10,11... | collective-permute-start | bytes 4718600 | tf_op jit(solution)/shard_map/ppermute | solution.py:68
  436.2 72.0 %collective-permute-start.50 = (bf16[384,2048]{1,0:T(8,128)(2,1)}, bf16[384,2048]{1,0:T(8,128)(2,1)}, u32[]{:S(2)}, u32[]{:S(2)}) collective-permute-start(bf16[384,2048]{1,0:T(8,128)(2,1)} %get-tuple-element.308), channel_id=1, source_target_pairs={{0,1},{1,0},{2,3},{3,2},{4,5},{5,4},{6,7},{7,6},{8,9},{9,8},{10,11... | collective-permute-start | bytes 4718600 | tf_op jit(solution)/shard_map/ppermute | solution.py:68
  480.9 28.1 %all-to-all-start.13 = ((bf16[4,96,2048]{2,1,0:T(8,128)(2,1)}), bf16[4,96,2048]{2,1,0:T(8,128)(2,1)}, u32[]{:S(2)}, u32[]{:S(2)}) async-start(bf16[4,96,2048]{2,1,0:T(8,128)(2,1)} %bitcast.51), calls=%async_computation.13 | async-start | bytes 3145728 | tf_op jit(solution)/shard_map/all_to_all | solution.py:649
  488.1 46.4 %collective-permute-start.30 = (bf16[384,2048]{1,0:T(8,128)(2,1)}, bf16[384,2048]{1,0:T(8,128)(2,1)}, u32[]{:S(2)}, u32[]{:S(2)}) collective-permute-start(bf16[384,2048]{1,0:T(8,128)(2,1)} %get-tuple-element.258), channel_id=1, source_target_pairs={{0,1},{1,0},{2,3},{3,2},{4,5},{5,4},{6,7},{7,6},{8,9},{9,8},{10,11... | collective-permute-start | bytes 4718600 | tf_op jit(solution)/shard_map/ppermute | solution.py:68
  488.1 46.4 %collective-permute-start.54 = (bf16[384,2048]{1,0:T(8,128)(2,1)}, bf16[384,2048]{1,0:T(8,128)(2,1)}, u32[]{:S(2)}, u32[]{:S(2)}) collective-permute-start(bf16[384,2048]{1,0:T(8,128)(2,1)} %get-tuple-element.333), channel_id=1, source_target_pairs={{0,1},{1,0},{2,3},{3,2},{4,5},{5,4},{6,7},{7,6},{8,9},{9,8},{10,11... | collective-permute-start | bytes 4718600 | tf_op jit(solution)/shard_map/ppermute | solution.py:68
  524.5 25.6 %collective-permute-start.44 = (bf16[128,2048]{1,0:T(8,128)(2,1)S(1)}, bf16[128,2048]{1,0:T(8,128)(2,1)}, u32[]{:S(2)}, u32[]{:S(2)}) collective-permute-start(bf16[128,2048]{1,0:T(8,128)(2,1)S(1)} %copy-done.72), channel_id=1, source_target_pairs={{0,4},{1,5},{2,6},{3,7},{4,0},{5,1},{6,2},{7,3},{8,12},{9,13},{10,... | collective-permute-start | bytes 1572872 | tf_op jit(solution)/shard_map/ppermute | solution.py:68
  529.7 71.9 %all-to-all-start.14 = ((bf16[4,96,2048]{2,1,0:T(8,128)(2,1)}), bf16[4,96,2048]{2,1,0:T(8,128)(2,1)S(1)}, u32[]{:S(2)}, u32[]{:S(2)}) async-start(bf16[4,96,2048]{2,1,0:T(8,128)(2,1)} %bitcast.176), calls=%async_computation.14 | async-start | bytes 3145728 | tf_op jit(solution)/shard_map/all_to_all | solution.py:649
  538.4 66.8 %collective-permute-start.49 = (bf16[128,2048]{1,0:T(8,128)(2,1)}, bf16[128,2048]{1,0:T(8,128)(2,1)}, u32[]{:S(2)}, u32[]{:S(2)}) collective-permute-start(bf16[128,2048]{1,0:T(8,128)(2,1)} %shard_map.330), channel_id=1, source_target_pairs={{0,8},{8,24},{24,16},{16,0},{1,9},{9,25},{25,17},{17,1},{2,10},{10... | collective-permute-start | bytes 1572872 | tf_op jit(solution)/shard_map/ppermute | solution.py:71
  551.7 30.2 %collective-permute-start.46 = (bf16[512,2048]{1,0:T(8,128)(2,1)S(1)}, bf16[512,2048]{1,0:T(8,128)(2,1)S(1)}, u32[]{:S(2)}, u32[]{:S(2)}) collective-permute-start(bf16[512,2048]{1,0:T(8,128)(2,1)S(1)} %pad_maximum_fusion.1), channel_id=1, source_target_pairs={{0,1},{1,0},{2,3},{3,2},{4,5},{5,4},{6,7},{7,6},{8,9},{9,8},{10,11... | collective-permute-start | bytes 6291464 | tf_op jit(solution)/shard_map/ppermute | solution.py:68
  558.3 51.6 %collective-permute-start.42 = (bf16[512,768]{1,0:T(8,128)(2,1)}, bf16[512,768]{1,0:T(8,128)(2,1)}, u32[]{:S(2)}, u32[]{:S(2)}) collective-permute-start(bf16[512,768]{1,0:T(8,128)(2,1)} %constant_dynamic-slice_fusion), channel_id=1, source_target_pairs={{0,8},{8,24},{24,16},{16,0},{1,9},{9,25},{25,17},{17,1},{2,10},{10... | collective-permute-start | bytes 2359304 | tf_op jit(solution)/shard_map/ppermute | solution.py:71
  601.7 46.4 %all-to-all-start.15 = ((bf16[4,96,2048]{2,1,0:T(8,128)(2,1)}), bf16[4,96,2048]{2,1,0:T(8,128)(2,1)S(1)}, u32[]{:S(2)}, u32[]{:S(2)}) async-start(bf16[4,96,2048]{2,1,0:T(8,128)(2,1)} %bitcast.177), calls=%async_computation.15 | async-start | bytes 3145728 | tf_op jit(solution)/shard_map/all_to_all | solution.py:649
  617.1 35.8 %collective-permute-start.52 = (bf16[64,2048]{1,0:T(8,128)(2,1)}, bf16[64,2048]{1,0:T(8,128)(2,1)S(1)}, u32[]{:S(2)}, u32[]{:S(2)}) collective-permute-start(bf16[64,2048]{1,0:T(8,128)(2,1)} %fusion.10), channel_id=1, source_target_pairs={{0,8},{8,24},{24,16},{16,0},{1,9},{9,25},{25,17},{17,1},{2,10},{10... | collective-permute-start | bytes 786440 | tf_op jit(solution)/shard_map/ppermute | solution.py:71
  618.6 34.3 %collective-permute-start.53 = (bf16[128,2048]{1,0:T(8,128)(2,1)}, bf16[128,2048]{1,0:T(8,128)(2,1)S(1)}, u32[]{:S(2)}, u32[]{:S(2)}) collective-permute-start(bf16[128,2048]{1,0:T(8,128)(2,1)} %shard_map.331), channel_id=1, source_target_pairs={{0,8},{8,24},{24,16},{16,0},{1,9},{9,25},{25,17},{17,1},{2,10},{10... | collective-permute-start | bytes 1572872 | tf_op jit(solution)/shard_map/ppermute | solution.py:71
  661.7 42.1 %collective-permute-start.41 = (bf16[96,2048]{1,0:T(8,128)(2,1)}, bf16[96,2048]{1,0:T(8,128)(2,1)S(1)}, u32[]{:S(2)}, u32[]{:S(2)}) collective-permute-start(bf16[96,2048]{1,0:T(8,128)(2,1)} %get-tuple-element.388), channel_id=1, source_target_pairs={{0,6},{1,7},{2,4},{3,5},{4,2},{5,3},{6,0},{7,1},{8,14},{9,15},{10,... | collective-permute-start | bytes 1179656 | tf_op jit(solution)/shard_map/ppermute | solution.py:68
  664.1 39.7 %collective-permute-start.40 = (bf16[96,2048]{1,0:T(8,128)(2,1)}, bf16[96,2048]{1,0:T(8,128)(2,1)}, u32[]{:S(2)}, u32[]{:S(2)}) collective-permute-start(bf16[96,2048]{1,0:T(8,128)(2,1)} %get-tuple-element.389), channel_id=1, source_target_pairs={{0,4},{1,5},{2,6},{3,7},{4,0},{5,1},{6,2},{7,3},{8,12},{9,13},{10,... | collective-permute-start | bytes 1179656 | tf_op jit(solution)/shard_map/ppermute | solution.py:68
  666.3 43.4 %collective-permute-start.58 = (bf16[512,2048]{1,0:T(8,128)(2,1)}, bf16[512,2048]{1,0:T(8,128)(2,1)}, u32[]{:S(2)}, u32[]{:S(2)}) collective-permute-start(bf16[512,2048]{1,0:T(8,128)(2,1)} %copy-done.58), channel_id=1, source_target_pairs={{0,1},{1,0},{2,3},{3,2},{4,5},{5,4},{6,7},{7,6},{8,9},{9,8},{10,11... | collective-permute-start | bytes 6291464 | tf_op jit(solution)/shard_map/ppermute | solution.py:68
  677.3 26.5 %collective-permute-start.39 = (bf16[96,2048]{1,0:T(8,128)(2,1)}, bf16[96,2048]{1,0:T(8,128)(2,1)S(1)}, u32[]{:S(2)}, u32[]{:S(2)}) collective-permute-start(bf16[96,2048]{1,0:T(8,128)(2,1)} %get-tuple-element.390), channel_id=1, source_target_pairs={{0,2},{1,3},{2,0},{3,1},{4,6},{5,7},{6,4},{7,5},{8,10},{9,11},{10,... | collective-permute-start | bytes 1179656 | tf_op jit(solution)/shard_map/ppermute | solution.py:68
  (181 other events, 2152.2 us)
Sparse Core Ops, SparseCore 0:
  91.8 112.7 all-gather.1

commit v3 on v2

--- a/solution.py
+++ b/solution.py
@@ -135,12 +135,13 @@
     def head_at(self, device, n):
         return ((device % self.group) * self.hpd + n) * (self.nc // self.group) + device // self.group
 
-    def weight_rows(self, grads, weights):
+    def weight_rows(self, grads, weights, gain):
         count, rows = len(weights), weights[0].shape[0]
         width = weights[0].shape[1]
 
-        def kernel(grads, *refs):
+        def kernel(gain, grads, *refs):
             sums = 0.0
+            gain_col = column(gain[...])
             for device in range(self.nc):
                 for w in range(count):
                     for n in range(self.hpd):
@@ -149,14 +150,34 @@
                         part = grads[device, :, start : start + HEAD_DIM].astype(F32)
                         refs[count + w][:, head] = part
                         sums += part * refs[w][:, head].astype(F32)
-            refs[-1][...] = as_row(jnp.sum(sums, axis=-1, keepdims=True))
+            refs[-1][...] = as_row(jnp.sum(sums, axis=-1, keepdims=True) / gain_col)
 
         shape = jax.ShapeDtypeStruct((rows, width), F32)
         return pl.pallas_call(
             kernel,
             out_shape=[shape] * count + [jax.ShapeDtypeStruct((1, rows), F32)],
             compiler_params=pltpu.CompilerParams(vmem_limit_bytes=24 * 2**20),
-        )(grads, *weights)
+        )(gain.astype(F32)[None], grads, *weights)
+
+    def slot_of(self, layer):
+        place = jnp.where(layer % 2 == 1, (layer + 1) // 2, jnp.where(layer == 0, 0, self.nz - layer // 2))
+        return (self.pos - place) % self.nz
+
+    def head_weights(self, blocks):
+        blocks = jnp.stack(blocks)
+        share = self.cx % self.group
+        rows = jnp.zeros((self.hpd, self.group) + blocks.shape[1:], blocks.dtype)
+        for k in range(self.group):
+            other = share ^ k
+            part = jnp.stack(
+                [
+                    lax.dynamic_index_in_dim(blocks, self.slot_of(other * self.hpd + n), 0, keepdims=False)
+                    for n in range(self.hpd)
+                ]
+            )
+            part = self.swap(part, k) if k else part
+            rows = lax.dynamic_update_slice(rows, part[:, None], (0, other, 0, 0))
+        return rows.reshape(self.cols, blocks.shape[-1])
 
     def own_heads(self, vector):
         return self.head_blocks(vector[None])[self.cx, 0]
@@ -193,9 +214,9 @@
     return jnp.sum(jnp.where(keep, notes.astype(F32), 0.0), axis=-1, keepdims=True)
 
 
-def pick_kernel(capacity, count, expert_ref, block, *outs):
+def pick_kernel(capacity, count, expert_ref, block, out):
     rows = block.shape[0]
-    width = outs[0].shape[1]
+    width = out.shape[1]
     start = block.shape[1] - NOTES
     before = lax.broadcasted_iota(jnp.int32, (rows, rows), 0) < lax.broadcasted_iota(jnp.int32, (rows, rows), 1)
     before = jnp.where(before, 1.0, 0.0).astype(BF)
@@ -205,31 +226,44 @@
         slot = dot(named.astype(BF), before)
         mine = lax.broadcasted_iota(jnp.int32, slot.shape, 0).astype(F32)
         choose = jnp.where((slot == mine) & (named > 0.5), 1.0, 0.0).astype(BF)
-        picked = dot(choose, block[:, :width]).astype(BF)
-        if len(outs) == 1:
-            outs[0][n * capacity : (n + 1) * capacity] = picked
-        else:
-            outs[n][...] = picked
-
-
-def pick_rows(block, experts, capacity, width, joined):
+        out[n * capacity : (n + 1) * capacity] = dot(choose, block[:, :width]).astype(BF)
+
+
+def pick_rows(block, experts, capacity, width):
     rows, wide = block.shape
     count = experts.shape[0]
-    shapes = [(count * capacity, width)] if joined else [(capacity, width)] * count
     return pl.pallas_call(
         functools.partial(pick_kernel, capacity, count),
         grid_spec=pltpu.PrefetchScalarGridSpec(
             num_scalar_prefetch=1,
             grid=(1,),
             in_specs=[pl.BlockSpec((rows, wide), lambda n, experts: (0, 0))],
-            out_specs=[pl.BlockSpec(shape, lambda n, experts: (0, 0)) for shape in shapes],
-        ),
-        out_shape=[jax.ShapeDtypeStruct(shape, BF) for shape in shapes],
+            out_specs=pl.BlockSpec((count * capacity, width), lambda n, experts: (0, 0)),
+        ),
+        out_shape=jax.ShapeDtypeStruct((count * capacity, width), BF),
         compiler_params=pltpu.CompilerParams(vmem_limit_bytes=24 * 2**20),
         cost_estimate=pl.CostEstimate(
             flops=2 * count * rows * capacity * width, bytes_accessed=4 * count * rows * width, transcendentals=0
         ),
     )(experts, block)
+
+
+def add_kernel(left, right, *refs):
+    refs[-1][...] = (left[...].astype(F32) + right[...].astype(F32)).astype(BF)
+
+
+def add_rows(left, right, *deps, tile=96):
+    rows, width = left.shape
+    row = pl.BlockSpec((tile, width), lambda n: (n, 0))
+    return pl.pallas_call(
+        add_kernel,
+        grid=(rows // tile,),
+        in_specs=[row, row] + [pl.BlockSpec(memory_space=pl.ANY)] * len(deps),
+        out_specs=row,
+        out_shape=jax.ShapeDtypeStruct((rows, width), BF),
+        compiler_params=pltpu.CompilerParams(vmem_limit_bytes=40 * 2**20),
+        cost_estimate=pl.CostEstimate(flops=rows * width, bytes_accessed=6 * rows * width, transcendentals=0),
+    )(left, right, *deps)
 
 
 def spread_kernel(capacity, has_sum, expert_ref, notes, *refs):
@@ -275,50 +309,49 @@
 
 
 def expert_kernel(
-    kinds, expert_ref, near, far, dy_near, dy_far, gate_w, up_w, down_w,
-    out_near, out_far, grad_near, grad_far, hidden_near, hidden_far, gate_near, gate_far, up_near, up_far,
+    kinds, expert_ref, near, far, dy_near, dy_far, gate_w, up_w, down_w, *refs,
 ):
+    sides, mids, outs = refs[-10:-8], refs[-8:-2], refs[-2:]
     tile = near.shape[0]
     width = dy_near.shape[1]
     expert = expert_ref[0]
     rows = jnp.concatenate([near[:, :width], far[:, :width]], axis=0)
     notes = jnp.concatenate([near[:, width:], far[:, width:]], axis=0)
     dy = jnp.concatenate([dy_near[...], dy_far[...]], axis=0)
+
+    def put(pair, start, value):
+        pair[0][:, start : start + value.shape[1]] = value[:tile]
+        pair[1][:, start : start + value.shape[1]] = value[tile:]
+
     gate_col = lane_pick(notes, expert + kinds, expert + 2 * kinds)
     gate_pre = dot(rows, gate_w[...])
     up_pre = dot(rows, up_w[...])
     sigmoid_val = jax.nn.sigmoid(gate_pre)
     silu = gate_pre * sigmoid_val
     hidden_f = silu * up_pre
-    out = (dot(hidden_f.astype(BF), down_w[...]) * gate_col).astype(BF)
-    out_near[...] = out[:tile]
-    out_far[...] = out[tile:]
+    put(outs, 0, (dot(hidden_f.astype(BF), down_w[...]) * gate_col).astype(BF))
     grad_hidden = times_transposed(dy, down_w[...])
     weighted = jnp.sum(grad_hidden * hidden_f, axis=-1, keepdims=True) * gate_col
     lane = lax.broadcasted_iota(jnp.int32, (2 * tile, NOTES), 1)
-    weighted = jnp.where(lane == expert, weighted, 0.0).astype(BF)
-    grad_near[:, width:] = weighted[:tile]
-    grad_far[:, width:] = weighted[tile:]
+    put(sides, width, jnp.where(lane == expert, weighted, 0.0).astype(BF))
     grad_hidden = grad_hidden * gate_col
     grad_gate_pre = (
         grad_hidden * up_pre * (sigmoid_val * (1.0 + gate_pre * (1.0 - sigmoid_val)))
     ).astype(BF)
     grad_up_pre = (grad_hidden * silu).astype(BF)
-    hidden = (hidden_f * gate_col).astype(BF)
-    hidden_near[...] = hidden[:tile]
-    hidden_far[...] = hidden[tile:]
-    gate_near[...] = grad_gate_pre[:tile]
-    gate_far[...] = grad_gate_pre[tile:]
-    up_near[...] = grad_up_pre[:tile]
-    up_far[...] = grad_up_pre[tile:]
-    grad = (
-        times_transposed(grad_gate_pre, gate_w[...]) + times_transposed(grad_up_pre, up_w[...])
-    ).astype(BF)
-    grad_near[:, :width] = grad[:tile]
-    grad_far[:, :width] = grad[tile:]
-
-
-def expert_chunk(kinds, expert, near, far, dy_near, dy_far, gate_w, up_w, down_w, tile=128):
+    for n, mid in enumerate(((hidden_f * gate_col).astype(BF), grad_gate_pre, grad_up_pre)):
+        mids[2 * n][...] = mid[:tile]
+        mids[2 * n + 1][...] = mid[tile:]
+    put(
+        sides,
+        0,
+        (
+            times_transposed(grad_gate_pre, gate_w[...]) + times_transposed(grad_up_pre, up_w[...])
+        ).astype(BF),
+    )
+
+
+def expert_chunk(kinds, expert, near, far, dy_near, dy_far, gate_w, up_w, down_w, *deps, tile=128):
     rows, width = dy_near.shape
     units = gate_w.shape[1]
 
@@ -328,37 +361,35 @@
     def whole(array):
         return pl.BlockSpec(array.shape, lambda i, expert: (0, 0), pipeline_mode=pl.Buffered(1))
 
-    def shape(cols):
-        return jax.ShapeDtypeStruct((rows, cols), BF)
-
     wide = near.shape[1]
-    outs = [width, width, wide, wide] + [units] * 6
+    outs = [wide] * 2 + [units] * 6 + [width] * 2
     return pl.pallas_call(
         functools.partial(expert_kernel, kinds),
         grid_spec=pltpu.PrefetchScalarGridSpec(
             num_scalar_prefetch=1,
             grid=(rows // tile,),
-            in_specs=[row(wide), row(wide), row(width), row(width), whole(gate_w), whole(up_w), whole(down_w)],
+            in_specs=[row(wide), row(wide), row(width), row(width), whole(gate_w), whole(up_w), whole(down_w)]
+            + [pl.BlockSpec(memory_space=pl.ANY)] * len(deps),
             out_specs=[row(cols) for cols in outs],
         ),
-        out_shape=[shape(cols) for cols in outs],
+        out_shape=[jax.ShapeDtypeStruct((rows, cols), BF) for cols in outs],
         compiler_params=pltpu.CompilerParams(vmem_limit_bytes=56 * 2**20),
         cost_estimate=pl.CostEstimate(
             flops=24 * rows * width * units,
             bytes_accessed=16 * rows * width,
             transcendentals=2 * rows * units,
         ),
-    )(expert, near, far, dy_near, dy_far, gate_w, up_w, down_w)
+    )(expert, near, far, dy_near, dy_far, gate_w, up_w, down_w, *deps)
 
 
 def contract_kernel(count, *refs):
     total = 0.0
-    for left, right in zip(refs[:count], refs[count:-1]):
+    for left, right in zip(refs[:count], refs[count : 2 * count]):
         total += contract_rows(left[...], right[...])
     refs[-1][...] = total
 
 
-def contract_many(lefts, rights, rows, cols, tile=256):
+def contract_many(lefts, rights, rows, cols, dep, tile=256):
     count = len(lefts)
     depth = lefts[0].shape[0]
     tall = rows >= cols
@@ -367,7 +398,9 @@
     return pl.pallas_call(
         functools.partial(contract_kernel, count),
         grid=(max(rows, cols) // tile,),
-        in_specs=[strip if tall else held] * count + [held if tall else strip] * count,
+        in_specs=[strip if tall else held] * count
+        + [held if tall else strip] * count
+        + [pl.BlockSpec(memory_space=pl.ANY)],
         out_specs=pl.BlockSpec((tile, cols), lambda i: (i, 0)) if tall else pl.BlockSpec((rows, tile), lambda i: (0, i)),
         out_shape=jax.ShapeDtypeStruct((rows, cols), F32),
         compiler_params=pltpu.CompilerParams(vmem_limit_bytes=56 * 2**20),
@@ -376,7 +409,7 @@
             bytes_accessed=2 * depth * count * (rows + cols) + 4 * rows * cols,
             transcendentals=0,
         ),
-    )(*lefts, *rights)
+    )(*lefts, *rights, dep)
 
 
 def columns(rows):
@@ -456,8 +489,42 @@
     )(layers, rows, *weights)
 
 
+def grad_blocks_kernel(layer_ref, rows, grads, *outs):
+    step = pl.program_id(0)
+    block = contract_rows(rows[...], grads[...]).astype(BF)
+    for n, out in enumerate(outs):
+
+        @pl.when(step == n)
+        def _():
+            out[...] = block
+
+
+def grad_blocks(layers, rows, grads):
+    total, width = rows.shape
+    wide = grads.shape[1]
+    count = layers.shape[0]
+    depth = width // count
+    return pl.pallas_call(
+        grad_blocks_kernel,
+        grid_spec=pltpu.PrefetchScalarGridSpec(
+            num_scalar_prefetch=1,
+            grid=(count,),
+            in_specs=[
+                pl.BlockSpec((total, depth), lambda n, layers: (0, layers[n])),
+                pl.BlockSpec((total, wide), lambda n, layers: (0, 0), pipeline_mode=pl.Buffered(1)),
+            ],
+            out_specs=[pl.BlockSpec((depth, wide), lambda n, layers: (0, 0))] * count,
+        ),
+        out_shape=[jax.ShapeDtypeStruct((depth, wide), BF)] * count,
+        compiler_params=pltpu.CompilerParams(vmem_limit_bytes=48 * 2**20),
+        cost_estimate=pl.CostEstimate(
+            flops=2 * total * width * wide, bytes_accessed=2 * (total + wide) * width, transcendentals=0
+        ),
+    )(layers, rows, grads)
+
+
 def project_back_kernel(count, half, layer_ref, block_ref, grads, *refs):
-    near, far = refs[count:]
+    near, far = refs[-2:]
     step = pl.program_id(0)
     blocks = near.shape[0] // half
     for side, out in enumerate((near, far)):
@@ -471,7 +538,7 @@
             out[:, pl.ds(start, depth)] = times_transposed(rows, refs[n][...]).astype(BF)
 
 
-def project_back(layers, blocks, grads, weights, half, tile=256):
+def project_back(layers, blocks, grads, weights, half, dep, tile=256):
     count = len(weights)
     total, wide = grads.shape
     width = count * weights[0].shape[0]
@@ -483,7 +550,8 @@
             num_scalar_prefetch=2,
             grid=(total // 2 // tile,),
             in_specs=[pl.BlockSpec((total, wide), lambda n, *refs: (0, 0), pipeline_mode=pl.Buffered(1))]
-            + [held] * count,
+            + [held] * count
+            + [pl.BlockSpec(memory_space=pl.ANY)],
             out_specs=[pl.BlockSpec((tile, width), lambda n, *refs: (n, 0))] * 2,
         ),
         out_shape=[out, out],
@@ -491,16 +559,11 @@
         cost_estimate=pl.CostEstimate(
             flops=2 * total * width * wide, bytes_accessed=2 * total * (width + wide), transcendentals=0
         ),
-    )(layers, blocks, grads, *weights)
+    )(layers, blocks, grads, *weights, dep)
 
 
 def turn(value, cosine, sine):
     return value * cosine + pltpu.roll(value, HEAD_DIM // 2, 1) * sine
-
-
-def half_blocks(rows, half):
-    count = rows // half
-    return [(2 * n if n < count // 2 else 2 * (count - 1 - n) + 1) * half for n in range(count)]
 
 
 def masked_scores(queries, keys, first, score_scale):
@@ -511,7 +574,7 @@
 
 
 def attention_kernel(
-    half, tile, score_scale, q_pre, k_pre, v_pre, inv, gains, cosine, sine,
+    half, tile, score_scale, place_ref, q_pre, k_pre, v_pre, inv, gains, cosine, sine,
     sent, attended, lse, query_rot, key_rot, value,
 ):
     rows = q_pre.shape[0]
@@ -529,17 +592,19 @@
         total = jnp.sum(probs, axis=-1, keepdims=True)
         lse[first:end] = jnp.broadcast_to(top + jnp.log(total), (tile, HEAD_DIM))
         attended[first:end] = dot((probs / total).astype(BF), value[:end])
-    for n, place in enumerate(half_blocks(rows, half)):
-        sent[place : place + half] = attended[n * half : (n + 1) * half].astype(BF)
+    for n in range(rows // half):
+        place = pl.multiple_of(place_ref[n] * half, half)
+        sent[pl.ds(place, half)] = attended[n * half : (n + 1) * half].astype(BF)
 
 
 def attention_grad_kernel(
-    half, tile, score_scale, sent_grad, attended, lse, query_rot, key_rot, value, q_pre, k_pre, inv, gains,
+    half, tile, score_scale, place_ref, sent_grad, attended, lse, query_rot, key_rot, value, q_pre, k_pre, inv, gains,
     cosine, sine, scaled_q, scaled_k, grad_value, dots, grad_gains, grad_heads, key_sum, value_sum, query_sum,
 ):
     rows = q_pre.shape[0]
-    for n, place in enumerate(half_blocks(rows, half)):
-        grad_heads[n * half : (n + 1) * half] = sent_grad[place : place + half]
+    for n in range(rows // half):
+        place = pl.multiple_of(place_ref[n] * half, half)
+        grad_heads[n * half : (n + 1) * half] = sent_grad[pl.ds(place, half)]
     key_sum[...] = jnp.zeros_like(key_sum)
     value_sum[...] = jnp.zeros_like(value_sum)
     for n in range(rows // tile):
@@ -573,14 +638,14 @@
         angles = position[:, None] * freq[None, :].astype(np.float32)
         self.cosine = jnp.asarray(np.concatenate([np.cos(angles)] * 2, axis=1), F32)
         self.sine = jnp.asarray(np.concatenate([-np.sin(angles), np.sin(angles)], axis=1), F32)
-        self.head = pl.BlockSpec((rows, HEAD_DIM), lambda h: (0, h))
-        self.keys = pl.BlockSpec((rows, HEAD_DIM), lambda h: (0, h + hpd))
-        self.values = pl.BlockSpec((rows, HEAD_DIM), lambda h: (0, h + 2 * hpd))
-        self.stat = pl.BlockSpec((2, rows), lambda h: (0, 0))
-        self.gain = pl.BlockSpec((2, HEAD_DIM), lambda h: (0, h))
-        self.table = pl.BlockSpec((rows, HEAD_DIM), lambda h: (0, 0))
+        self.head = pl.BlockSpec((rows, HEAD_DIM), lambda h, place: (0, h))
+        self.keys = pl.BlockSpec((rows, HEAD_DIM), lambda h, place: (0, h + hpd))
+        self.values = pl.BlockSpec((rows, HEAD_DIM), lambda h, place: (0, h + 2 * hpd))
+        self.stat = pl.BlockSpec((2, rows), lambda h, place: (0, 0))
+        self.gain = pl.BlockSpec((2, HEAD_DIM), lambda h, place: (0, h))
+        self.table = pl.BlockSpec((rows, HEAD_DIM), lambda h, place: (0, 0))
         self.args = (half, self.tile, 1.0 / math.sqrt(HEAD_DIM))
-        self.params = pltpu.CompilerParams(vmem_limit_bytes=48 * 2**20)
+        self.params = pltpu.CompilerParams(vmem_limit_bytes=60 * 2**20)
 
     def shape(self, dtype):
         return jax.ShapeDtypeStruct((self.rows, self.hpd * HEAD_DIM), dtype)
@@ -591,31 +656,32 @@
             flops=products * area * HEAD_DIM, bytes_accessed=self.hpd * self.rows * HEAD_DIM * 24, transcendentals=area
         )
 
-    def forward(self, qkv, inv, gains):
+    def call(self, kernel, ins, outs, shapes, scratch, products):
         return pl.pallas_call(
-            functools.partial(attention_kernel, *self.args),
-            grid=(self.hpd,),
-            in_specs=[self.head, self.keys, self.values, self.stat, self.gain, self.table, self.table],
-            out_specs=[self.head] * 6,
-            out_shape=[self.shape(t) for t in (BF, F32, F32, BF, BF, BF)],
+            functools.partial(kernel, *self.args),
+            grid_spec=pltpu.PrefetchScalarGridSpec(
+                num_scalar_prefetch=1, grid=(self.hpd,), in_specs=ins, out_specs=outs, scratch_shapes=scratch
+            ),
+            out_shape=shapes,
             compiler_params=self.params,
-            cost_estimate=self.cost(3),
-        )(qkv, qkv, qkv, inv, gains, self.cosine, self.sine)
-
-    def backward(self, sent_grad, kept, qkv, inv, gains):
+            cost_estimate=self.cost(products),
+        )
+
+    def forward(self, places, qkv, inv, gains):
+        ins = [self.head, self.keys, self.values, self.stat, self.gain, self.table, self.table]
+        shapes = [self.shape(t) for t in (BF, F32, F32, BF, BF, BF)]
+        run = self.call(attention_kernel, ins, [self.head] * 6, shapes, [], 3)
+        return run(places, qkv, qkv, qkv, inv, gains, self.cosine, self.sine)
+
+    def backward(self, places, sent_grad, kept, qkv, inv, gains):
         rows, hpd = self.rows, self.hpd
-        line = pl.BlockSpec((None, 2, rows), lambda h: (h, 0, 0))
-        return pl.pallas_call(
-            functools.partial(attention_grad_kernel, *self.args),
-            grid=(hpd,),
-            in_specs=[self.head] * 6 + [self.head, self.keys, self.stat, self.gain, self.table, self.table],
-            out_specs=[self.head] * 3 + [line, self.gain],
-            out_shape=[self.shape(F32), self.shape(F32), self.shape(BF)]
-            + [jax.ShapeDtypeStruct((hpd, 2, rows), F32), jax.ShapeDtypeStruct((2, hpd * HEAD_DIM), F32)],
-            scratch_shapes=[pltpu.VMEM((rows, HEAD_DIM), BF)] + [pltpu.VMEM((rows, HEAD_DIM), F32)] * 3,
-            compiler_params=self.params,
-            cost_estimate=self.cost(6),
-        )(sent_grad, *kept, qkv, qkv, inv, gains, self.cosine, self.sine)
+        line = pl.BlockSpec((None, 2, rows), lambda h, place: (h, 0, 0))
+        ins = [self.head] * 6 + [self.head, self.keys, self.stat, self.gain, self.table, self.table]
+        shapes = [self.shape(F32), self.shape(F32), self.shape(BF)]
+        shapes += [jax.ShapeDtypeStruct((hpd, 2, rows), F32), jax.ShapeDtypeStruct((2, hpd * HEAD_DIM), F32)]
+        scratch = [pltpu.VMEM((rows, HEAD_DIM), BF)] + [pltpu.VMEM((rows, HEAD_DIM), F32)] * 3
+        run = self.call(attention_grad_kernel, ins, [self.head] * 3 + [line, self.gain], shapes, scratch, 6)
+        return run(places, sent_grad, *kept, qkv, qkv, inv, gains, self.cosine, self.sine)
 
 
 class Gathered:
@@ -630,104 +696,119 @@
         self.own = self.flipped[:1]
         self.straight = (first + jnp.arange(lay.nc // 2)).astype(jnp.int32)
 
-    def experts(self, step):
-        return self.straight if step else self.flipped
-
     def noted(self, rows, *notes):
         notes = [self.chosen.astype(BF)] + list(notes)
         rest = NOTES - self.kinds * len(notes)
         return jnp.concatenate([rows] + notes + [jnp.zeros((self.tok_rows, rest), BF)], axis=1)
 
-    def offer(self, step, block, width=None):
-        return pick_rows(block, self.experts(step), self.capacity, width or block.shape[1], step > 0)
-
-    def exchange(self, parts):
-        if len(parts) > 1:
-            return [parts[0]] + [self.lay.swap(p, flip) for p, flip in zip(parts[1:], self.lay.flips)]
+    def offer(self, block, width=None):
+        return pick_rows(block, self.straight, self.capacity, width or block.shape[1])
+
+    def exchange(self, offered):
         groups = [list(range(core, self.lay.nc, 2)) for core in (0, 1)]
-        return [
-            lax.all_to_all(parts[0], "ctx", split_axis=0, concat_axis=0, tiled=True, axis_index_groups=groups)
+        return lax.all_to_all(
+            offered, "ctx", split_axis=0, concat_axis=0, tiled=True, axis_index_groups=groups
+        )
+
+    def send_back(self, sums):
+        chip = self.lay.cx // 2
+        parts = [
+            lax.dynamic_slice_in_dim(sums, (chip ^ n) * self.capacity, self.capacity, 0)
+            for n in range(self.lay.nc // 2)
         ]
-
-    def joined(self, parts):
-        return jnp.concatenate(parts, axis=0) if len(parts) > 1 else parts[0]
-
-    def give_back(self, step, near, far):
-        sums = (near.astype(F32) + far.astype(F32)).astype(BF)
-        if step:
-            return self.exchange([sums])
-        count = len(self.lay.flips) + 1
-        return self.exchange([sums[n * self.capacity : (n + 1) * self.capacity] for n in range(count)])
+        return [parts[0]] + [self.lay.swap(p, flip) for p, flip in zip(parts[1:], self.lay.flips)]
 
     def spread(self, step, parts, total):
-        return spread_rows(self.blocks[step], self.experts(step), parts, total, self.capacity)
-
-    def run(self, block, dy, gate_w, up_w, down_w):
+        experts = self.flipped if len(parts) > 1 else self.straight
+        return spread_rows(self.blocks[step], experts, parts, total, self.capacity)
+
+    def straighten(self, parts):
+        chip = self.lay.cx // 2
+        whole = jnp.zeros((len(parts) * self.capacity, parts[0].shape[1]), parts[0].dtype)
+        for n, part in enumerate(parts):
+            whole = lax.dynamic_update_slice_in_dim(whole, part, (chip ^ n) * self.capacity, 0)
+        return whole
+
+    def run(self, block, dy, dy_last, gate_w, up_w, down_w):
         lay, nz = self.lay, self.lay.nz
         self.blocks = blocks = [block]
         self.rows, self.done, self.dy = rows, done, dy = [], [], dy
-        back, far_grads = {}, {}
-        parts = self.exchange(self.offer(0, block))
+        back, far_sums = {}, {}
+        near = self.exchange(self.offer(block))
         coming = lay.ring_step(block)
-        coming, *parts = sync(coming, *parts)
+        coming, near = sync(coming, near)
         for step in range(nz):
-            near = self.joined(parts)
             far = lay.swap(near, 1)
+            rows += [near, far]
             if step:
-                far_grads[step - 1] = lay.swap(done[-1][3], 1)
+                far_sums[step - 1] = lay.swap(done[-1][1], 1)
             if step + 1 < nz:
                 blocks.append(coming)
-                parts = self.exchange(self.offer(step + 1, coming))
+                near = self.exchange(self.offer(coming))
                 if step + 2 < nz:
                     coming = lay.ring_step(coming)
-            for pair in dy[step + 1 : step + 2]:
-                if len(pair) == 1:
-                    pair.append(lay.swap(pair[0], 1))
-            if step > 1:
-                far, far_grads[step - 2] = sync(far, far_grads[step - 2])
-                back[step - 2] = self.give_back(step - 2, done[step - 2][2], far_grads[step - 2])
-            rows += [near, far]
-            made = list(expert_chunk(self.kinds, self.own, near, far, *dy[step], gate_w, up_w, down_w))
-            held = [made[3], coming] + (list(parts) if step + 1 < nz else [])
-            if step:
-                held.append(far_grads[step - 1])
+            if step == 0:
+                late = self.send_back(dy_last)
+            if step == nz - 2:
+                last_dy = self.straighten(late)
+                dy.append([last_dy, lay.swap(last_dy, 1)])
+            sent, deps = [], []
+            if step == nz - 1:
+                for n in range(1, nz - 1):
+                    deps.append(add_rows(done[n][0], far_sums[n]))
+                    back[n] = [self.exchange(deps[-1])] if n == 1 else self.send_back(deps[-1])
+                    sent += back[n]
+            made = list(
+                expert_chunk(self.kinds, self.own, *rows[-2:], *dy[step], gate_w, up_w, down_w, *deps)
+            )
+            held = [made[1], coming] + ([near] if step + 1 < nz else [])
+            held += sent[:1] + (late[1:] if step == 1 else []) + (dy[-1][1:] if step == nz - 2 else [])
             held = list(sync(*held))
-            made[3], coming = held[:2]
+            made[1], coming = held[:2]
             if step + 1 < nz:
-                parts = held[2 : 2 + len(parts)]
-            if step:
-                far_grads[step - 1] = held[-1]
+                near = held[2]
+            if step == 1:
+                late[1:] = held[3:]
+            if step == nz - 2:
+                dy[-1][1] = held[3]
+            if step == nz - 1:
+                back[1] = held[2:]
             done.append(made)
-        last = nz - 1
-        far_grads[last] = lay.swap(done[last][3], 1)
-        back[last - 1] = self.give_back(last - 1, done[last - 1][2], far_grads[last - 1])
-        far_outs = [lay.swap(after(d[1], done[last][3]), 1) for d in done]
-        self.outs = [(d[0], other) for d, other in zip(done, far_outs)]
-        total = None
-        for step in list(range(1, nz)) + [0]:
-            if total is not None:
-                total = lay.ring_step(total)
-            if step == last - 1:
-                total, far_grads[last], *back[step] = sync(total, far_grads[last], *back[step])
-                back[last] = self.give_back(last, done[last][2], far_grads[last])
-            elif step == last:
-                total, *back[step] = sync(total, *back[step])
-            total = self.spread(step, back[step], total)
-        total = total.astype(F32)
-        self.tail = back[last][-1]
-        return total[:, : self.width], total[:, self.width : self.width + self.kinds]
-
-    def mixture_parts(self, step, dep):
-        near, far = self.outs[step]
-        return self.give_back(step, near, after(far, dep))
+        self.grads = {}
+        total = self.spread(1, back[1], None)
+        far_sums[nz - 1] = lay.swap(done[-1][1], 1)
+        for n, step in enumerate(list(range(2, nz)) + [0]):
+            coming = lay.ring_step(total)
+            if step not in back:
+                sums = add_rows(done[step][0], far_sums[step])
+                back[step] = [self.exchange(sums)] if step == nz - 1 else self.send_back(sums)
+            beside = list(back[step])
+            if n < 3:
+                self.grads[n] = self.weight_grads(n, total)
+                beside.append(self.grads[n])
+            if n == 0:
+                beside.append(far_sums[nz - 1])
+            coming, *beside = sync(coming, *beside)
+            if n == 0:
+                far_sums[nz - 1] = beside.pop()
+            if n < 3:
+                self.grads[n] = beside.pop()
+            if step == nz - 1:
+                beside[0], far_sums[0] = sync(beside[0], far_sums[0])
+            total = self.spread(step, beside, coming)
+        return total[:, : self.width].astype(F32), total[:, self.width : self.width + self.kinds].astype(F32)
+
+    def out_sum(self, step, *deps):
+        near, far = self.done[step][-2:]
+        return add_rows(near, self.lay.swap(far, 1), *deps)
 
     def weight_grads(self, which, dep):
-        near = 4 + 2 * which
-        mids = [after(d[k], dep) for d in self.done for k in (near, near + 1)]
+        near = 2 + 2 * which
+        mids = [d[k] for d in self.done for k in (near, near + 1)]
         units = mids[0].shape[1]
         if which == 0:
-            return contract_many(mids, [d for pair in self.dy for d in pair], units, self.width)
-        return contract_many(self.rows, mids, self.width, units)
+            return contract_many(mids, [d for pair in self.dy for d in pair], units, self.width, dep)
+        return contract_many(self.rows, mids, self.width, units, dep)
 
 
 def experts_sent(lay, mlp_normed, routes, router_probs, grad_result, gate_w, up_w, down_w):
@@ -782,7 +863,7 @@
     )
     grad_sum = jnp.sum(collect(a2a(grad_copy, ALL)), axis=1)
     weighted = router_probs * jnp.einsum("tk,tke->te", grad_gates, chosen)
-    return (mixture, grad_sum, weighted, lambda which, dep: (grad_down_w, grad_gate_w, grad_up_w)[which])
+    return (mixture, grad_sum, weighted, (grad_down_w, grad_gate_w, grad_up_w))
 
 
 def body(
@@ -814,7 +895,10 @@
     devices = nz * nc
     capacity = 3 * tok_rows * TOP // (2 * expert_count)
     gathered = (
-        devices * tok_rows <= 4 * expert_count * capacity and 3 * expert_count <= NOTES and capacity % 16 == 0
+        nz > 3
+        and devices * tok_rows <= 4 * expert_count * capacity
+        and 3 * expert_count <= NOTES
+        and capacity % 16 == 0
     )
 
     sent = jnp.concatenate(
@@ -822,58 +906,67 @@
     )
     kinds = expert_count + 4
     small = jnp.concatenate(
-        [router_weight] + [g[:, None] for g in (attn_gain, query_gain, key_gain, mlp_gain)], axis=1
+        [router_weight] + [g[:, None] for g in (query_gain, key_gain, mlp_gain, attn_gain)], axis=1
     )
     small = jnp.broadcast_to(small.T.reshape(1, kinds * rb), (devices, kinds * rb))
     block = a2a(sent, "ctx").reshape(nc * rb, 3 * cols)
     parts = [tokens[0]] + [lay.swap(tokens[0], flip) for flip in lay.flips]
+    places = lay.arrival_place()
+    places = jnp.concatenate([places * 2, (places * 2 + 1)[::-1]]).astype(jnp.int32)
     if gathered:
         moe = Gathered(lay, routes[0], expert_count, capacity, width)
         dy_blocks = [moe.noted(cotangent[0])]
         dy_blocks.append(lay.ring_step(dy_blocks[0]))
-        block, dy_blocks[1] = sync(block, dy_blocks[1])
-    ring = [block]
+        offered = moe.offer(dy_blocks[0], width)
+    out_blocks = [out_weight, lay.ring_step(out_weight)]
+    if gathered:
+        block, out_blocks[1], dy_blocks[1], offered, *parts[1:3] = sync(
+            block, out_blocks[1], dy_blocks[1], offered, *parts[1:3]
+        )
+    ring, dy = [block], []
     for step in range(1, nz):
         block = lay.ring_step(block)
         beside = []
         if step == 1:
-            small = a2a(small, ALL)
-            beside = [small] + parts[1:]
+            beside = [a2a(small, ALL)] + parts[1:]
         elif step == 2:
             seq_near = jnp.concatenate(parts, axis=0)
-            seq_far = lay.swap(seq_near, 1)
-            beside = [seq_far]
-            if gathered:
-                dy0 = moe.exchange(moe.offer(0, after(dy_blocks[0], ring[-1]), width))
-                beside += dy0[1:]
+            beside = [lay.swap(seq_near, 1)]
         elif step == 3:
+            beside = [norm_in_order(places, seq_near, seq_far, attn_gain_f[None], half)]
+            if nz == 4:
+                beside.append(lay.head_weights(out_blocks))
+        if gathered and step > 1:
+            dy.append([moe.exchange(offered)])
+            beside.append(dy[-1][0])
+            if step == 2:
+                offered = moe.offer(dy_blocks[1], width)
+                beside.append(offered)
+        if step + 1 < nz:
+            beside.append(lay.ring_step(out_blocks[-1]))
+        block, out_blocks[-1], *beside = sync(block, out_blocks[-1], *beside)
+        if step + 1 < nz:
+            out_blocks.append(beside.pop())
+        if step == 1:
+            small, parts[1:] = beside[0], beside[1:]
             small = small.reshape(devices, kinds, rb).transpose(1, 0, 2).reshape(kinds, width)
             router_t = small[:expert_count]
-            attn_gain_f, qgain_f, kgain_f, mlp_gain_f = (
-                small[expert_count + k].astype(F32) for k in range(4)
-            )
-            places = lay.arrival_place()
-            places = jnp.concatenate([places * 2, (places * 2 + 1)[::-1]]).astype(jnp.int32)
-            normed = norm_in_order(places, seq_near, seq_far, attn_gain_f[None], half)
-            beside = [normed]
-            if gathered:
-                dy = [[moe.joined(dy0)]]
-                dy[0].append(lay.swap(dy[0][0], 1))
-                dy1 = moe.exchange(moe.offer(1, after(dy_blocks[1], ring[-1]), width))
-                beside += [dy[0][1]] + dy1
-        block, *beside = sync(block, *beside)
-        if step == 1:
-            small, parts[1:] = beside[0], beside[1:]
+            qgain_f, kgain_f, mlp_gain_f, attn_gain_f = (small[expert_count + k].astype(F32) for k in range(4))
         elif step == 2:
             seq_far = beside[0]
-            if gathered:
-                dy0[1:] = beside[1:]
         elif step == 3:
             normed = beside[0]
-            if gathered:
-                dy[0][1], dy1 = beside[1], beside[2:]
+            if nz == 4:
+                out_rows = beside.pop(1)
+        if gathered and step > 1:
+            dy[-1][0] = beside[1]
+            if step == 2:
+                offered = beside[2]
         ring.append(block)
-    out_w = lax.all_gather(after(out_weight, ring[2]), ALL, axis=0, tiled=True)
+    if nz < 4:
+        normed = norm_in_order(places, seq_near, seq_far, attn_gain_f[None], half)
+    if nz != 4:
+        out_rows = lay.head_weights(out_blocks)
     if gathered:
         dy_blocks.append(lay.ring_step(after(dy_blocks[1], ring[-1])))
     layers = jnp.stack([lay.layer_at(step) for step in range(nz)]).astype(jnp.int32)
@@ -890,21 +983,25 @@
     if gathered:
         inv, dy_blocks[2] = sync(inv, dy_blocks[2])
         dy_blocks.append(lay.ring_step(dy_blocks[2]))
-        dy.append([moe.joined(dy1)])
-        dy.append(moe.exchange(moe.offer(2, dy_blocks[2], width)))
-    attended_b, *kept = attention.forward(qkv, inv, own_gains)
-    if gathered:
-        attended_b, dy_blocks[3], *dy[2] = sync(attended_b, dy_blocks[3], *dy[2])
-        for pair in dy[1:3]:
+        dy.append([moe.exchange(moe.offer(dy_blocks[2], width))])
+        for pair in dy[:2]:
             pair.append(lay.swap(pair[0], 1))
-        offered = moe.offer(3, dy_blocks[3], width)
-    attended_own = a2a(attended_b.reshape(nc, tok_rows, cols), "ctx")
-    if gathered:
-        attended_own, dy[1][1], dy[2][1], *offered = sync(attended_own, dy[1][1], dy[2][1], *offered)
-        dy.append(moe.exchange(offered))
-    attended_own = lay.head_rows(attended_own)
+    attended_b, *kept = attention.forward(places, qkv, inv, own_gains)
+    if gathered:
+        attended_b, out_rows, dy_blocks[3], dy[2][0], dy[0][1], dy[1][1] = sync(
+            attended_b, out_rows, dy_blocks[3], dy[2][0], dy[0][1], dy[1][1]
+        )
+    near, far = (dot(attended_b[part], out_rows).astype(BF) for part in (slice(0, seq_rows // 2), slice(seq_rows // 2, None)))
+    branch = near.astype(F32) + lay.swap(far, 1).astype(F32)
+    if gathered:
+        offered = moe.offer(dy_blocks[3], width)
+        branch, offered = sync(branch.astype(BF), offered)
+        dy[2].append(lay.swap(dy[2][0], 1))
+    branch = lay.reduce_chips(branch.astype(BF))
+    if gathered:
+        branch, dy[2][1], offered = sync(branch, dy[2][1], offered)
     inputs_f = tokens[0].astype(F32)
-    middle = inputs_f + dot(attended_own, out_w)
+    middle = inputs_f + branch.astype(F32)
     mlp_inv = inverse_rms(middle)
     mlp_normed = (middle * mlp_inv * mlp_gain_f).astype(BF)
     router_probs = jax.nn.softmax(times_transposed(mlp_normed, router_t), axis=-1)
@@ -912,12 +1009,10 @@
     if gathered:
         combine = jnp.where(moe.chosen, router_probs, 0.0)
         high = combine.astype(BF)
-        mlp_normed, high, *dy[3] = sync(mlp_normed, high, *dy[3])
         block = moe.noted(mlp_normed, high, (combine - high.astype(F32)).astype(BF))
         grad_mlp_normed, weighted = moe.run(
-            block, dy, gate_weight[0], up_weight[0], down_weight[0]
+            block, dy, offered, gate_weight[0], up_weight[0], down_weight[0]
         )
-        weight_grads = moe.weight_grads
     else:
         mixture, grad_mlp_normed, weighted, weight_grads = experts_sent(
             lay, mlp_normed, routes[0], router_probs, grad_result, gate_weight[0], up_weight[0], down_weight[0]
@@ -928,30 +1023,15 @@
     grad_middle_norm, grad_mlp_gain = norm_backward(middle, mlp_inv, mlp_gain_f, grad_mlp_normed)
     grad_middle = grad_result + grad_middle_norm
     grad_branch = grad_middle.astype(BF)
-    grad_attended = times_transposed(grad_branch, out_w).astype(BF)
-    grad_heads = a2a(lay.head_blocks(grad_attended), "ctx").reshape(seq_rows, cols)
-
-    if gathered:
-        mix = {1: moe.mixture_parts(1, moe.tail), 2: moe.mixture_parts(2, grad_heads)}
-    scaled_q, scaled_k, grad_value, dots, grad_gains = attention.backward(grad_heads, kept, qkv, inv, own_gains)
-    if gathered:
-        dots, *mix[1] = sync(dots, *mix[1])
-        mixture = lay.ring_step(moe.spread(1, mix[1], None))
-    dots = sum_heads(dots.sum(0))
-
-    def through_norm(scaled, pre, n):
-        inverse = inv[n][:, None]
-        return (inverse * scaled - pre * (inverse * inverse * inverse) * dots[n][:, None]).astype(BF)
-
-    grad_pre = jnp.concatenate(
-        [through_norm(scaled_q, query_pre, 0), through_norm(scaled_k, key_pre, 1), grad_value], axis=-1
-    )
-    grad_qkv = contract_rows(normed, grad_pre).astype(BF)
-    layer_rows = nc * rb
-
-    def qkv_part(step):
-        return lax.dynamic_slice_in_dim(grad_qkv, lay.layer_at(step) * layer_rows, layer_rows, 0)
-
+    branch_near = lay.gather_near(grad_branch)
+    if gathered:
+        branch_near, first = sync(branch_near, moe.out_sum(1))
+        first = moe.exchange(first)
+    branch_far = lay.swap(branch_near, 1)
+    grad_heads = jnp.concatenate(
+        [times_transposed(part, out_rows).astype(BF) for part in (branch_near, branch_far)], axis=0
+    )
+    scaled_q, scaled_k, grad_value, dots, grad_gains = attention.backward(places, grad_heads, kept, qkv, inv, own_gains)
     packed = jnp.concatenate(
         [grad_router_t]
         + [g[None] for g in (lay.all_heads(grad_gains[0]), lay.all_heads(grad_gains[1]), grad_mlp_gain)],
@@ -959,73 +1039,87 @@
     )
     kinds = expert_count + 3
     packed = packed.reshape(kinds, devices, rb).transpose(1, 0, 2).reshape(devices, kinds * rb)
-    packed = a2a(packed, ALL).sum(0).reshape(kinds, rb)
+    if gathered:
+        dots, first, packed = sync(dots, first, packed)
+        mixture = lay.ring_step(moe.spread(1, [first], None))
+    packed = a2a(packed, ALL)
+    dots = sum_heads(dots.sum(0))
+    if gathered:
+        dots, packed, mixture = sync(dots, packed, mixture)
+
+    def through_norm(scaled, pre, n):
+        inverse = inv[n][:, None]
+        return (inverse * scaled - pre * (inverse * inverse * inverse) * dots[n][:, None]).astype(BF)
+
+    grad_pre = jnp.concatenate(
+        [through_norm(scaled_q, query_pre, 0), through_norm(scaled_k, key_pre, 1), grad_value], axis=-1
+    )
+    grad_qkv = grad_blocks(layers, normed, grad_pre)
     halves = jnp.stack([lay.arrival(), 2 * nc - 1 - lay.arrival()], axis=1).reshape(-1).astype(jnp.int32)
-    branch_all = jnp.concatenate(lay.gather_ctx(after(grad_branch, grad_pre)), axis=0)
-    attended_arrival = attended_b.reshape(nc, tok_rows, cols)[lay.arrival()].reshape(seq_rows, cols)
-    grad_out = contract_rows(attended_arrival, branch_all).astype(BF).reshape(hpd, lay.group, rb, width)
     share = cx % lay.group
-    terms = []
-    for k in range(lay.group):
-        term = lax.dynamic_index_in_dim(grad_out, share ^ k, 1, keepdims=False)
-        terms.append(lay.swap(term, k) if k else term)
-    terms = jnp.stack(terms)
-
-    def out_part(step):
+
+    def out_terms(near, far):
+        grad_out = contract_rows(attended_b[: seq_rows // 2], near) + contract_rows(attended_b[seq_rows // 2 :], far)
+        grad_out = grad_out.astype(BF).reshape(hpd, lay.group, rb, width)
+        terms = []
+        for k in range(lay.group):
+            term = lax.dynamic_index_in_dim(grad_out, share ^ k, 1, keepdims=False)
+            terms.append(lay.swap(term, k) if k else term)
+        return jnp.stack(terms)
+
+    def out_part(terms, step):
         layer = lay.layer_at(step)
         return terms[(layer // hpd) ^ share, layer % hpd]
 
-    total, out_total = qkv_part(1), out_part(1)
-    expert_grads = []
-    if gathered:
-        mix.update({step: moe.mixture_parts(step, grad_pre) for step in (3, 0)})
+    total = grad_qkv[1]
+    if not gathered:
+        mixture = mixture.astype(BF)
     for n, step in enumerate(list(range(2, nz)) + [0]):
-        total, out_total = lay.ring_step(total), lay.ring_step(out_total)
-        beside = []
-        if n < 3:
-            expert_grads.append(weight_grads(n, total if n else grad_pre))
-            beside.append(expert_grads[-1])
+        ready = total
+        total = lay.ring_step(total)
         if n == 0:
-            near, far = project_back(layers, halves, grad_pre, ring, half)
-            beside += [near, far]
+            near, far = project_back(layers, halves, grad_pre, ring, half, ready)
+            total, near, far, branch_near = sync(total, near, far, branch_near)
+        elif n == 1:
+            far = lay.swap(far, 1)
             if gathered:
-                mixture, *mix[2] = sync(mixture, *mix[2])
-                mixture = moe.spread(2, mix[2], mixture)
-                beside.append(mixture)
-        elif n == 1:
-            grad_normed = lay.reduce_ctx(near, far)
+                part = moe.exchange(moe.out_sum(2, ready))
+                total, far, part = sync(total, far, part)
+        elif n == 2:
+            terms = out_terms(branch_near, branch_far)
+            grad_normed = lay.reduce_chips((near.astype(F32) + far.astype(F32)).astype(BF))
             if gathered:
-                mixture = lay.ring_step(mixture)
-                beside += [mixture] + mix[3]
-        elif n == 2 and gathered:
-            mixture = lay.ring_step(moe.spread(3, mix[3], mixture))
-            beside.append(mixture)
-        total, out_total, *beside = sync(total, out_total, *beside)
-        if n < 3:
-            expert_grads[-1] = beside.pop(0)
-        if n == 0:
-            near, far = beside[:2]
-            if gathered:
-                mixture = beside[2]
-        elif n == 1 and gathered:
-            mixture, mix[3] = beside[0], beside[1:]
-        elif n == 2 and gathered:
-            mixture = beside[0]
-        total = (total.astype(F32) + qkv_part(step).astype(F32)).astype(BF)
-        out_total = (out_total.astype(F32) + out_part(step).astype(F32)).astype(BF)
+                mixture = lay.ring_step(moe.spread(2, [part], mixture))
+                part = moe.exchange(moe.out_sum(3, ready))
+                total, terms, grad_normed, mixture, part = sync(total, terms, grad_normed, mixture, part)
+                mixture = lay.ring_step(moe.spread(3, [part], mixture))
+                last = moe.send_back(moe.out_sum(0, total))
+            out_total = lay.ring_step(out_part(terms, 1))
+        total = (total.astype(F32) + grad_qkv[step].astype(F32)).astype(BF)
     grad_qkv = a2a(total.reshape(nc, rb, 3 * cols), "ctx")
+    for step in list(range(2, nz)) + [0]:
+        out_total = (out_total.astype(F32) + out_part(terms, step).astype(F32)).astype(BF)
+        if step:
+            out_total = lay.ring_step(out_total)
     grad_out_w = out_total.astype(F32)
-    grad_down_w, grad_gate_w, grad_up_w = expert_grads
-    if gathered:
-        mixture = moe.spread(0, mix[0], mixture).astype(F32)
-    result = middle + mixture
+    if gathered:
+        weight_grads = [moe.grads[n] for n in range(3)]
+    if gathered:
+        mixture = moe.spread(0, last, mixture)
+    grad_down_w, grad_gate_w, grad_up_w = weight_grads
+    result = middle + mixture.astype(F32)
     grad_query_w, grad_key_w, grad_value_w, grad_attn_gain = lay.weight_rows(
-        grad_qkv, (query_weight, key_weight, value_weight)
-    )
-    grad_attn_gain = grad_attn_gain[0] / attn_gain.astype(F32)
+        grad_qkv, (query_weight, key_weight, value_weight), attn_gain
+    )
+    grad_attn_gain = grad_attn_gain[0]
     attn_inv = inverse_rms(inputs_f)
-    grad_inputs_norm, _ = norm_backward(inputs_f, attn_inv, attn_gain_f, grad_normed.astype(F32))
-    grad_inputs = grad_middle + grad_inputs_norm
+    scaled = grad_normed.astype(F32) * attn_gain_f
+    grad_inputs = (
+        grad_middle
+        + attn_inv * scaled
+        - inputs_f * (attn_inv * attn_inv * attn_inv) * jnp.mean(scaled * inputs_f, axis=-1, keepdims=True)
+    )
+    packed = packed.sum(0).reshape(kinds, rb)
     gains = [grad_attn_gain] + [packed[expert_count + k] for k in range(3)]
     return (
         result.astype(BF)[None],

time: 759 us -> 717 us (0.945)
  Pallas kernels: 196 us -> 227 us
  waiting for transfers between devices: 203 us -> 181 us
  other arithmetic: 62.3 us -> 43.2 us
  local copies, waits for them, and re-layouts: 74.1 us -> 55.9 us
  between operations: 16.6 us -> 2.78 us
    pallas_call x2 -> x11, Pallas kernels: 18.8 us -> 52.6 us  [the longest x8 22.8 us: add_rows(): pl.pallas_call(add_kernel, grid=(rows // tile,), in_specs=[row, row] + [p...]
    convert_element_type x16 -> x7, other arithmetic: 36 us -> 13.3 us  [the longest x3 5.89 us: body(): total = (total.astype(F32) + grad_qkv[step].astype(F32)).astype(BF)]
    unnamed x277 -> x210, local copies, waits for them, and re-layouts: 52.2 us -> 29.7 us
    all_to_all x12, waiting for transfers between devices: 41.2 us -> 22.1 us  [exchange(): lax.all_to_all(offered, 'ctx', split_axis=0, concat_axis=0, tiled=True, a...]
    ppermute x42 -> x48, waiting for transfers between devices: 78.2 us -> 90.9 us  [swap(): return lax.ppermute(value, 'ctx', [(i, i ^ bit) for i in range(self.nc)])]
    all_to_all x5 -> x3, waiting for transfers between devices: 12.9 us -> 3.58 us  [a2a(): return lax.all_to_all(value, axes, split_axis=0, concat_axis=0, tiled=True)]
    all_to_all x5 -> x3, starting transfers between devices: 20.8 us -> 13.4 us  [a2a(): return lax.all_to_all(value, axes, split_axis=0, concat_axis=0, tiled=True)]
    ppermute x21 -> x24, starting transfers between devices: 33 us -> 39.4 us  [ring_step(): return lax.ppermute(value, 'dp', self.ring)]
  transfers between devices with their start and end apart: 81 -> 87, of which waited for: 29 -> 35; matrix products, arithmetic and copies ran while one was open for 14% -> 10% of each run, Pallas kernels for 26% -> 31%
where the time goes in v3:
time: 717 us; the launch traced here: 705 us
  Pallas kernels  227 us (32%)
  waiting for transfers between devices  181 us (25%)
  starting transfers between devices  138 us (19%)
  local copies, waits for them, and re-layouts  55.9 us (8%)
  other arithmetic  43.2 us (6%)
  blocking collectives  40.1 us (6%)
  matrix products  17.7 us (2%)
    ppermute x48, waiting for transfers between devices, swap(): return lax.ppermute(value, 'ctx', [(i, i ^ bit) for i in range(self.nc)])  90.9 us
    pallas_call x4, Pallas kernels, expert_chunk(): pl.pallas_call(functools.partial(expert_kernel, kinds), grid_spec=pltpu.P...  66.7 us
    ppermute x24, waiting for transfers between devices, ring_step(): return lax.ppermute(value, 'dp', self.ring)  64.6 us
    all_to_all x12, starting transfers between devices, exchange(): lax.all_to_all(offered, 'ctx', split_axis=0, concat_axis=0, tiled=True, a...  49.1 us
    pallas_call x3, Pallas kernels, contract_many(): pl.pallas_call(functools.partial(contract_kernel, count), grid=(max(rows,...  44.4 us
    ppermute x24, starting transfers between devices, ring_step(): return lax.ppermute(value, 'dp', self.ring)  39.4 us
    ppermute x48, starting transfers between devices, swap(): return lax.ppermute(value, 'ctx', [(i, i ^ bit) for i in range(self.nc)])  35.7 us
    unnamed x210, local copies, waits for them, and re-layouts  29.7 us
  transfers between devices with their start and end apart: 87, of which 35 were waited for; matrix products, arithmetic and copies ran while one was open for 10% of the time, Pallas kernels for 31%

profile of v3, /device:TPU:0, one launch (start us, length us, event | category | flops | bytes accessed | tf_op | source)
XLA Modules:
  0.0 705.4 jit_solution(16080205905972911486)
XLA Ops:
  4.3 5.3 all-to-all-start
  20.8 11.1 %collective-permute-done = bf16[64,2048]{1,0:T(8,128)(2,1)} collective-permute-done((bf16[64,2048]{1,0:T(8,128)(2,1)S(1)}, bf16[64,2048]{1,0:T(8,128)(2,1)}, u32[]{:S(2)}, u32[]{:S(2)}) %collective-permute-start) | collective-permute-done | bytes 262176 | tf_op jit(solution)/shard_map/ppermute | solution.py:71
  40.6 21.0 %all_to_all.175 = bf16[32,2,640]{2,1,0:T(2,128)(2,1)S(1)} all-to-all(bf16[32,2,640]{2,1,0:T(2,128)(2,1)S(1)} %reshape.363), channel_id=1, replica_groups=mesh['dp'=4,'ctx'=8] {'dp','ctx'}, dimensions={0} | all-to-all | bytes 163840 | tf_op jit(solution)/shard_map/all_to_all | solution.py:200
  76.3 19.9 %collective-permute-done.9 = bf16[64,2048]{1,0:T(8,128)(2,1)} collective-permute-done((bf16[64,2048]{1,0:T(8,128)(2,1)}, bf16[64,2048]{1,0:T(8,128)(2,1)}, u32[]{:S(2)}, u32[]{:S(2)}) %collective-permute-start.9) | collective-permute-done | bytes 262176 | tf_op jit(solution)/shard_map/ppermute | solution.py:71
  106.4 9.9 %shard_map.301.rows = bf16[1024,2048]{1,0:T(8,128)(2,1)S(1)} custom-call(s32[16]{0:T(128)S(1)} %pad_add_fusion.1.place_ref, bf16[512,2048]{1,0:T(8,128)(2,1)S(1)} %pad_maximum_fusion.near, bf16[512,2048]{1,0:T(8,128)(2,1)} %collective-permute-done.8.far, f32[1,2048]{1,0:T(1,128)S(1)} %reshape.315.gain), custom_call_target="tpu_custom_call" | custom-call | flops 8388608 | bytes 12582912 | tf_op jit(solution)/shard_map/pallas_call | solution.py:435
  129.0 6.6 shard_map.302
  137.3 9.7 %all_gather.6 = f32[8,16,128]{2,1,0:T(8,128)S(1)} all-gather(f32[1,16,128]{2,1,0:T(8,128)S(1)} %all_gather_reshape.6), channel_id=1, replica_groups=mesh['dp'=4,'ctx'=8] {'ctx'}, dimensions={0}, use_global_device_ids=true | all-gather | bytes 73728 | tf_op jit(solution)/shard_map/all_gather | solution.py:977
  158.8 11.6 %shard_map.303 = (bf16[1024,256]{1,0:T(8,128)(2,1)}, f32[1024,256]{1,0:T(8,128)}, f32[1024,256]{1,0:T(8,128)}, bf16[1024,256]{1,0:T(8,128)(2,1)}, bf16[1024,256]{1,0:T(8,128)(2,1)}, /*index=5*/bf16[1024,256]{1,0:T(8,128)(2,1)}) custom-call(s32[16]{0:T(128)} %copy-done.52, f32[1024,768]{1,0:T(8,128)} %copy-done, f32[1024,768]{1,0:T(8,128)} %copy-done, ...), custom_call_target="tpu_custom_call" | custom-call | flops 805306368 | bytes 6291456 | tf_op jit(solution)/shard_map/pallas_call | solution.py:674
  186.0 10.9 %collective-permute-done.17 = bf16[2,64,2048]{2,1,0:T(8,128)(2,1)S(1)} collective-permute-done((bf16[2,64,2048]{2,1,0:T(8,128)(2,1)}, bf16[2,64,2048]{2,1,0:T(8,128)(2,1)S(1)}, u32[]{:S(2)}, u32[]{:S(2)}) %collective-permute-start.17) | collective-permute-done | bytes 524320 | tf_op jit(solution)/shard_map/ppermute | solution.py:68
  200.4 5.3 collective-permute-done.18
  220.2 10.2 %collective-permute-done.22.block.notes = bf16[128,2176]{1,0:T(8,128)(2,1)S(1)} collective-permute-done((bf16[128,2176]{1,0:T(8,128)(2,1)S(1)}, bf16[128,2176]{1,0:T(8,128)(2,1)S(1)}, u32[]{:S(2)}, u32[]{:S(2)}) %collective-permute-start.22) | collective-permute-done | bytes 557088 | tf_op jit(solution)/shard_map/ppermute | solution.py:71
  230.4 5.3 all-to-all-done.5
  247.1 16.6 %shard_map.307 = (bf16[384,2176]{1,0:T(8,128)(2,1)}, bf16[384,2176]{1,0:T(8,128)(2,1)}, bf16[384,512]{1,0:T(8,128)(2,1)}, bf16[384,512]{1,0:T(8,128)(2,1)}, bf16...) custom-call(s32[1]{0:T(128)} %bitcast.178, ...), custom_call_target="tpu_custom_call" | custom-call | flops 9663676416 | bytes 12582912 | tf_op jit(solution)/shard_map/pallas_call | solution.py:366
  280.9 16.6 %shard_map.309 = (bf16[384,2176]{1,0:T(8,128)(2,1)}, bf16[384,2176]{1,0:T(8,128)(2,1)}, bf16[384,512]{1,0:T(8,128)(2,1)}, bf16[384,512]{1,0:T(8,128)(2,1)}, bf16...) custom-call(s32[1]{0:T(128)} %bitcast.179, ...), custom_call_target="tpu_custom_call" | custom-call | flops 9663676416 | bytes 12582912 | tf_op jit(solution)/shard_map/pallas_call | solution.py:366
  302.7 7.0 collective-permute-done.29
  320.6 16.7 %shard_map.311 = (bf16[384,2176]{1,0:T(8,128)(2,1)}, bf16[384,2176]{1,0:T(8,128)(2,1)}, bf16[384,512]{1,0:T(8,128)(2,1)}, bf16[384,512]{1,0:T(8,128)(2,1)}, bf16...) custom-call(s32[1]{0:T(128)} %bitcast.180, ...), custom_call_target="tpu_custom_call" | custom-call | flops 9663676416 | bytes 12582912 | tf_op jit(solution)/shard_map/pallas_call | solution.py:366
  353.7 16.8 %shard_map.315 = (bf16[384,2176]{1,0:T(8,128)(2,1)}, bf16[384,2176]{1,0:T(8,128)(2,1)}, bf16[384,512]{1,0:T(8,128)(2,1)}, bf16[384,512]{1,0:T(8,128)(2,1)}, bf16...) custom-call(s32[1]{0:T(128)} %bitcast.181, ...), custom_call_target="tpu_custom_call" | custom-call | flops 9663676416 | bytes 12582912 | tf_op jit(solution)/shard_map/pallas_call | solution.py:366
  378.9 6.5 collective-permute-done.39.refs_3_
  389.5 15.1 %shard_map.317 = f32[512,2048]{1,0:T(8,128)} custom-call(bf16[384,512]{1,0:T(8,128)(2,1)} %get-tuple-element.230.refs_0_, bf16[384,512]{1,0:T(8,128)(2,1)} %get-tuple-element.231.refs_1_, bf16[384,512]{1,0:T(8,128)(2,1)} %get-tuple-element.232.refs_2_, bf16[384,512]{1,0:T(8,128)(2,1)} %get-tuple-element.233.refs_3_, ...), custom_call_target="tpu_custom_call" | custom-call | flops 6442450944 | bytes 19922944 | tf_op jit(solution)/shard_map/pallas_call | solution.py:398
  418.5 14.6 %shard_map.320 = f32[2048,512]{1,0:T(8,128)} custom-call(bf16[384,2176]{1,0:T(8,128)(2,1)} %bitcast.41.near.refs_0_, bf16[384,2176]{1,0:T(8,128)(2,1)} %collective-permute-done.23.far.refs_1_, bf16[384,2176]{1,0:T(8,128)(2,1)} %bitcast.47.near.refs_2_, bf16[384,2176]{1,0:T(8,128)(2,1)} %collective-permute-done.26.far.refs_3_, ...), custom_call_target="tpu_custom_call" | custom-call | flops 6442450944 | bytes 19922944 | tf_op jit(solution)/shard_map/pallas_call | solution.py:398
  444.4 14.6 %shard_map.323 = f32[2048,512]{1,0:T(8,128)} custom-call(bf16[384,2176]{1,0:T(8,128)(2,1)} %bitcast.41.near.refs_0_, bf16[384,2176]{1,0:T(8,128)(2,1)} %collective-permute-done.23.far.refs_1_, bf16[384,2176]{1,0:T(8,128)(2,1)} %bitcast.47.near.refs_2_, bf16[384,2176]{1,0:T(8,128)(2,1)} %collective-permute-done.26.far.refs_3_, ...), custom_call_target="tpu_custom_call" | custom-call | flops 6442450944 | bytes 19922944 | tf_op jit(solution)/shard_map/pallas_call | solution.py:398
  470.6 8.5 %collective-permute-done.49 = bf16[128,2048]{1,0:T(8,128)(2,1)S(1)} collective-permute-done((bf16[128,2048]{1,0:T(8,128)(2,1)S(1)}, bf16[128,2048]{1,0:T(8,128)(2,1)S(1)}, u32[]{:S(2)}, u32[]{:S(2)}) %collective-permute-start.49) | collective-permute-done | bytes 524320 | tf_op jit(solution)/shard_map/ppermute | solution.py:68
  479.1 9.9 %collective-permute-done.48 = bf16[128,2048]{1,0:T(8,128)(2,1)S(1)} collective-permute-done((bf16[128,2048]{1,0:T(8,128)(2,1)S(1)}, bf16[128,2048]{1,0:T(8,128)(2,1)S(1)}, u32[]{:S(2)}, u32[]{:S(2)}) %collective-permute-start.48) | collective-permute-done | bytes 524320 | tf_op jit(solution)/shard_map/ppermute | solution.py:68
  501.1 11.0 %shard_map.326 = (f32[1024,256]{1,0:T(8,128)}, f32[1024,256]{1,0:T(8,128)}, bf16[1024,256]{1,0:T(8,128)(2,1)}, f32[2,2,1024]{2,1,0:T(2,128)}, f32[2,256]{1,0:T(2,128)}) custom-call(s32[16]{0:T(128)} %copy-done.52, bf16[1024,256]{1,0:T(8,128)(2,1)} %pad_maximum_fusion.9.sent_grad, f32[1024,256]{1,0:T(8,128)} %get-tuple-element.276.attended, ...), custom_call_target="tpu_custom_call" | custom-call | flops 1610612736 | bytes 6291456 | tf_op jit(solution)/shard_map/pallas_call | solution.py:684
  527.6 9.4 %all_gather.7 = f32[8,16,128]{2,1,0:T(8,128)S(1)} all-gather(f32[1,16,128]{2,1,0:T(8,128)S(1)} %all_gather_reshape.7), channel_id=1, replica_groups=mesh['dp'=4,'ctx'=8] {'ctx'}, dimensions={0}, use_global_device_ids=true | all-gather | bytes 73728 | tf_op jit(solution)/shard_map/all_gather | solution.py:977
  544.0 7.3 %shard_map.328 = (bf16[512,768]{1,0:T(8,128)(2,1)S(1)}, bf16[512,768]{1,0:T(8,128)(2,1)}, bf16[512,768]{1,0:T(8,128)(2,1)S(1)}, bf16[512,768]{1,0:T(8,128)(2,1)S(1)}) custom-call(s32[4]{0:T(128)S(1)} %pad_add_fusion.2.layer_ref, bf16[1024,2048]{1,0:T(8,128)(2,1)} %copy-done.18, bf16[1024,768]{1,0:T(8,128)(2,1)S(1)} %pad_maximum_fusion.2.grads), custom_call_target="tpu_custom_call" | custom-call | flops 3221225472 | bytes 7340032 | tf_op jit(solution)/shard_map/pallas_call | solution.py:507
  555.3 6.6 shard_map.329
  561.9 11.9 %collective-permute-done.53 = bf16[512,768]{1,0:T(8,128)(2,1)} collective-permute-done((bf16[512,768]{1,0:T(8,128)(2,1)}, bf16[512,768]{1,0:T(8,128)(2,1)}, u32[]{:S(2)}, u32[]{:S(2)}) %collective-permute-start.53) | collective-permute-done | bytes 786464 | tf_op jit(solution)/shard_map/ppermute | solution.py:71
  599.9 6.6 all-to-all-done.13
  635.5 14.1 %collective-permute-done.60 = bf16[1,64,2048]{2,1,0:T(8,128)(2,1)S(1)} collective-permute-done((bf16[1,64,2048]{2,1,0:T(8,128)(2,1)S(1)}, bf16[1,64,2048]{2,1,0:T(8,128)(2,1)S(1)}, u32[]{:S(2)}, u32[]{:S(2)}) %collective-permute-start.60) | collective-permute-done | bytes 262176 | tf_op jit(solution)/shard_map/ppermute | solution.py:68
  678.7 12.5 %collective-permute-done.67.refs_3_ = bf16[96,2048]{1,0:T(8,128)(2,1)S(1)} collective-permute-done((bf16[96,2048]{1,0:T(8,128)(2,1)}, bf16[96,2048]{1,0:T(8,128)(2,1)S(1)}, u32[]{:S(2)}, u32[]{:S(2)}) %collective-permute-start.67) | collective-permute-done | bytes 393248 | tf_op jit(solution)/shard_map/ppermute | solution.py:68
  691.2 7.0 collective-permute-done.66.refs_2_
  (545 shorter events, 346.5 us)
Async XLA Ops:
  4.3 28.4 %all-to-all-start = ((bf16[8,64,768]{2,1,0:T(8,128)(2,1)}), bf16[8,64,768]{2,1,0:T(8,128)(2,1)S(1)}, u32[]{:S(2)}, u32[]{:S(2)}) async-start(bf16[8,64,768]{2,1,0:T(8,128)(2,1)} %pad_maximum_fusion.5), calls=%async_computation | async-start | bytes 1572864 | tf_op jit(solution)/shard_map/all_to_all | solution.py:200
  32.7 29.0 %collective-permute-start.4 = (bf16[512,768]{1,0:T(8,128)(2,1)S(1)}, bf16[512,768]{1,0:T(8,128)(2,1)S(1)}, u32[]{:S(2)}, u32[]{:S(2)}) collective-permute-start(bf16[512,768]{1,0:T(8,128)(2,1)S(1)} %bitcast.175), channel_id=1, source_target_pairs={{0,8},{8,24},{24,16},{16,0},{1,9},{9,25},{25,17},{17,1},{2,10},{10... | collective-permute-start | bytes 2359304 | tf_op jit(solution)/shard_map/ppermute | solution.py:71
  34.4 27.3 %collective-permute-start.5 = (bf16[128,2048]{1,0:T(8,128)(2,1)S(1)}, bf16[128,2048]{1,0:T(8,128)(2,1)}, u32[]{:S(2)}, u32[]{:S(2)}) collective-permute-start(bf16[128,2048]{1,0:T(8,128)(2,1)S(1)} %bitcast.185), channel_id=1, source_target_pairs={{0,6},{1,7},{2,4},{3,5},{4,2},{5,3},{6,0},{7,1},{8,14},{9,15},{10,... | collective-permute-start | bytes 1572872 | tf_op jit(solution)/shard_map/ppermute | solution.py:68
  35.8 25.9 %collective-permute-start.6 = (bf16[64,2048]{1,0:T(8,128)(2,1)}, bf16[64,2048]{1,0:T(8,128)(2,1)S(1)}, u32[]{:S(2)}, u32[]{:S(2)}) collective-permute-start(bf16[64,2048]{1,0:T(8,128)(2,1)} %collective-permute-done), channel_id=1, source_target_pairs={{0,8},{8,24},{24,16},{16,0},{1,9},{9,25},{25,17},{17,1},{2,10},{10... | collective-permute-start | bytes 786440 | tf_op jit(solution)/shard_map/ppermute | solution.py:71
  65.0 31.3 %collective-permute-start.8 = (bf16[512,2048]{1,0:T(8,128)(2,1)S(1)}, bf16[512,2048]{1,0:T(8,128)(2,1)}, u32[]{:S(2)}, u32[]{:S(2)}) collective-permute-start(bf16[512,2048]{1,0:T(8,128)(2,1)S(1)} %pad_maximum_fusion.near), channel_id=1, source_target_pairs={{0,1},{1,0},{2,3},{3,2},{4,5},{5,4},{6,7},{7,6},{8,9},{9,8},{10,11... | collective-permute-start | bytes 6291464 | tf_op jit(solution)/shard_map/ppermute | solution.py:68
  65.2 31.1 %all-to-all-start.2 = ((bf16[4,96,2048]{2,1,0:T(8,128)(2,1)}), bf16[4,96,2048]{2,1,0:T(8,128)(2,1)}, u32[]{:S(2)}, u32[]{:S(2)}) async-start(bf16[4,96,2048]{2,1,0:T(8,128)(2,1)} %bitcast.169), calls=%async_computation.2 | async-start | bytes 3145728 | tf_op jit(solution)/shard_map/all_to_all | solution.py:709
  69.5 26.7 %collective-permute-start.7 = (bf16[512,768]{1,0:T(8,128)(2,1)}, bf16[512,768]{1,0:T(8,128)(2,1)}, u32[]{:S(2)}, u32[]{:S(2)}) collective-permute-start(bf16[512,768]{1,0:T(8,128)(2,1)} %copy-done.54), channel_id=1, source_target_pairs={{0,8},{8,24},{24,16},{16,0},{1,9},{9,25},{25,17},{17,1},{2,10},{10... | collective-permute-start | bytes 2359304 | tf_op jit(solution)/shard_map/ppermute | solution.py:71
  70.2 26.0 %collective-permute-start.9 = (bf16[64,2048]{1,0:T(8,128)(2,1)}, bf16[64,2048]{1,0:T(8,128)(2,1)}, u32[]{:S(2)}, u32[]{:S(2)}) collective-permute-start(bf16[64,2048]{1,0:T(8,128)(2,1)} %copy-done.88), channel_id=1, source_target_pairs={{0,8},{8,24},{24,16},{16,0},{1,9},{9,25},{25,17},{17,1},{2,10},{10... | collective-permute-start | bytes 786440 | tf_op jit(solution)/shard_map/ppermute | solution.py:71
  96.3 29.7 %all-to-all-start.3 = ((bf16[4,96,2048]{2,1,0:T(8,128)(2,1)}), bf16[4,96,2048]{2,1,0:T(8,128)(2,1)}, u32[]{:S(2)}, u32[]{:S(2)}) async-start(bf16[4,96,2048]{2,1,0:T(8,128)(2,1)} %bitcast.170), calls=%async_computation.3 | async-start | bytes 3145728 | tf_op jit(solution)/shard_map/all_to_all | solution.py:709
  126.3 44.1 %collective-permute-start.14 = (bf16[384,2048]{1,0:T(8,128)(2,1)}, bf16[384,2048]{1,0:T(8,128)(2,1)}, u32[]{:S(2)}, u32[]{:S(2)}) collective-permute-start(bf16[384,2048]{1,0:T(8,128)(2,1)} %bitcast.17.dy_near.refs_8_), channel_id=1, source_target_pairs={{0,1},{1,0},{2,3},{3,2},{4,5},{5,4},{6,7},{7,6},{8,9},{9,8},{10,11... | collective-permute-start | bytes 4718600 | tf_op jit(solution)/shard_map/ppermute | solution.py:68
  126.3 44.1 %collective-permute-start.15 = (bf16[384,2048]{1,0:T(8,128)(2,1)}, bf16[384,2048]{1,0:T(8,128)(2,1)}, u32[]{:S(2)}, u32[]{:S(2)}) collective-permute-start(bf16[384,2048]{1,0:T(8,128)(2,1)} %bitcast.28.dy_near.refs_10_), channel_id=1, source_target_pairs={{0,1},{1,0},{2,3},{3,2},{4,5},{5,4},{6,7},{7,6},{8,9},{9,8},{10,11... | collective-permute-start | bytes 4718600 | tf_op jit(solution)/shard_map/ppermute | solution.py:68
  238.7 25.7 %all-to-all-start.6 = ((bf16[4,96,2176]{2,1,0:T(8,128)(2,1)}), bf16[4,96,2176]{2,1,0:T(8,128)(2,1)}, u32[]{:S(2)}, u32[]{:S(2)}) async-start(bf16[4,96,2176]{2,1,0:T(8,128)(2,1)} %bitcast.46), calls=%async_computation.6 | async-start | bytes 3342336 | tf_op jit(solution)/shard_map/all_to_all | solution.py:709
  267.4 42.5 %all-to-all-start.7 = ((bf16[4,96,2176]{2,1,0:T(8,128)(2,1)}), bf16[4,96,2176]{2,1,0:T(8,128)(2,1)}, u32[]{:S(2)}, u32[]{:S(2)}) async-start(bf16[4,96,2176]{2,1,0:T(8,128)(2,1)} %bitcast.48), calls=%async_computation.7 | async-start | bytes 3342336 | tf_op jit(solution)/shard_map/all_to_all | solution.py:709
  274.0 28.7 %collective-permute-start.30 = (bf16[96,2048]{1,0:T(8,128)(2,1)S(1)}, bf16[96,2048]{1,0:T(8,128)(2,1)S(1)}, u32[]{:S(2)}, u32[]{:S(2)}) collective-permute-start(bf16[96,2048]{1,0:T(8,128)(2,1)S(1)} %get-tuple-element.353), channel_id=1, source_target_pairs={{0,6},{1,7},{2,4},{3,5},{4,2},{5,3},{6,0},{7,1},{8,14},{9,15},{10,... | collective-permute-start | bytes 1179656 | tf_op jit(solution)/shard_map/ppermute | solution.py:68
  276.9 32.9 %collective-permute-start.29 = (bf16[96,2048]{1,0:T(8,128)(2,1)S(1)}, bf16[96,2048]{1,0:T(8,128)(2,1)S(1)}, u32[]{:S(2)}, u32[]{:S(2)}) collective-permute-start(bf16[96,2048]{1,0:T(8,128)(2,1)S(1)} %get-tuple-element.354), channel_id=1, source_target_pairs={{0,4},{1,5},{2,6},{3,7},{4,0},{5,1},{6,2},{7,3},{8,12},{9,13},{10,... | collective-permute-start | bytes 1179656 | tf_op jit(solution)/shard_map/ppermute | solution.py:68
  277.4 32.4 %collective-permute-start.28 = (bf16[96,2048]{1,0:T(8,128)(2,1)S(1)}, bf16[96,2048]{1,0:T(8,128)(2,1)S(1)}, u32[]{:S(2)}, u32[]{:S(2)}) collective-permute-start(bf16[96,2048]{1,0:T(8,128)(2,1)S(1)} %get-tuple-element.355), channel_id=1, source_target_pairs={{0,2},{1,3},{2,0},{3,1},{4,6},{5,7},{6,4},{7,5},{8,10},{9,11},{10,... | collective-permute-start | bytes 1179656 | tf_op jit(solution)/shard_map/ppermute | solution.py:68
  277.5 32.3 %collective-permute-start.27 = (bf16[128,2176]{1,0:T(8,128)(2,1)S(1)}, bf16[128,2176]{1,0:T(8,128)(2,1)S(1)}, u32[]{:S(2)}, u32[]{:S(2)}) collective-permute-start(bf16[128,2176]{1,0:T(8,128)(2,1)S(1)} %collective-permute-done.25.block.notes), channel_id=1, source_target_pairs={{0,8},{8,24},{24,16},{16,0},{1,9},{9,25},{25,17},{17,1},{2,10},{10... | collective-permute-start | bytes 1671176 | tf_op jit(solution)/shard_map/ppermute | solution.py:71
  312.4 28.9 %collective-permute-start.32 = (bf16[384,2048]{1,0:T(8,128)(2,1)}, bf16[384,2048]{1,0:T(8,128)(2,1)}, u32[]{:S(2)}, u32[]{:S(2)}) collective-permute-start(bf16[384,2048]{1,0:T(8,128)(2,1)} %constant_dynamic-update-slice_fusion.2.dy_near.refs_14_), channel_id=1, source_target_pairs={{0,1},{1,0},{2,3},{3,2},{4,5},{5,4},{6,7},{7,6},{8,9},{9,8},{10,11... | collective-permute-start | bytes 4718600 | tf_op jit(solution)/shard_map/ppermute | solution.py:68
  370.9 33.8 %collective-permute-start.40 = (bf16[384,2176]{1,0:T(8,128)(2,1)}, bf16[384,2176]{1,0:T(8,128)(2,1)S(1)}, u32[]{:S(2)}, u32[]{:S(2)}) collective-permute-start(bf16[384,2176]{1,0:T(8,128)(2,1)} %get-tuple-element.238), channel_id=1, source_target_pairs={{0,1},{1,0},{2,3},{3,2},{4,5},{5,4},{6,7},{7,6},{8,9},{9,8},{10,11... | collective-permute-start | bytes 5013512 | tf_op jit(solution)/shard_map/ppermute | solution.py:68
  374.6 59.6 %collective-permute-start.42 = (bf16[384,2176]{1,0:T(8,128)(2,1)}, bf16[384,2176]{1,0:T(8,128)(2,1)}, u32[]{:S(2)}, u32[]{:S(2)}) collective-permute-start(bf16[384,2176]{1,0:T(8,128)(2,1)} %get-tuple-element.255), channel_id=1, source_target_pairs={{0,1},{1,0},{2,3},{3,2},{4,5},{5,4},{6,7},{7,6},{8,9},{9,8},{10,11... | collective-permute-start | bytes 5013512 | tf_op jit(solution)/shard_map/ppermute | solution.py:68
  374.8 29.8 %collective-permute-start.38 = (bf16[96,2176]{1,0:T(8,128)(2,1)}, bf16[96,2176]{1,0:T(8,128)(2,1)S(1)}, u32[]{:S(2)}, u32[]{:S(2)}) collective-permute-start(bf16[96,2176]{1,0:T(8,128)(2,1)} %get-tuple-element.345), channel_id=1, source_target_pairs={{0,4},{1,5},{2,6},{3,7},{4,0},{5,1},{6,2},{7,3},{8,12},{9,13},{10,... | collective-permute-start | bytes 1253384 | tf_op jit(solution)/shard_map/ppermute | solution.py:68
  375.3 29.3 %collective-permute-start.37 = (bf16[96,2176]{1,0:T(8,128)(2,1)}, bf16[96,2176]{1,0:T(8,128)(2,1)S(1)}, u32[]{:S(2)}, u32[]{:S(2)}) collective-permute-start(bf16[96,2176]{1,0:T(8,128)(2,1)} %get-tuple-element.346), channel_id=1, source_target_pairs={{0,2},{1,3},{2,0},{3,1},{4,6},{5,7},{6,4},{7,5},{8,10},{9,11},{10,... | collective-permute-start | bytes 1253384 | tf_op jit(solution)/shard_map/ppermute | solution.py:68
  406.8 27.3 %all-to-all-start.10 = ((bf16[4,96,2176]{2,1,0:T(8,128)(2,1)}), bf16[4,96,2176]{2,1,0:T(8,128)(2,1)S(1)}, u32[]{:S(2)}, u32[]{:S(2)}) async-start(bf16[4,96,2176]{2,1,0:T(8,128)(2,1)} %bitcast.54), calls=%async_computation.10 | async-start | bytes 3342336 | tf_op jit(solution)/shard_map/all_to_all | solution.py:709
  410.7 56.2 %collective-permute-start.50 = (bf16[384,2048]{1,0:T(8,128)(2,1)}, bf16[384,2048]{1,0:T(8,128)(2,1)}, u32[]{:S(2)}, u32[]{:S(2)}) collective-permute-start(bf16[384,2048]{1,0:T(8,128)(2,1)} %get-tuple-element.274), channel_id=1, source_target_pairs={{0,1},{1,0},{2,3},{3,2},{4,5},{5,4},{6,7},{7,6},{8,9},{9,8},{10,11... | collective-permute-start | bytes 4718600 | tf_op jit(solution)/shard_map/ppermute | solution.py:68
  527.3 51.8 %collective-permute-start.56 = (bf16[384,2048]{1,0:T(8,128)(2,1)}, bf16[384,2048]{1,0:T(8,128)(2,1)}, u32[]{:S(2)}, u32[]{:S(2)}) collective-permute-start(bf16[384,2048]{1,0:T(8,128)(2,1)} %get-tuple-element.298), channel_id=1, source_target_pairs={{0,1},{1,0},{2,3},{3,2},{4,5},{5,4},{6,7},{7,6},{8,9},{9,8},{10,11... | collective-permute-start | bytes 4718600 | tf_op jit(solution)/shard_map/ppermute | solution.py:68
  573.8 32.7 %collective-permute-start.55 = (bf16[512,2048]{1,0:T(8,128)(2,1)}, bf16[512,2048]{1,0:T(8,128)(2,1)}, u32[]{:S(2)}, u32[]{:S(2)}) collective-permute-start(bf16[512,2048]{1,0:T(8,128)(2,1)} %get-tuple-element.296), channel_id=1, source_target_pairs={{0,1},{1,0},{2,3},{3,2},{4,5},{5,4},{6,7},{7,6},{8,9},{9,8},{10,11... | collective-permute-start | bytes 6291464 | tf_op jit(solution)/shard_map/ppermute | solution.py:68
  591.9 67.0 %collective-permute-start.24 = (bf16[384,2048]{1,0:T(8,128)(2,1)}, bf16[384,2048]{1,0:T(8,128)(2,1)}, u32[]{:S(2)}, u32[]{:S(2)}) collective-permute-start(bf16[384,2048]{1,0:T(8,128)(2,1)} %get-tuple-element.207), channel_id=1, source_target_pairs={{0,1},{1,0},{2,3},{3,2},{4,5},{5,4},{6,7},{7,6},{8,9},{9,8},{10,11... | collective-permute-start | bytes 4718600 | tf_op jit(solution)/shard_map/ppermute | solution.py:68
  592.0 25.7 %collective-permute-start.64 = (bf16[384,2048]{1,0:T(8,128)(2,1)}, bf16[384,2048]{1,0:T(8,128)(2,1)}, u32[]{:S(2)}, u32[]{:S(2)}) collective-permute-start(bf16[384,2048]{1,0:T(8,128)(2,1)} %get-tuple-element.307), channel_id=1, source_target_pairs={{0,1},{1,0},{2,3},{3,2},{4,5},{5,4},{6,7},{7,6},{8,9},{9,8},{10,11... | collective-permute-start | bytes 4718600 | tf_op jit(solution)/shard_map/ppermute | solution.py:68
  616.4 34.2 %collective-permute-start.57 = (bf16[512,768]{1,0:T(8,128)(2,1)}, bf16[512,768]{1,0:T(8,128)(2,1)}, u32[]{:S(2)}, u32[]{:S(2)}) collective-permute-start(bf16[512,768]{1,0:T(8,128)(2,1)} %add_convert_fusion.3.refs_0_), channel_id=1, source_target_pairs={{0,8},{8,24},{24,16},{16,0},{1,9},{9,25},{25,17},{17,1},{2,10},{10... | collective-permute-start | bytes 2359304 | tf_op jit(solution)/shard_map/ppermute | solution.py:71
  621.3 29.3 %all-to-all-start.14 = ((bf16[4,96,2048]{2,1,0:T(8,128)(2,1)}), bf16[4,96,2048]{2,1,0:T(8,128)(2,1)S(1)}, u32[]{:S(2)}, u32[]{:S(2)}) async-start(bf16[4,96,2048]{2,1,0:T(8,128)(2,1)} %bitcast.174), calls=%async_computation.14 | async-start | bytes 3145728 | tf_op jit(solution)/shard_map/all_to_all | solution.py:709
  655.3 42.9 %collective-permute-start.68 = (bf16[128,2048]{1,0:T(8,128)(2,1)}, bf16[128,2048]{1,0:T(8,128)(2,1)S(1)}, u32[]{:S(2)}, u32[]{:S(2)}) collective-permute-start(bf16[128,2048]{1,0:T(8,128)(2,1)} %shard_map.334), channel_id=1, source_target_pairs={{0,8},{8,24},{24,16},{16,0},{1,9},{9,25},{25,17},{17,1},{2,10},{10... | collective-permute-start | bytes 1572872 | tf_op jit(solution)/shard_map/ppermute | solution.py:71
  666.1 35.8 %all-to-all-start.15 = ((bf16[8,64,768]{2,1,0:T(8,128)(2,1)}), bf16[8,64,768]{2,1,0:T(8,128)(2,1)S(1)}, u32[]{:S(2)}, u32[]{:S(2)}) async-start(bf16[8,64,768]{2,1,0:T(8,128)(2,1)} %bitcast.194), calls=%async_computation.15 | async-start | bytes 1572864 | tf_op jit(solution)/shard_map/all_to_all | solution.py:200
  (158 other events, 2631.3 us)

commit v4 on v3

--- a/solution.py
+++ b/solution.py
@@ -482,7 +482,7 @@
             ],
         ),
         out_shape=[jax.ShapeDtypeStruct((total, wide), F32), jax.ShapeDtypeStruct((2, total), F32)],
-        compiler_params=pltpu.CompilerParams(vmem_limit_bytes=40 * 2**20),
+        compiler_params=pltpu.CompilerParams(vmem_limit_bytes=60 * 2**20),
         cost_estimate=pl.CostEstimate(
             flops=2 * total * width * wide, bytes_accessed=2 * total * width + 6 * total * wide, transcendentals=0
         ),
@@ -763,6 +763,7 @@
             )
             held = [made[1], coming] + ([near] if step + 1 < nz else [])
             held += sent[:1] + (late[1:] if step == 1 else []) + (dy[-1][1:] if step == nz - 2 else [])
+            held += [far_sums[0]] if step == nz - 1 else []
             held = list(sync(*held))
             made[1], coming = held[:2]
             if step + 1 < nz:
@@ -772,7 +773,7 @@
             if step == nz - 2:
                 dy[-1][1] = held[3]
             if step == nz - 1:
-                back[1] = held[2:]
+                back[1], far_sums[0] = held[2:3], held[3]
             done.append(made)
         self.grads = {}
         total = self.spread(1, back[1], None)
@@ -1025,8 +1026,8 @@
     grad_branch = grad_middle.astype(BF)
     branch_near = lay.gather_near(grad_branch)
     if gathered:
-        branch_near, first = sync(branch_near, moe.out_sum(1))
-        first = moe.exchange(first)
+        branch_near, first, *out_sums = sync(branch_near, *(moe.out_sum(n) for n in (1, 2, 3, 0)))
+        first, second = moe.exchange(first), moe.send_back(out_sums.pop(0))
     branch_far = lay.swap(branch_near, 1)
     grad_heads = jnp.concatenate(
         [times_transposed(part, out_rows).astype(BF) for part in (branch_near, branch_far)], axis=0
@@ -1079,23 +1080,29 @@
         total = lay.ring_step(total)
         if n == 0:
             near, far = project_back(layers, halves, grad_pre, ring, half, ready)
-            total, near, far, branch_near = sync(total, near, far, branch_near)
+            beside = second + out_sums if gathered else []
+            total, near, far, branch_near, *beside = sync(total, near, far, branch_near, *beside)
         elif n == 1:
-            far = lay.swap(far, 1)
+            terms = out_terms(branch_near, branch_far)
+            grad_normed = lay.reduce_ctx(near, far)
             if gathered:
-                part = moe.exchange(moe.out_sum(2, ready))
-                total, far, part = sync(total, far, part)
+                mixture = lay.ring_step(moe.spread(2, beside[:-2], mixture))
+                part = moe.exchange(beside[-2])
+                beside = [mixture, part, beside[-1]]
+            total, terms, grad_normed, *beside = sync(total, terms, grad_normed, *beside)
         elif n == 2:
-            terms = out_terms(branch_near, branch_far)
-            grad_normed = lay.reduce_chips((near.astype(F32) + far.astype(F32)).astype(BF))
+            out_total = lay.ring_step(out_part(terms, 1))
             if gathered:
-                mixture = lay.ring_step(moe.spread(2, [part], mixture))
-                part = moe.exchange(moe.out_sum(3, ready))
-                total, terms, grad_normed, mixture, part = sync(total, terms, grad_normed, mixture, part)
-                mixture = lay.ring_step(moe.spread(3, [part], mixture))
-                last = moe.send_back(moe.out_sum(0, total))
-            out_total = lay.ring_step(out_part(terms, 1))
+                mixture, part, last = beside
+                mixture = moe.spread(3, [part], mixture)
+                last = moe.exchange(last)
+                total, out_total, mixture, last = sync(total, out_total, mixture, last)
+                mixture = lay.ring_step(mixture)
         total = (total.astype(F32) + grad_qkv[step].astype(F32)).astype(BF)
+        if n == 0:
+            total, near, far, branch_near, *beside = sync(total, near, far, branch_near, *beside)
+        elif n == 1:
+            total, terms, *beside = sync(total, terms, *beside)
     grad_qkv = a2a(total.reshape(nc, rb, 3 * cols), "ctx")
     for step in list(range(2, nz)) + [0]:
         out_total = (out_total.astype(F32) + out_part(terms, step).astype(F32)).astype(BF)
@@ -1105,7 +1112,7 @@
     if gathered:
         weight_grads = [moe.grads[n] for n in range(3)]
     if gathered:
-        mixture = moe.spread(0, last, mixture)
+        mixture = moe.spread(0, [last], mixture)
     grad_down_w, grad_gate_w, grad_up_w = weight_grads
     result = middle + mixture.astype(F32)
     grad_query_w, grad_key_w, grad_value_w, grad_attn_gain = lay.weight_rows(

time: 717 us -> 710 us (level)
  starting transfers between devices: 138 us -> 148 us
    pallas_call x8, Pallas kernels: 22.8 us -> 13.8 us  [add_rows(): pl.pallas_call(add_kernel, grid=(rows // tile,), in_specs=[row, row] + [p...]
    ppermute x24, waiting for transfers between devices: 64.6 us -> 73.4 us  [ring_step(): return lax.ppermute(value, 'dp', self.ring)]
    all_to_all x12, waiting for transfers between devices: 22.1 us -> 14.6 us  [exchange(): lax.all_to_all(offered, 'ctx', split_axis=0, concat_axis=0, tiled=True, a...]
    unnamed x210 -> x218, local copies, waits for them, and re-layouts: 29.7 us -> 25.6 us
  transfers between devices with their start and end apart: 87 -> 87, of which waited for: 35 -> 32; matrix products, arithmetic and copies ran while one was open for 10% -> 9% of each run, Pallas kernels for 31% -> 29%
where the time goes in v4:
time: 710 us; the launch traced here: 699 us
  Pallas kernels  222 us (31%)
  waiting for transfers between devices  177 us (25%)
  starting transfers between devices  148 us (21%)
  local copies, waits for them, and re-layouts  51.6 us (7%)
  other arithmetic  40.8 us (6%)
  blocking collectives  40.1 us (6%)
  matrix products  15.4 us (2%)
    ppermute x48, waiting for transfers between devices, swap(): return lax.ppermute(value, 'ctx', [(i, i ^ bit) for i in range(self.nc)])  85.9 us
    ppermute x24, waiting for transfers between devices, ring_step(): return lax.ppermute(value, 'dp', self.ring)  73.4 us
    pallas_call x4, Pallas kernels, expert_chunk(): pl.pallas_call(functools.partial(expert_kernel, kinds), grid_spec=pltpu.P...  66.9 us
    all_to_all x12, starting transfers between devices, exchange(): lax.all_to_all(offered, 'ctx', split_axis=0, concat_axis=0, tiled=True, a...  51.2 us
    ppermute x24, starting transfers between devices, ring_step(): return lax.ppermute(value, 'dp', self.ring)  45.6 us
    pallas_call x3, Pallas kernels, contract_many(): pl.pallas_call(functools.partial(contract_kernel, count), grid=(max(rows,...  44.4 us
    ppermute x48, starting transfers between devices, swap(): return lax.ppermute(value, 'ctx', [(i, i ^ bit) for i in range(self.nc)])  35.8 us
    unnamed x218, local copies, waits for them, and re-layouts  25.6 us
  transfers between devices with their start and end apart: 87, of which 32 were waited for; matrix products, arithmetic and copies ran while one was open for 9% of the time, Pallas kernels for 29%

profile of v4, /device:TPU:0, one launch (start us, length us, event | category | flops | bytes accessed | tf_op | source)
XLA Modules:
  0.0 698.5 jit_solution(5408162238229289488)
XLA Ops:
  4.3 5.3 all-to-all-start
  20.8 11.1 %collective-permute-done = bf16[64,2048]{1,0:T(8,128)(2,1)} collective-permute-done((bf16[64,2048]{1,0:T(8,128)(2,1)S(1)}, bf16[64,2048]{1,0:T(8,128)(2,1)}, u32[]{:S(2)}, u32[]{:S(2)}) %collective-permute-start) | collective-permute-done | bytes 262176 | tf_op jit(solution)/shard_map/ppermute | solution.py:71
  40.6 21.0 %all_to_all.175 = bf16[32,2,640]{2,1,0:T(2,128)(2,1)S(1)} all-to-all(bf16[32,2,640]{2,1,0:T(2,128)(2,1)S(1)} %reshape.363), channel_id=1, replica_groups=mesh['dp'=4,'ctx'=8] {'dp','ctx'}, dimensions={0} | all-to-all | bytes 163840 | tf_op jit(solution)/shard_map/all_to_all | solution.py:200
  76.5 19.7 %collective-permute-done.9 = bf16[64,2048]{1,0:T(8,128)(2,1)} collective-permute-done((bf16[64,2048]{1,0:T(8,128)(2,1)}, bf16[64,2048]{1,0:T(8,128)(2,1)}, u32[]{:S(2)}, u32[]{:S(2)}) %collective-permute-start.9) | collective-permute-done | bytes 262176 | tf_op jit(solution)/shard_map/ppermute | solution.py:71
  104.3 9.9 %shard_map.301.rows = bf16[1024,2048]{1,0:T(8,128)(2,1)S(1)} custom-call(s32[16]{0:T(128)S(1)} %pad_add_fusion.1.place_ref, bf16[512,2048]{1,0:T(8,128)(2,1)S(1)} %pad_maximum_fusion.near, bf16[512,2048]{1,0:T(8,128)(2,1)} %collective-permute-done.8.far, f32[1,2048]{1,0:T(1,128)S(1)} %reshape.315.gain), custom_call_target="tpu_custom_call" | custom-call | flops 8388608 | bytes 12582912 | tf_op jit(solution)/shard_map/pallas_call | solution.py:435
  117.6 6.9 collective-permute-done.10.refs_3_
  125.8 8.4 %shard_map.302 = (f32[1024,768]{1,0:T(8,128)}, f32[2,1024]{1,0:T(2,128)}) custom-call(s32[4]{0:T(128)} %pad_add_fusion.2.layer_ref, bf16[1024,2048]{1,0:T(8,128)(2,1)} %copy-done.11, bf16[512,768]{1,0:T(8,128)(2,1)} %bitcast.176, bf16[512,768]{1,0:T(8,128)(2,1)} %copy-done.58, bf16[512,768]{1,0:T(8,128)(2,1)} %collective-permute-done.7.refs_2_, ...), custom_call_target="tpu_custom_call" | custom-call | flops 3221225472 | bytes 8912896 | tf_op jit(solution)/shard_map/pallas_call | solution.py:473
  135.0 9.7 %all_gather.6 = f32[8,16,128]{2,1,0:T(8,128)S(1)} all-gather(f32[1,16,128]{2,1,0:T(8,128)S(1)} %all_gather_reshape.6), channel_id=1, replica_groups=mesh['dp'=4,'ctx'=8] {'ctx'}, dimensions={0}, use_global_device_ids=true | all-gather | bytes 73728 | tf_op jit(solution)/shard_map/all_gather | solution.py:978
  156.9 11.6 %shard_map.303 = (bf16[1024,256]{1,0:T(8,128)(2,1)}, f32[1024,256]{1,0:T(8,128)}, f32[1024,256]{1,0:T(8,128)}, bf16[1024,256]{1,0:T(8,128)(2,1)}, bf16[1024,256]{1,0:T(8,128)(2,1)}, /*index=5*/bf16[1024,256]{1,0:T(8,128)(2,1)}) custom-call(s32[16]{0:T(128)} %copy-done.55, f32[1024,768]{1,0:T(8,128)} %get-tuple-element.215.q_pre.k_pre.v_pre, ...), custom_call_target="tpu_custom_call" | custom-call | flops 805306368 | bytes 6291456 | tf_op jit(solution)/shard_map/pallas_call | solution.py:674
  183.6 11.0 %collective-permute-done.17 = bf16[2,64,2048]{2,1,0:T(8,128)(2,1)} collective-permute-done((bf16[2,64,2048]{2,1,0:T(8,128)(2,1)}, bf16[2,64,2048]{2,1,0:T(8,128)(2,1)}, u32[]{:S(2)}, u32[]{:S(2)}) %collective-permute-start.17) | collective-permute-done | bytes 524320 | tf_op jit(solution)/shard_map/ppermute | solution.py:68
  219.3 10.2 %collective-permute-done.22.block.notes = bf16[128,2176]{1,0:T(8,128)(2,1)S(1)} collective-permute-done((bf16[128,2176]{1,0:T(8,128)(2,1)S(1)}, bf16[128,2176]{1,0:T(8,128)(2,1)S(1)}, u32[]{:S(2)}, u32[]{:S(2)}) %collective-permute-start.22) | collective-permute-done | bytes 557088 | tf_op jit(solution)/shard_map/ppermute | solution.py:71
  246.3 16.6 %shard_map.307 = (bf16[384,2176]{1,0:T(8,128)(2,1)}, bf16[384,2176]{1,0:T(8,128)(2,1)}, bf16[384,512]{1,0:T(8,128)(2,1)}, bf16[384,512]{1,0:T(8,128)(2,1)}, bf16...) custom-call(s32[1]{0:T(128)} %bitcast.178, ...), custom_call_target="tpu_custom_call" | custom-call | flops 9663676416 | bytes 12582912 | tf_op jit(solution)/shard_map/pallas_call | solution.py:366
  280.0 16.7 %shard_map.309 = (bf16[384,2176]{1,0:T(8,128)(2,1)}, bf16[384,2176]{1,0:T(8,128)(2,1)}, bf16[384,512]{1,0:T(8,128)(2,1)}, bf16[384,512]{1,0:T(8,128)(2,1)}, bf16...) custom-call(s32[1]{0:T(128)} %bitcast.179, ...), custom_call_target="tpu_custom_call" | custom-call | flops 9663676416 | bytes 12582912 | tf_op jit(solution)/shard_map/pallas_call | solution.py:366
  301.8 7.1 %collective-permute-done.28 = bf16[96,2048]{1,0:T(8,128)(2,1)S(1)} collective-permute-done((bf16[96,2048]{1,0:T(8,128)(2,1)S(1)}, bf16[96,2048]{1,0:T(8,128)(2,1)S(1)}, u32[]{:S(2)}, u32[]{:S(2)}) %collective-permute-start.28) | collective-permute-done | bytes 393248 | tf_op jit(solution)/shard_map/ppermute | solution.py:68
  319.5 16.8 %shard_map.311 = (bf16[384,2176]{1,0:T(8,128)(2,1)}, bf16[384,2176]{1,0:T(8,128)(2,1)}, bf16[384,512]{1,0:T(8,128)(2,1)}, bf16[384,512]{1,0:T(8,128)(2,1)}, bf16...) custom-call(s32[1]{0:T(128)} %bitcast.180, ...), custom_call_target="tpu_custom_call" | custom-call | flops 9663676416 | bytes 12582912 | tf_op jit(solution)/shard_map/pallas_call | solution.py:366
  352.6 16.8 %shard_map.315 = (bf16[384,2176]{1,0:T(8,128)(2,1)}, bf16[384,2176]{1,0:T(8,128)(2,1)}, bf16[384,512]{1,0:T(8,128)(2,1)}, bf16[384,512]{1,0:T(8,128)(2,1)}, bf16...) custom-call(s32[1]{0:T(128)} %bitcast.181, ...), custom_call_target="tpu_custom_call" | custom-call | flops 9663676416 | bytes 12582912 | tf_op jit(solution)/shard_map/pallas_call | solution.py:366
  381.6 15.1 %shard_map.317 = f32[512,2048]{1,0:T(8,128)} custom-call(bf16[384,512]{1,0:T(8,128)(2,1)} %get-tuple-element.256.refs_0_, bf16[384,512]{1,0:T(8,128)(2,1)} %get-tuple-element.257.refs_1_, bf16[384,512]{1,0:T(8,128)(2,1)} %get-tuple-element.258.refs_2_, bf16[384,512]{1,0:T(8,128)(2,1)} %get-tuple-element.259.refs_3_, ...), custom_call_target="tpu_custom_call" | custom-call | flops 6442450944 | bytes 19922944 | tf_op jit(solution)/shard_map/pallas_call | solution.py:398
  410.8 14.7 %shard_map.320 = f32[2048,512]{1,0:T(8,128)} custom-call(bf16[384,2176]{1,0:T(8,128)(2,1)} %bitcast.42.near.refs_0_, bf16[384,2176]{1,0:T(8,128)(2,1)} %collective-permute-done.23.far.refs_1_, bf16[384,2176]{1,0:T(8,128)(2,1)} %bitcast.47.near.refs_2_, bf16[384,2176]{1,0:T(8,128)(2,1)} %collective-permute-done.25.far.refs_3_, ...), custom_call_target="tpu_custom_call" | custom-call | flops 6442450944 | bytes 19922944 | tf_op jit(solution)/shard_map/pallas_call | solution.py:398
  437.1 7.6 %collective-permute-done.45.refs_3_ = bf16[96,2176]{1,0:T(8,128)(2,1)S(1)} collective-permute-done((bf16[96,2176]{1,0:T(8,128)(2,1)S(1)}, bf16[96,2176]{1,0:T(8,128)(2,1)S(1)}, u32[]{:S(2)}, u32[]{:S(2)}) %collective-permute-start.45) | collective-permute-done | bytes 417824 | tf_op jit(solution)/shard_map/ppermute | solution.py:68
  446.1 14.7 %shard_map.323 = f32[2048,512]{1,0:T(8,128)} custom-call(bf16[384,2176]{1,0:T(8,128)(2,1)} %bitcast.42.near.refs_0_, bf16[384,2176]{1,0:T(8,128)(2,1)} %collective-permute-done.23.far.refs_1_, bf16[384,2176]{1,0:T(8,128)(2,1)} %bitcast.47.near.refs_2_, bf16[384,2176]{1,0:T(8,128)(2,1)} %collective-permute-done.25.far.refs_3_, ...), custom_call_target="tpu_custom_call" | custom-call | flops 6442450944 | bytes 19922944 | tf_op jit(solution)/shard_map/pallas_call | solution.py:398
  475.1 6.6 collective-permute-done.48
  481.7 10.6 %collective-permute-done.47 = bf16[128,2048]{1,0:T(8,128)(2,1)S(1)} collective-permute-done((bf16[128,2048]{1,0:T(8,128)(2,1)S(1)}, bf16[128,2048]{1,0:T(8,128)(2,1)S(1)}, u32[]{:S(2)}, u32[]{:S(2)}) %collective-permute-start.47) | collective-permute-done | bytes 524320 | tf_op jit(solution)/shard_map/ppermute | solution.py:68
  505.3 11.0 %shard_map.329 = (f32[1024,256]{1,0:T(8,128)}, f32[1024,256]{1,0:T(8,128)}, bf16[1024,256]{1,0:T(8,128)(2,1)}, f32[2,2,1024]{2,1,0:T(2,128)}, f32[2,256]{1,0:T(2,128)}) custom-call(s32[16]{0:T(128)} %copy-done.55, bf16[1024,256]{1,0:T(8,128)(2,1)} %pad_maximum_fusion.9.sent_grad, f32[1024,256]{1,0:T(8,128)} %get-tuple-element.308.attended, ...), custom_call_target="tpu_custom_call" | custom-call | flops 1610612736 | bytes 6291456 | tf_op jit(solution)/shard_map/pallas_call | solution.py:684
  526.5 5.8 all-to-all-start.12
  532.4 9.4 %all_gather.7 = f32[8,16,128]{2,1,0:T(8,128)S(1)} all-gather(f32[1,16,128]{2,1,0:T(8,128)S(1)} %all_gather_reshape.7), channel_id=1, replica_groups=mesh['dp'=4,'ctx'=8] {'ctx'}, dimensions={0}, use_global_device_ids=true | all-gather | bytes 73728 | tf_op jit(solution)/shard_map/all_gather | solution.py:978
  550.4 7.3 %shard_map.331 = (bf16[512,768]{1,0:T(8,128)(2,1)S(1)}, bf16[512,768]{1,0:T(8,128)(2,1)}, bf16[512,768]{1,0:T(8,128)(2,1)S(1)}, bf16[512,768]{1,0:T(8,128)(2,1)S(1)}) custom-call(s32[4]{0:T(128)S(1)} %copy-done.57, bf16[1024,2048]{1,0:T(8,128)(2,1)} %copy-done.11, bf16[1024,768]{1,0:T(8,128)(2,1)S(1)} %pad_maximum_fusion.2.grads), custom_call_target="tpu_custom_call" | custom-call | flops 3221225472 | bytes 7340032 | tf_op jit(solution)/shard_map/pallas_call | solution.py:507
  565.5 6.6 shard_map.332
  572.8 7.0 %collective-permute-done.57.refs_2_ = bf16[96,2048]{1,0:T(8,128)(2,1)} collective-permute-done((bf16[96,2048]{1,0:T(8,128)(2,1)}, bf16[96,2048]{1,0:T(8,128)(2,1)}, u32[]{:S(2)}, u32[]{:S(2)}) %collective-permute-start.57) | collective-permute-done | bytes 393248 | tf_op jit(solution)/shard_map/ppermute | solution.py:68
  607.9 13.1 %collective-permute-done.62 = bf16[2,64,2048]{2,1,0:T(8,128)(2,1)S(1)} collective-permute-done((bf16[2,64,2048]{2,1,0:T(8,128)(2,1)S(1)}, bf16[2,64,2048]{2,1,0:T(8,128)(2,1)S(1)}, u32[]{:S(2)}, u32[]{:S(2)}) %collective-permute-start.62) | collective-permute-done | bytes 524320 | tf_op jit(solution)/shard_map/ppermute | solution.py:68
  623.4 5.8 collective-permute-done.63
  650.2 14.1 %collective-permute-done.68 = bf16[64,2048]{1,0:T(8,128)(2,1)} collective-permute-done((bf16[64,2048]{1,0:T(8,128)(2,1)}, bf16[64,2048]{1,0:T(8,128)(2,1)}, u32[]{:S(2)}, u32[]{:S(2)}) %collective-permute-start.68) | collective-permute-done | bytes 262176 | tf_op jit(solution)/shard_map/ppermute | solution.py:71
  683.2 6.5 collective-permute-done.71
  (553 shorter events, 340.8 us)
Async XLA Ops:
  4.3 28.4 %all-to-all-start = ((bf16[8,64,768]{2,1,0:T(8,128)(2,1)}), bf16[8,64,768]{2,1,0:T(8,128)(2,1)S(1)}, u32[]{:S(2)}, u32[]{:S(2)}) async-start(bf16[8,64,768]{2,1,0:T(8,128)(2,1)} %pad_maximum_fusion.5), calls=%async_computation | async-start | bytes 1572864 | tf_op jit(solution)/shard_map/all_to_all | solution.py:200
  32.7 29.0 %collective-permute-start.4 = (bf16[512,768]{1,0:T(8,128)(2,1)S(1)}, bf16[512,768]{1,0:T(8,128)(2,1)S(1)}, u32[]{:S(2)}, u32[]{:S(2)}) collective-permute-start(bf16[512,768]{1,0:T(8,128)(2,1)S(1)} %bitcast.175), channel_id=1, source_target_pairs={{0,8},{8,24},{24,16},{16,0},{1,9},{9,25},{25,17},{17,1},{2,10},{10... | collective-permute-start | bytes 2359304 | tf_op jit(solution)/shard_map/ppermute | solution.py:71
  34.4 27.3 %collective-permute-start.5 = (bf16[128,2048]{1,0:T(8,128)(2,1)S(1)}, bf16[128,2048]{1,0:T(8,128)(2,1)}, u32[]{:S(2)}, u32[]{:S(2)}) collective-permute-start(bf16[128,2048]{1,0:T(8,128)(2,1)S(1)} %bitcast.185), channel_id=1, source_target_pairs={{0,6},{1,7},{2,4},{3,5},{4,2},{5,3},{6,0},{7,1},{8,14},{9,15},{10,... | collective-permute-start | bytes 1572872 | tf_op jit(solution)/shard_map/ppermute | solution.py:68
  35.8 25.9 %collective-permute-start.6 = (bf16[64,2048]{1,0:T(8,128)(2,1)}, bf16[64,2048]{1,0:T(8,128)(2,1)S(1)}, u32[]{:S(2)}, u32[]{:S(2)}) collective-permute-start(bf16[64,2048]{1,0:T(8,128)(2,1)} %collective-permute-done), channel_id=1, source_target_pairs={{0,8},{8,24},{24,16},{16,0},{1,9},{9,25},{25,17},{17,1},{2,10},{10... | collective-permute-start | bytes 786440 | tf_op jit(solution)/shard_map/ppermute | solution.py:71
  65.0 31.2 %collective-permute-start.8 = (bf16[512,2048]{1,0:T(8,128)(2,1)S(1)}, bf16[512,2048]{1,0:T(8,128)(2,1)}, u32[]{:S(2)}, u32[]{:S(2)}) collective-permute-start(bf16[512,2048]{1,0:T(8,128)(2,1)S(1)} %pad_maximum_fusion.near), channel_id=1, source_target_pairs={{0,1},{1,0},{2,3},{3,2},{4,5},{5,4},{6,7},{7,6},{8,9},{9,8},{10,11... | collective-permute-start | bytes 6291464 | tf_op jit(solution)/shard_map/ppermute | solution.py:68
  65.2 31.0 %all-to-all-start.2 = ((bf16[4,96,2048]{2,1,0:T(8,128)(2,1)}), bf16[4,96,2048]{2,1,0:T(8,128)(2,1)}, u32[]{:S(2)}, u32[]{:S(2)}) async-start(bf16[4,96,2048]{2,1,0:T(8,128)(2,1)} %bitcast.169), calls=%async_computation.2 | async-start | bytes 3145728 | tf_op jit(solution)/shard_map/all_to_all | solution.py:709
  69.7 26.5 %collective-permute-start.7 = (bf16[512,768]{1,0:T(8,128)(2,1)S(1)}, bf16[512,768]{1,0:T(8,128)(2,1)}, u32[]{:S(2)}, u32[]{:S(2)}) collective-permute-start(bf16[512,768]{1,0:T(8,128)(2,1)S(1)} %copy-done.59), channel_id=1, source_target_pairs={{0,8},{8,24},{24,16},{16,0},{1,9},{9,25},{25,17},{17,1},{2,10},{10... | collective-permute-start | bytes 2359304 | tf_op jit(solution)/shard_map/ppermute | solution.py:71
  70.4 25.8 %collective-permute-start.9 = (bf16[64,2048]{1,0:T(8,128)(2,1)}, bf16[64,2048]{1,0:T(8,128)(2,1)}, u32[]{:S(2)}, u32[]{:S(2)}) collective-permute-start(bf16[64,2048]{1,0:T(8,128)(2,1)} %copy-done.93), channel_id=1, source_target_pairs={{0,8},{8,24},{24,16},{16,0},{1,9},{9,25},{25,17},{17,1},{2,10},{10... | collective-permute-start | bytes 786440 | tf_op jit(solution)/shard_map/ppermute | solution.py:71
  96.2 28.2 %all-to-all-start.3 = ((bf16[4,96,2048]{2,1,0:T(8,128)(2,1)}), bf16[4,96,2048]{2,1,0:T(8,128)(2,1)}, u32[]{:S(2)}, u32[]{:S(2)}) async-start(bf16[4,96,2048]{2,1,0:T(8,128)(2,1)} %bitcast.170), calls=%async_computation.3 | async-start | bytes 3145728 | tf_op jit(solution)/shard_map/all_to_all | solution.py:709
  125.3 43.2 %collective-permute-start.14 = (bf16[384,2048]{1,0:T(8,128)(2,1)}, bf16[384,2048]{1,0:T(8,128)(2,1)}, u32[]{:S(2)}, u32[]{:S(2)}) collective-permute-start(bf16[384,2048]{1,0:T(8,128)(2,1)} %bitcast.17.dy_near.refs_8_), channel_id=1, source_target_pairs={{0,1},{1,0},{2,3},{3,2},{4,5},{5,4},{6,7},{7,6},{8,9},{9,8},{10,11... | collective-permute-start | bytes 4718600 | tf_op jit(solution)/shard_map/ppermute | solution.py:68
  125.3 43.3 %collective-permute-start.15 = (bf16[384,2048]{1,0:T(8,128)(2,1)}, bf16[384,2048]{1,0:T(8,128)(2,1)}, u32[]{:S(2)}, u32[]{:S(2)}) collective-permute-start(bf16[384,2048]{1,0:T(8,128)(2,1)} %bitcast.28.dy_near.refs_10_), channel_id=1, source_target_pairs={{0,1},{1,0},{2,3},{3,2},{4,5},{5,4},{6,7},{7,6},{8,9},{9,8},{10,11... | collective-permute-start | bytes 4718600 | tf_op jit(solution)/shard_map/ppermute | solution.py:68
  237.8 25.7 %all-to-all-start.6 = ((bf16[4,96,2176]{2,1,0:T(8,128)(2,1)}), bf16[4,96,2176]{2,1,0:T(8,128)(2,1)}, u32[]{:S(2)}, u32[]{:S(2)}) async-start(bf16[4,96,2176]{2,1,0:T(8,128)(2,1)} %bitcast.46), calls=%async_computation.6 | async-start | bytes 3342336 | tf_op jit(solution)/shard_map/all_to_all | solution.py:709
  266.4 42.5 %all-to-all-start.7 = ((bf16[4,96,2176]{2,1,0:T(8,128)(2,1)}), bf16[4,96,2176]{2,1,0:T(8,128)(2,1)}, u32[]{:S(2)}, u32[]{:S(2)}) async-start(bf16[4,96,2176]{2,1,0:T(8,128)(2,1)} %bitcast.48), calls=%async_computation.7 | async-start | bytes 3342336 | tf_op jit(solution)/shard_map/all_to_all | solution.py:709
  273.1 28.7 %collective-permute-start.29 = (bf16[96,2048]{1,0:T(8,128)(2,1)S(1)}, bf16[96,2048]{1,0:T(8,128)(2,1)S(1)}, u32[]{:S(2)}, u32[]{:S(2)}) collective-permute-start(bf16[96,2048]{1,0:T(8,128)(2,1)S(1)} %get-tuple-element.407), channel_id=1, source_target_pairs={{0,6},{1,7},{2,4},{3,5},{4,2},{5,3},{6,0},{7,1},{8,14},{9,15},{10,... | collective-permute-start | bytes 1179656 | tf_op jit(solution)/shard_map/ppermute | solution.py:68
  275.9 32.9 %collective-permute-start.28 = (bf16[96,2048]{1,0:T(8,128)(2,1)S(1)}, bf16[96,2048]{1,0:T(8,128)(2,1)S(1)}, u32[]{:S(2)}, u32[]{:S(2)}) collective-permute-start(bf16[96,2048]{1,0:T(8,128)(2,1)S(1)} %get-tuple-element.408), channel_id=1, source_target_pairs={{0,4},{1,5},{2,6},{3,7},{4,0},{5,1},{6,2},{7,3},{8,12},{9,13},{10,... | collective-permute-start | bytes 1179656 | tf_op jit(solution)/shard_map/ppermute | solution.py:68
  276.5 32.5 %collective-permute-start.27 = (bf16[96,2048]{1,0:T(8,128)(2,1)S(1)}, bf16[96,2048]{1,0:T(8,128)(2,1)S(1)}, u32[]{:S(2)}, u32[]{:S(2)}) collective-permute-start(bf16[96,2048]{1,0:T(8,128)(2,1)S(1)} %get-tuple-element.409), channel_id=1, source_target_pairs={{0,2},{1,3},{2,0},{3,1},{4,6},{5,7},{6,4},{7,5},{8,10},{9,11},{10,... | collective-permute-start | bytes 1179656 | tf_op jit(solution)/shard_map/ppermute | solution.py:68
  276.6 32.4 %collective-permute-start.26 = (bf16[128,2176]{1,0:T(8,128)(2,1)S(1)}, bf16[128,2176]{1,0:T(8,128)(2,1)S(1)}, u32[]{:S(2)}, u32[]{:S(2)}) collective-permute-start(bf16[128,2176]{1,0:T(8,128)(2,1)S(1)} %collective-permute-done.24.block.notes), channel_id=1, source_target_pairs={{0,8},{8,24},{24,16},{16,0},{1,9},{9,25},{25,17},{17,1},{2,10},{10... | collective-permute-start | bytes 1671176 | tf_op jit(solution)/shard_map/ppermute | solution.py:71
  311.3 28.9 %collective-permute-start.31 = (bf16[384,2048]{1,0:T(8,128)(2,1)}, bf16[384,2048]{1,0:T(8,128)(2,1)}, u32[]{:S(2)}, u32[]{:S(2)}) collective-permute-start(bf16[384,2048]{1,0:T(8,128)(2,1)} %constant_dynamic-update-slice_fusion.2.dy_near.refs_14_), channel_id=1, source_target_pairs={{0,1},{1,0},{2,3},{3,2},{4,5},{5,4},{6,7},{7,6},{8,9},{9,8},{10,11... | collective-permute-start | bytes 4718600 | tf_op jit(solution)/shard_map/ppermute | solution.py:68
  314.8 25.4 %all-to-all-start.8 = ((bf16[4,96,2176]{2,1,0:T(8,128)(2,1)}), bf16[4,96,2176]{2,1,0:T(8,128)(2,1)}, u32[]{:S(2)}, u32[]{:S(2)}) async-start(bf16[4,96,2176]{2,1,0:T(8,128)(2,1)} %bitcast.50), calls=%async_computation.8 | async-start | bytes 3342336 | tf_op jit(solution)/shard_map/all_to_all | solution.py:709
  340.8 28.7 %collective-permute-start.35 = (bf16[384,2176]{1,0:T(8,128)(2,1)}, bf16[384,2176]{1,0:T(8,128)(2,1)}, u32[]{:S(2)}, u32[]{:S(2)}) collective-permute-start(bf16[384,2176]{1,0:T(8,128)(2,1)} %get-tuple-element.254), channel_id=1, source_target_pairs={{0,1},{1,0},{2,3},{3,2},{4,5},{5,4},{6,7},{7,6},{8,9},{9,8},{10,11... | collective-permute-start | bytes 5013512 | tf_op jit(solution)/shard_map/ppermute | solution.py:68
  344.5 25.8 %all-to-all-start.9 = ((bf16[4,96,2176]{2,1,0:T(8,128)(2,1)}), bf16[4,96,2176]{2,1,0:T(8,128)(2,1)}, u32[]{:S(2)}, u32[]{:S(2)}) async-start(bf16[4,96,2176]{2,1,0:T(8,128)(2,1)} %bitcast.52), calls=%async_computation.9 | async-start | bytes 3342336 | tf_op jit(solution)/shard_map/all_to_all | solution.py:709
  370.3 26.4 %collective-permute-start.40 = (bf16[384,2176]{1,0:T(8,128)(2,1)}, bf16[384,2176]{1,0:T(8,128)(2,1)S(1)}, u32[]{:S(2)}, u32[]{:S(2)}) collective-permute-start(bf16[384,2176]{1,0:T(8,128)(2,1)} %get-tuple-element.264), channel_id=1, source_target_pairs={{0,1},{1,0},{2,3},{3,2},{4,5},{5,4},{6,7},{7,6},{8,9},{9,8},{10,11... | collective-permute-start | bytes 5013512 | tf_op jit(solution)/shard_map/ppermute | solution.py:68
  398.9 27.3 %all-to-all-start.10 = ((bf16[4,96,2176]{2,1,0:T(8,128)(2,1)}), bf16[4,96,2176]{2,1,0:T(8,128)(2,1)S(1)}, u32[]{:S(2)}, u32[]{:S(2)}) async-start(bf16[4,96,2176]{2,1,0:T(8,128)(2,1)} %bitcast.54), calls=%async_computation.10 | async-start | bytes 3342336 | tf_op jit(solution)/shard_map/all_to_all | solution.py:709
  434.1 34.8 %collective-permute-start.52 = (bf16[384,2048]{1,0:T(8,128)(2,1)}, bf16[384,2048]{1,0:T(8,128)(2,1)S(1)}, u32[]{:S(2)}, u32[]{:S(2)}) collective-permute-start(bf16[384,2048]{1,0:T(8,128)(2,1)} %get-tuple-element.306), channel_id=1, source_target_pairs={{0,1},{1,0},{2,3},{3,2},{4,5},{5,4},{6,7},{7,6},{8,9},{9,8},{10,11... | collective-permute-start | bytes 4718600 | tf_op jit(solution)/shard_map/ppermute | solution.py:68
  434.1 35.4 %collective-permute-start.49 = (bf16[384,2048]{1,0:T(8,128)(2,1)}, bf16[384,2048]{1,0:T(8,128)(2,1)S(1)}, u32[]{:S(2)}, u32[]{:S(2)}) collective-permute-start(bf16[384,2048]{1,0:T(8,128)(2,1)} %get-tuple-element.300), channel_id=1, source_target_pairs={{0,1},{1,0},{2,3},{3,2},{4,5},{5,4},{6,7},{7,6},{8,9},{9,8},{10,11... | collective-permute-start | bytes 4718600 | tf_op jit(solution)/shard_map/ppermute | solution.py:68
  434.6 26.2 %collective-permute-start.44 = (bf16[96,2176]{1,0:T(8,128)(2,1)}, bf16[96,2176]{1,0:T(8,128)(2,1)}, u32[]{:S(2)}, u32[]{:S(2)}) collective-permute-start(bf16[96,2176]{1,0:T(8,128)(2,1)} %get-tuple-element.395), channel_id=1, source_target_pairs={{0,4},{1,5},{2,6},{3,7},{4,0},{5,1},{6,2},{7,3},{8,12},{9,13},{10,... | collective-permute-start | bytes 1253384 | tf_op jit(solution)/shard_map/ppermute | solution.py:68
  435.2 25.7 %collective-permute-start.43 = (bf16[96,2176]{1,0:T(8,128)(2,1)}, bf16[96,2176]{1,0:T(8,128)(2,1)}, u32[]{:S(2)}, u32[]{:S(2)}) collective-permute-start(bf16[96,2176]{1,0:T(8,128)(2,1)} %get-tuple-element.396), channel_id=1, source_target_pairs={{0,2},{1,3},{2,0},{3,1},{4,6},{5,7},{6,4},{7,5},{8,10},{9,11},{10,... | collective-permute-start | bytes 1253384 | tf_op jit(solution)/shard_map/ppermute | solution.py:68
  495.6 25.8 %all-to-all-start.11 = ((bf16[4,96,2048]{2,1,0:T(8,128)(2,1)}), bf16[4,96,2048]{2,1,0:T(8,128)(2,1)S(1)}, u32[]{:S(2)}, u32[]{:S(2)}) async-start(bf16[4,96,2048]{2,1,0:T(8,128)(2,1)} %bitcast.174), calls=%async_computation.11 | async-start | bytes 3145728 | tf_op jit(solution)/shard_map/all_to_all | solution.py:709
  585.8 46.1 %all-to-all-start.13 = ((bf16[4,96,2048]{2,1,0:T(8,128)(2,1)}), bf16[4,96,2048]{2,1,0:T(8,128)(2,1)S(1)}, u32[]{:S(2)}, u32[]{:S(2)}) async-start(bf16[4,96,2048]{2,1,0:T(8,128)(2,1)} %bitcast.173), calls=%async_computation.13 | async-start | bytes 3145728 | tf_op jit(solution)/shard_map/all_to_all | solution.py:709
  596.9 35.0 %collective-permute-start.66 = (bf16[128,2048]{1,0:T(8,128)(2,1)S(1)}, bf16[128,2048]{1,0:T(8,128)(2,1)S(1)}, u32[]{:S(2)}, u32[]{:S(2)}) collective-permute-start(bf16[128,2048]{1,0:T(8,128)(2,1)S(1)} %shard_map.333), channel_id=1, source_target_pairs={{0,8},{8,24},{24,16},{16,0},{1,9},{9,25},{25,17},{17,1},{2,10},{10... | collective-permute-start | bytes 1572872 | tf_op jit(solution)/shard_map/ppermute | solution.py:71
  599.4 32.4 %collective-permute-start.59 = (bf16[512,768]{1,0:T(8,128)(2,1)S(1)}, bf16[512,768]{1,0:T(8,128)(2,1)}, u32[]{:S(2)}, u32[]{:S(2)}) collective-permute-start(bf16[512,768]{1,0:T(8,128)(2,1)S(1)} %copy-done.85), channel_id=1, source_target_pairs={{0,8},{8,24},{24,16},{16,0},{1,9},{9,25},{25,17},{17,1},{2,10},{10... | collective-permute-start | bytes 2359304 | tf_op jit(solution)/shard_map/ppermute | solution.py:71
  634.3 30.0 %all-to-all-start.14 = ((bf16[4,96,2048]{2,1,0:T(8,128)(2,1)}), bf16[4,96,2048]{2,1,0:T(8,128)(2,1)}, u32[]{:S(2)}, u32[]{:S(2)}) async-start(bf16[4,96,2048]{2,1,0:T(8,128)(2,1)} %bitcast.83), calls=%async_computation.14 | async-start | bytes 3145728 | tf_op jit(solution)/shard_map/all_to_all | solution.py:709
  (162 other events, 1687.1 us)

commit v5 on v4

--- a/solution.py
+++ b/solution.py
@@ -1084,7 +1084,7 @@
             total, near, far, branch_near, *beside = sync(total, near, far, branch_near, *beside)
         elif n == 1:
             terms = out_terms(branch_near, branch_far)
-            grad_normed = lay.reduce_ctx(near, far)
+            grad_normed = lay.reduce_chips(both)
             if gathered:
                 mixture = lay.ring_step(moe.spread(2, beside[:-2], mixture))
                 part = moe.exchange(beside[-2])
@@ -1100,7 +1100,8 @@
                 mixture = lay.ring_step(mixture)
         total = (total.astype(F32) + grad_qkv[step].astype(F32)).astype(BF)
         if n == 0:
-            total, near, far, branch_near, *beside = sync(total, near, far, branch_near, *beside)
+            both = (near.astype(F32) + lay.swap(far, 1).astype(F32)).astype(BF)
+            both, branch_near, *beside = sync(both, branch_near, *beside)
         elif n == 1:
             total, terms, *beside = sync(total, terms, *beside)
     grad_qkv = a2a(total.reshape(nc, rb, 3 * cols), "ctx")

time: 710 us -> 706 us (level)
    unnamed x218 -> x220, local copies, waits for them, and re-layouts: 25.6 us -> 26.9 us
  transfers between devices with their start and end apart: 87 -> 87, of which waited for: 32 -> 29; matrix products, arithmetic and copies ran while one was open for 9% -> 9% of each run, Pallas kernels for 29% -> 29%
where the time goes in v5:
time: 706 us; the launch traced here: 695 us
  Pallas kernels  223 us (32%)
  waiting for transfers between devices  178 us (25%)
  starting transfers between devices  142 us (20%)
  local copies, waits for them, and re-layouts  54.8 us (8%)
  other arithmetic  41.1 us (6%)
  blocking collectives  40.1 us (6%)
  matrix products  13.4 us (2%)
    ppermute x48, waiting for transfers between devices, swap(): return lax.ppermute(value, 'ctx', [(i, i ^ bit) for i in range(self.nc)])  80.4 us
    ppermute x24, waiting for transfers between devices, ring_step(): return lax.ppermute(value, 'dp', self.ring)  79.2 us
    pallas_call x4, Pallas kernels, expert_chunk(): pl.pallas_call(functools.partial(expert_kernel, kinds), grid_spec=pltpu.P...  66.7 us
    all_to_all x12, starting transfers between devices, exchange(): lax.all_to_all(offered, 'ctx', split_axis=0, concat_axis=0, tiled=True, a...  50.9 us
    pallas_call x3, Pallas kernels, contract_many(): pl.pallas_call(functools.partial(contract_kernel, count), grid=(max(rows,...  44.4 us
    ppermute x24, starting transfers between devices, ring_step(): return lax.ppermute(value, 'dp', self.ring)  40.6 us
    ppermute x48, starting transfers between devices, swap(): return lax.ppermute(value, 'ctx', [(i, i ^ bit) for i in range(self.nc)])  35.4 us
    unnamed x220, local copies, waits for them, and re-layouts  26.9 us
  transfers between devices with their start and end apart: 87, of which 29 were waited for; matrix products, arithmetic and copies ran while one was open for 9% of the time, Pallas kernels for 29%

profile of v5, /device:TPU:0, one launch (start us, length us, event | category | flops | bytes accessed | tf_op | source)
XLA Modules:
  0.0 694.9 jit_solution(556576804541684605)
XLA Ops:
  4.3 5.3 all-to-all-start
  20.8 11.1 %collective-permute-done = bf16[64,2048]{1,0:T(8,128)(2,1)} collective-permute-done((bf16[64,2048]{1,0:T(8,128)(2,1)S(1)}, bf16[64,2048]{1,0:T(8,128)(2,1)}, u32[]{:S(2)}, u32[]{:S(2)}) %collective-permute-start) | collective-permute-done | bytes 262176 | tf_op jit(solution)/shard_map/ppermute | solution.py:71
  40.6 21.0 %all_to_all.175 = bf16[32,2,640]{2,1,0:T(2,128)(2,1)S(1)} all-to-all(bf16[32,2,640]{2,1,0:T(2,128)(2,1)S(1)} %reshape.363), channel_id=1, replica_groups=mesh['dp'=4,'ctx'=8] {'dp','ctx'}, dimensions={0} | all-to-all | bytes 163840 | tf_op jit(solution)/shard_map/all_to_all | solution.py:200
  76.4 19.7 %collective-permute-done.9 = bf16[64,2048]{1,0:T(8,128)(2,1)} collective-permute-done((bf16[64,2048]{1,0:T(8,128)(2,1)}, bf16[64,2048]{1,0:T(8,128)(2,1)}, u32[]{:S(2)}, u32[]{:S(2)}) %collective-permute-start.9) | collective-permute-done | bytes 262176 | tf_op jit(solution)/shard_map/ppermute | solution.py:71
  104.3 9.9 %shard_map.301.rows = bf16[1024,2048]{1,0:T(8,128)(2,1)S(1)} custom-call(s32[16]{0:T(128)S(1)} %pad_add_fusion.1.place_ref, bf16[512,2048]{1,0:T(8,128)(2,1)S(1)} %pad_maximum_fusion.near, bf16[512,2048]{1,0:T(8,128)(2,1)} %collective-permute-done.8.far, f32[1,2048]{1,0:T(1,128)S(1)} %reshape.315.gain), custom_call_target="tpu_custom_call" | custom-call | flops 8388608 | bytes 12582912 | tf_op jit(solution)/shard_map/pallas_call | solution.py:435
  117.6 6.9 collective-permute-done.10.refs_3_
  125.9 8.4 %shard_map.302 = (f32[1024,768]{1,0:T(8,128)}, f32[2,1024]{1,0:T(2,128)}) custom-call(s32[4]{0:T(128)} %pad_add_fusion.2.layer_ref, bf16[1024,2048]{1,0:T(8,128)(2,1)} %copy-done.10, bf16[512,768]{1,0:T(8,128)(2,1)} %bitcast.175, bf16[512,768]{1,0:T(8,128)(2,1)} %copy-done.55, bf16[512,768]{1,0:T(8,128)(2,1)} %collective-permute-done.7.refs_2_, ...), custom_call_target="tpu_custom_call" | custom-call | flops 3221225472 | bytes 8912896 | tf_op jit(solution)/shard_map/pallas_call | solution.py:473
  135.1 9.7 %all_gather.6 = f32[8,16,128]{2,1,0:T(8,128)S(1)} all-gather(f32[1,16,128]{2,1,0:T(8,128)S(1)} %all_gather_reshape.6), channel_id=1, replica_groups=mesh['dp'=4,'ctx'=8] {'ctx'}, dimensions={0}, use_global_device_ids=true | all-gather | bytes 73728 | tf_op jit(solution)/shard_map/all_gather | solution.py:978
  157.0 11.6 %shard_map.303 = (bf16[1024,256]{1,0:T(8,128)(2,1)}, f32[1024,256]{1,0:T(8,128)}, f32[1024,256]{1,0:T(8,128)}, bf16[1024,256]{1,0:T(8,128)(2,1)}, bf16[1024,256]{1,0:T(8,128)(2,1)}, /*index=5*/bf16[1024,256]{1,0:T(8,128)(2,1)}) custom-call(s32[16]{0:T(128)} %copy-done.52, f32[1024,768]{1,0:T(8,128)} %get-tuple-element.213.q_pre.k_pre.v_pre, ...), custom_call_target="tpu_custom_call" | custom-call | flops 805306368 | bytes 6291456 | tf_op jit(solution)/shard_map/pallas_call | solution.py:674
  183.7 10.9 %collective-permute-done.17 = bf16[2,64,2048]{2,1,0:T(8,128)(2,1)S(1)} collective-permute-done((bf16[2,64,2048]{2,1,0:T(8,128)(2,1)}, bf16[2,64,2048]{2,1,0:T(8,128)(2,1)S(1)}, u32[]{:S(2)}, u32[]{:S(2)}) %collective-permute-start.17) | collective-permute-done | bytes 524320 | tf_op jit(solution)/shard_map/ppermute | solution.py:68
  198.1 5.3 collective-permute-done.18
  217.8 10.2 %collective-permute-done.22.block.notes = bf16[128,2176]{1,0:T(8,128)(2,1)S(1)} collective-permute-done((bf16[128,2176]{1,0:T(8,128)(2,1)S(1)}, bf16[128,2176]{1,0:T(8,128)(2,1)S(1)}, u32[]{:S(2)}, u32[]{:S(2)}) %collective-permute-start.22) | collective-permute-done | bytes 557088 | tf_op jit(solution)/shard_map/ppermute | solution.py:71
  244.8 16.6 %shard_map.307 = (bf16[384,2176]{1,0:T(8,128)(2,1)}, bf16[384,2176]{1,0:T(8,128)(2,1)}, bf16[384,512]{1,0:T(8,128)(2,1)}, bf16[384,512]{1,0:T(8,128)(2,1)}, bf16...) custom-call(s32[1]{0:T(128)} %bitcast.177, ...), custom_call_target="tpu_custom_call" | custom-call | flops 9663676416 | bytes 12582912 | tf_op jit(solution)/shard_map/pallas_call | solution.py:366
  278.5 16.6 %shard_map.309 = (bf16[384,2176]{1,0:T(8,128)(2,1)}, bf16[384,2176]{1,0:T(8,128)(2,1)}, bf16[384,512]{1,0:T(8,128)(2,1)}, bf16[384,512]{1,0:T(8,128)(2,1)}, bf16...) custom-call(s32[1]{0:T(128)} %bitcast.178, ...), custom_call_target="tpu_custom_call" | custom-call | flops 9663676416 | bytes 12582912 | tf_op jit(solution)/shard_map/pallas_call | solution.py:366
  300.4 7.0 %collective-permute-done.28 = bf16[96,2048]{1,0:T(8,128)(2,1)S(1)} collective-permute-done((bf16[96,2048]{1,0:T(8,128)(2,1)S(1)}, bf16[96,2048]{1,0:T(8,128)(2,1)S(1)}, u32[]{:S(2)}, u32[]{:S(2)}) %collective-permute-start.28) | collective-permute-done | bytes 393248 | tf_op jit(solution)/shard_map/ppermute | solution.py:68
  318.1 16.8 %shard_map.311 = (bf16[384,2176]{1,0:T(8,128)(2,1)}, bf16[384,2176]{1,0:T(8,128)(2,1)}, bf16[384,512]{1,0:T(8,128)(2,1)}, bf16[384,512]{1,0:T(8,128)(2,1)}, bf16...) custom-call(s32[1]{0:T(128)} %bitcast.179, ...), custom_call_target="tpu_custom_call" | custom-call | flops 9663676416 | bytes 12582912 | tf_op jit(solution)/shard_map/pallas_call | solution.py:366
  351.2 16.8 %shard_map.315 = (bf16[384,2176]{1,0:T(8,128)(2,1)}, bf16[384,2176]{1,0:T(8,128)(2,1)}, bf16[384,512]{1,0:T(8,128)(2,1)}, bf16[384,512]{1,0:T(8,128)(2,1)}, bf16...) custom-call(s32[1]{0:T(128)} %bitcast.180, ...), custom_call_target="tpu_custom_call" | custom-call | flops 9663676416 | bytes 12582912 | tf_op jit(solution)/shard_map/pallas_call | solution.py:366
  380.2 15.1 %shard_map.317 = f32[512,2048]{1,0:T(8,128)} custom-call(bf16[384,512]{1,0:T(8,128)(2,1)} %get-tuple-element.254.refs_0_, bf16[384,512]{1,0:T(8,128)(2,1)} %get-tuple-element.255.refs_1_, bf16[384,512]{1,0:T(8,128)(2,1)} %get-tuple-element.256.refs_2_, bf16[384,512]{1,0:T(8,128)(2,1)} %get-tuple-element.257.refs_3_, ...), custom_call_target="tpu_custom_call" | custom-call | flops 6442450944 | bytes 19922944 | tf_op jit(solution)/shard_map/pallas_call | solution.py:398
  409.4 14.7 %shard_map.320 = f32[2048,512]{1,0:T(8,128)} custom-call(bf16[384,2176]{1,0:T(8,128)(2,1)} %bitcast.42.near.refs_0_, bf16[384,2176]{1,0:T(8,128)(2,1)} %collective-permute-done.23.far.refs_1_, bf16[384,2176]{1,0:T(8,128)(2,1)} %bitcast.47.near.refs_2_, bf16[384,2176]{1,0:T(8,128)(2,1)} %collective-permute-done.25.far.refs_3_, ...), custom_call_target="tpu_custom_call" | custom-call | flops 6442450944 | bytes 19922944 | tf_op jit(solution)/shard_map/pallas_call | solution.py:398
  435.8 7.6 %collective-permute-done.45.refs_3_ = bf16[96,2176]{1,0:T(8,128)(2,1)S(1)} collective-permute-done((bf16[96,2176]{1,0:T(8,128)(2,1)S(1)}, bf16[96,2176]{1,0:T(8,128)(2,1)S(1)}, u32[]{:S(2)}, u32[]{:S(2)}) %collective-permute-start.45) | collective-permute-done | bytes 417824 | tf_op jit(solution)/shard_map/ppermute | solution.py:68
  444.8 14.7 %shard_map.323 = f32[2048,512]{1,0:T(8,128)} custom-call(bf16[384,2176]{1,0:T(8,128)(2,1)} %bitcast.42.near.refs_0_, bf16[384,2176]{1,0:T(8,128)(2,1)} %collective-permute-done.23.far.refs_1_, bf16[384,2176]{1,0:T(8,128)(2,1)} %bitcast.47.near.refs_2_, bf16[384,2176]{1,0:T(8,128)(2,1)} %collective-permute-done.25.far.refs_3_, ...), custom_call_target="tpu_custom_call" | custom-call | flops 6442450944 | bytes 19922944 | tf_op jit(solution)/shard_map/pallas_call | solution.py:398
  480.3 10.6 %collective-permute-done.47 = bf16[128,2048]{1,0:T(8,128)(2,1)S(1)} collective-permute-done((bf16[128,2048]{1,0:T(8,128)(2,1)S(1)}, bf16[128,2048]{1,0:T(8,128)(2,1)S(1)}, u32[]{:S(2)}, u32[]{:S(2)}) %collective-permute-start.47) | collective-permute-done | bytes 524320 | tf_op jit(solution)/shard_map/ppermute | solution.py:68
  503.9 11.0 %shard_map.329 = (f32[1024,256]{1,0:T(8,128)}, f32[1024,256]{1,0:T(8,128)}, bf16[1024,256]{1,0:T(8,128)(2,1)}, f32[2,2,1024]{2,1,0:T(2,128)}, f32[2,256]{1,0:T(2,128)}) custom-call(s32[16]{0:T(128)} %copy-done.52, bf16[1024,256]{1,0:T(8,128)(2,1)} %pad_maximum_fusion.9.sent_grad, f32[1024,256]{1,0:T(8,128)} %get-tuple-element.306.attended, ...), custom_call_target="tpu_custom_call" | custom-call | flops 1610612736 | bytes 6291456 | tf_op jit(solution)/shard_map/pallas_call | solution.py:684
  525.0 5.9 all-to-all-start.12
  530.9 9.4 %all_gather.7 = f32[8,16,128]{2,1,0:T(8,128)S(1)} all-gather(f32[1,16,128]{2,1,0:T(8,128)S(1)} %all_gather_reshape.7), channel_id=1, replica_groups=mesh['dp'=4,'ctx'=8] {'ctx'}, dimensions={0}, use_global_device_ids=true | all-gather | bytes 73728 | tf_op jit(solution)/shard_map/all_gather | solution.py:978
  549.0 7.3 %shard_map.331 = (bf16[512,768]{1,0:T(8,128)(2,1)S(1)}, bf16[512,768]{1,0:T(8,128)(2,1)}, bf16[512,768]{1,0:T(8,128)(2,1)S(1)}, bf16[512,768]{1,0:T(8,128)(2,1)S(1)}) custom-call(s32[4]{0:T(128)S(1)} %copy-done.54, bf16[1024,2048]{1,0:T(8,128)(2,1)} %copy-done.10, bf16[1024,768]{1,0:T(8,128)(2,1)S(1)} %pad_maximum_fusion.2.grads), custom_call_target="tpu_custom_call" | custom-call | flops 3221225472 | bytes 7340032 | tf_op jit(solution)/shard_map/pallas_call | solution.py:507
  564.2 5.6 shard_map.332
  571.5 7.0 %collective-permute-done.57.refs_2_ = bf16[96,2048]{1,0:T(8,128)(2,1)} collective-permute-done((bf16[96,2048]{1,0:T(8,128)(2,1)}, bf16[96,2048]{1,0:T(8,128)(2,1)}, u32[]{:S(2)}, u32[]{:S(2)}) %collective-permute-start.57) | collective-permute-done | bytes 393248 | tf_op jit(solution)/shard_map/ppermute | solution.py:68
  611.7 15.5 %collective-permute-done.63 = bf16[1,64,2048]{2,1,0:T(8,128)(2,1)S(1)} collective-permute-done((bf16[1,64,2048]{2,1,0:T(8,128)(2,1)S(1)}, bf16[1,64,2048]{2,1,0:T(8,128)(2,1)S(1)}, u32[]{:S(2)}, u32[]{:S(2)}) %collective-permute-start.63) | collective-permute-done | bytes 262176 | tf_op jit(solution)/shard_map/ppermute | solution.py:68
  643.5 17.2 %collective-permute-done.68 = bf16[64,2048]{1,0:T(8,128)(2,1)} collective-permute-done((bf16[64,2048]{1,0:T(8,128)(2,1)}, bf16[64,2048]{1,0:T(8,128)(2,1)}, u32[]{:S(2)}, u32[]{:S(2)}) %collective-permute-start.68) | collective-permute-done | bytes 262176 | tf_op jit(solution)/shard_map/ppermute | solution.py:71
  665.0 7.1 %collective-permute-done.70 = bf16[64,2048]{1,0:T(8,128)(2,1)S(1)} collective-permute-done((bf16[64,2048]{1,0:T(8,128)(2,1)S(1)}, bf16[64,2048]{1,0:T(8,128)(2,1)S(1)}, u32[]{:S(2)}, u32[]{:S(2)}) %collective-permute-start.70) | collective-permute-done | bytes 262176 | tf_op jit(solution)/shard_map/ppermute | solution.py:71
  679.0 7.0 %collective-permute-done.71 = bf16[64,2048]{1,0:T(8,128)(2,1)S(1)} collective-permute-done((bf16[64,2048]{1,0:T(8,128)(2,1)S(1)}, bf16[64,2048]{1,0:T(8,128)(2,1)S(1)}, u32[]{:S(2)}, u32[]{:S(2)}) %collective-permute-start.71) | collective-permute-done | bytes 262176 | tf_op jit(solution)/shard_map/ppermute | solution.py:71
  (555 shorter events, 332.4 us)
Async XLA Ops:
  4.3 28.4 %all-to-all-start = ((bf16[8,64,768]{2,1,0:T(8,128)(2,1)}), bf16[8,64,768]{2,1,0:T(8,128)(2,1)S(1)}, u32[]{:S(2)}, u32[]{:S(2)}) async-start(bf16[8,64,768]{2,1,0:T(8,128)(2,1)} %pad_maximum_fusion.5), calls=%async_computation | async-start | bytes 1572864 | tf_op jit(solution)/shard_map/all_to_all | solution.py:200
  32.7 29.0 %collective-permute-start.4 = (bf16[512,768]{1,0:T(8,128)(2,1)S(1)}, bf16[512,768]{1,0:T(8,128)(2,1)S(1)}, u32[]{:S(2)}, u32[]{:S(2)}) collective-permute-start(bf16[512,768]{1,0:T(8,128)(2,1)S(1)} %bitcast.174), channel_id=1, source_target_pairs={{0,8},{8,24},{24,16},{16,0},{1,9},{9,25},{25,17},{17,1},{2,10},{10... | collective-permute-start | bytes 2359304 | tf_op jit(solution)/shard_map/ppermute | solution.py:71
  34.4 27.3 %collective-permute-start.5 = (bf16[128,2048]{1,0:T(8,128)(2,1)S(1)}, bf16[128,2048]{1,0:T(8,128)(2,1)}, u32[]{:S(2)}, u32[]{:S(2)}) collective-permute-start(bf16[128,2048]{1,0:T(8,128)(2,1)S(1)} %bitcast.184), channel_id=1, source_target_pairs={{0,6},{1,7},{2,4},{3,5},{4,2},{5,3},{6,0},{7,1},{8,14},{9,15},{10,... | collective-permute-start | bytes 1572872 | tf_op jit(solution)/shard_map/ppermute | solution.py:68
  35.8 25.9 %collective-permute-start.6 = (bf16[64,2048]{1,0:T(8,128)(2,1)}, bf16[64,2048]{1,0:T(8,128)(2,1)S(1)}, u32[]{:S(2)}, u32[]{:S(2)}) collective-permute-start(bf16[64,2048]{1,0:T(8,128)(2,1)} %collective-permute-done), channel_id=1, source_target_pairs={{0,8},{8,24},{24,16},{16,0},{1,9},{9,25},{25,17},{17,1},{2,10},{10... | collective-permute-start | bytes 786440 | tf_op jit(solution)/shard_map/ppermute | solution.py:71
  65.0 31.2 %collective-permute-start.8 = (bf16[512,2048]{1,0:T(8,128)(2,1)S(1)}, bf16[512,2048]{1,0:T(8,128)(2,1)}, u32[]{:S(2)}, u32[]{:S(2)}) collective-permute-start(bf16[512,2048]{1,0:T(8,128)(2,1)S(1)} %pad_maximum_fusion.near), channel_id=1, source_target_pairs={{0,1},{1,0},{2,3},{3,2},{4,5},{5,4},{6,7},{7,6},{8,9},{9,8},{10,11... | collective-permute-start | bytes 6291464 | tf_op jit(solution)/shard_map/ppermute | solution.py:68
  65.2 31.0 %all-to-all-start.2 = ((bf16[4,96,2048]{2,1,0:T(8,128)(2,1)}), bf16[4,96,2048]{2,1,0:T(8,128)(2,1)}, u32[]{:S(2)}, u32[]{:S(2)}) async-start(bf16[4,96,2048]{2,1,0:T(8,128)(2,1)} %bitcast.169), calls=%async_computation.2 | async-start | bytes 3145728 | tf_op jit(solution)/shard_map/all_to_all | solution.py:709
  69.7 26.5 %collective-permute-start.7 = (bf16[512,768]{1,0:T(8,128)(2,1)S(1)}, bf16[512,768]{1,0:T(8,128)(2,1)}, u32[]{:S(2)}, u32[]{:S(2)}) collective-permute-start(bf16[512,768]{1,0:T(8,128)(2,1)S(1)} %copy-done.56), channel_id=1, source_target_pairs={{0,8},{8,24},{24,16},{16,0},{1,9},{9,25},{25,17},{17,1},{2,10},{10... | collective-permute-start | bytes 2359304 | tf_op jit(solution)/shard_map/ppermute | solution.py:71
  70.4 25.8 %collective-permute-start.9 = (bf16[64,2048]{1,0:T(8,128)(2,1)}, bf16[64,2048]{1,0:T(8,128)(2,1)}, u32[]{:S(2)}, u32[]{:S(2)}) collective-permute-start(bf16[64,2048]{1,0:T(8,128)(2,1)} %copy-done.94), channel_id=1, source_target_pairs={{0,8},{8,24},{24,16},{16,0},{1,9},{9,25},{25,17},{17,1},{2,10},{10... | collective-permute-start | bytes 786440 | tf_op jit(solution)/shard_map/ppermute | solution.py:71
  96.2 28.3 %all-to-all-start.3 = ((bf16[4,96,2048]{2,1,0:T(8,128)(2,1)}), bf16[4,96,2048]{2,1,0:T(8,128)(2,1)}, u32[]{:S(2)}, u32[]{:S(2)}) async-start(bf16[4,96,2048]{2,1,0:T(8,128)(2,1)} %bitcast.170), calls=%async_computation.3 | async-start | bytes 3145728 | tf_op jit(solution)/shard_map/all_to_all | solution.py:709
  125.4 43.2 %collective-permute-start.14 = (bf16[384,2048]{1,0:T(8,128)(2,1)}, bf16[384,2048]{1,0:T(8,128)(2,1)}, u32[]{:S(2)}, u32[]{:S(2)}) collective-permute-start(bf16[384,2048]{1,0:T(8,128)(2,1)} %bitcast.17.dy_near.refs_8_), channel_id=1, source_target_pairs={{0,1},{1,0},{2,3},{3,2},{4,5},{5,4},{6,7},{7,6},{8,9},{9,8},{10,11... | collective-permute-start | bytes 4718600 | tf_op jit(solution)/shard_map/ppermute | solution.py:68
  125.4 43.3 %collective-permute-start.15 = (bf16[384,2048]{1,0:T(8,128)(2,1)}, bf16[384,2048]{1,0:T(8,128)(2,1)}, u32[]{:S(2)}, u32[]{:S(2)}) collective-permute-start(bf16[384,2048]{1,0:T(8,128)(2,1)} %bitcast.28.dy_near.refs_10_), channel_id=1, source_target_pairs={{0,1},{1,0},{2,3},{3,2},{4,5},{5,4},{6,7},{7,6},{8,9},{9,8},{10,11... | collective-permute-start | bytes 4718600 | tf_op jit(solution)/shard_map/ppermute | solution.py:68
  236.3 25.7 %all-to-all-start.6 = ((bf16[4,96,2176]{2,1,0:T(8,128)(2,1)}), bf16[4,96,2176]{2,1,0:T(8,128)(2,1)}, u32[]{:S(2)}, u32[]{:S(2)}) async-start(bf16[4,96,2176]{2,1,0:T(8,128)(2,1)} %bitcast.46), calls=%async_computation.6 | async-start | bytes 3342336 | tf_op jit(solution)/shard_map/all_to_all | solution.py:709
  265.0 42.5 %all-to-all-start.7 = ((bf16[4,96,2176]{2,1,0:T(8,128)(2,1)}), bf16[4,96,2176]{2,1,0:T(8,128)(2,1)}, u32[]{:S(2)}, u32[]{:S(2)}) async-start(bf16[4,96,2176]{2,1,0:T(8,128)(2,1)} %bitcast.48), calls=%async_computation.7 | async-start | bytes 3342336 | tf_op jit(solution)/shard_map/all_to_all | solution.py:709
  271.6 28.7 %collective-permute-start.29 = (bf16[96,2048]{1,0:T(8,128)(2,1)S(1)}, bf16[96,2048]{1,0:T(8,128)(2,1)S(1)}, u32[]{:S(2)}, u32[]{:S(2)}) collective-permute-start(bf16[96,2048]{1,0:T(8,128)(2,1)S(1)} %get-tuple-element.403), channel_id=1, source_target_pairs={{0,6},{1,7},{2,4},{3,5},{4,2},{5,3},{6,0},{7,1},{8,14},{9,15},{10,... | collective-permute-start | bytes 1179656 | tf_op jit(solution)/shard_map/ppermute | solution.py:68
  274.5 32.9 %collective-permute-start.28 = (bf16[96,2048]{1,0:T(8,128)(2,1)S(1)}, bf16[96,2048]{1,0:T(8,128)(2,1)S(1)}, u32[]{:S(2)}, u32[]{:S(2)}) collective-permute-start(bf16[96,2048]{1,0:T(8,128)(2,1)S(1)} %get-tuple-element.404), channel_id=1, source_target_pairs={{0,4},{1,5},{2,6},{3,7},{4,0},{5,1},{6,2},{7,3},{8,12},{9,13},{10,... | collective-permute-start | bytes 1179656 | tf_op jit(solution)/shard_map/ppermute | solution.py:68
  275.0 32.5 %collective-permute-start.27 = (bf16[96,2048]{1,0:T(8,128)(2,1)S(1)}, bf16[96,2048]{1,0:T(8,128)(2,1)S(1)}, u32[]{:S(2)}, u32[]{:S(2)}) collective-permute-start(bf16[96,2048]{1,0:T(8,128)(2,1)S(1)} %get-tuple-element.405), channel_id=1, source_target_pairs={{0,2},{1,3},{2,0},{3,1},{4,6},{5,7},{6,4},{7,5},{8,10},{9,11},{10,... | collective-permute-start | bytes 1179656 | tf_op jit(solution)/shard_map/ppermute | solution.py:68
  275.1 32.4 %collective-permute-start.26 = (bf16[128,2176]{1,0:T(8,128)(2,1)S(1)}, bf16[128,2176]{1,0:T(8,128)(2,1)S(1)}, u32[]{:S(2)}, u32[]{:S(2)}) collective-permute-start(bf16[128,2176]{1,0:T(8,128)(2,1)S(1)} %collective-permute-done.24.block.notes), channel_id=1, source_target_pairs={{0,8},{8,24},{24,16},{16,0},{1,9},{9,25},{25,17},{17,1},{2,10},{10... | collective-permute-start | bytes 1671176 | tf_op jit(solution)/shard_map/ppermute | solution.py:71
  309.9 28.9 %collective-permute-start.31 = (bf16[384,2048]{1,0:T(8,128)(2,1)}, bf16[384,2048]{1,0:T(8,128)(2,1)}, u32[]{:S(2)}, u32[]{:S(2)}) collective-permute-start(bf16[384,2048]{1,0:T(8,128)(2,1)} %constant_dynamic-update-slice_fusion.2.dy_near.refs_14_), channel_id=1, source_target_pairs={{0,1},{1,0},{2,3},{3,2},{4,5},{5,4},{6,7},{7,6},{8,9},{9,8},{10,11... | collective-permute-start | bytes 4718600 | tf_op jit(solution)/shard_map/ppermute | solution.py:68
  313.4 25.4 %all-to-all-start.8 = ((bf16[4,96,2176]{2,1,0:T(8,128)(2,1)}), bf16[4,96,2176]{2,1,0:T(8,128)(2,1)}, u32[]{:S(2)}, u32[]{:S(2)}) async-start(bf16[4,96,2176]{2,1,0:T(8,128)(2,1)} %bitcast.50), calls=%async_computation.8 | async-start | bytes 3342336 | tf_op jit(solution)/shard_map/all_to_all | solution.py:709
  339.3 28.6 %collective-permute-start.35 = (bf16[384,2176]{1,0:T(8,128)(2,1)}, bf16[384,2176]{1,0:T(8,128)(2,1)}, u32[]{:S(2)}, u32[]{:S(2)}) collective-permute-start(bf16[384,2176]{1,0:T(8,128)(2,1)} %get-tuple-element.252), channel_id=1, source_target_pairs={{0,1},{1,0},{2,3},{3,2},{4,5},{5,4},{6,7},{7,6},{8,9},{9,8},{10,11... | collective-permute-start | bytes 5013512 | tf_op jit(solution)/shard_map/ppermute | solution.py:68
  343.1 25.8 %all-to-all-start.9 = ((bf16[4,96,2176]{2,1,0:T(8,128)(2,1)}), bf16[4,96,2176]{2,1,0:T(8,128)(2,1)}, u32[]{:S(2)}, u32[]{:S(2)}) async-start(bf16[4,96,2176]{2,1,0:T(8,128)(2,1)} %bitcast.52), calls=%async_computation.9 | async-start | bytes 3342336 | tf_op jit(solution)/shard_map/all_to_all | solution.py:709
  368.9 26.5 %collective-permute-start.40 = (bf16[384,2176]{1,0:T(8,128)(2,1)}, bf16[384,2176]{1,0:T(8,128)(2,1)S(1)}, u32[]{:S(2)}, u32[]{:S(2)}) collective-permute-start(bf16[384,2176]{1,0:T(8,128)(2,1)} %get-tuple-element.262), channel_id=1, source_target_pairs={{0,1},{1,0},{2,3},{3,2},{4,5},{5,4},{6,7},{7,6},{8,9},{9,8},{10,11... | collective-permute-start | bytes 5013512 | tf_op jit(solution)/shard_map/ppermute | solution.py:68
  397.6 27.3 %all-to-all-start.10 = ((bf16[4,96,2176]{2,1,0:T(8,128)(2,1)}), bf16[4,96,2176]{2,1,0:T(8,128)(2,1)S(1)}, u32[]{:S(2)}, u32[]{:S(2)}) async-start(bf16[4,96,2176]{2,1,0:T(8,128)(2,1)} %bitcast.54), calls=%async_computation.10 | async-start | bytes 3342336 | tf_op jit(solution)/shard_map/all_to_all | solution.py:709
  432.7 34.8 %collective-permute-start.52 = (bf16[384,2048]{1,0:T(8,128)(2,1)}, bf16[384,2048]{1,0:T(8,128)(2,1)S(1)}, u32[]{:S(2)}, u32[]{:S(2)}) collective-permute-start(bf16[384,2048]{1,0:T(8,128)(2,1)} %get-tuple-element.304), channel_id=1, source_target_pairs={{0,1},{1,0},{2,3},{3,2},{4,5},{5,4},{6,7},{7,6},{8,9},{9,8},{10,11... | collective-permute-start | bytes 4718600 | tf_op jit(solution)/shard_map/ppermute | solution.py:68
  432.7 35.3 %collective-permute-start.49 = (bf16[384,2048]{1,0:T(8,128)(2,1)}, bf16[384,2048]{1,0:T(8,128)(2,1)S(1)}, u32[]{:S(2)}, u32[]{:S(2)}) collective-permute-start(bf16[384,2048]{1,0:T(8,128)(2,1)} %get-tuple-element.298), channel_id=1, source_target_pairs={{0,1},{1,0},{2,3},{3,2},{4,5},{5,4},{6,7},{7,6},{8,9},{9,8},{10,11... | collective-permute-start | bytes 4718600 | tf_op jit(solution)/shard_map/ppermute | solution.py:68
  433.3 26.2 %collective-permute-start.44 = (bf16[96,2176]{1,0:T(8,128)(2,1)}, bf16[96,2176]{1,0:T(8,128)(2,1)}, u32[]{:S(2)}, u32[]{:S(2)}) collective-permute-start(bf16[96,2176]{1,0:T(8,128)(2,1)} %get-tuple-element.391), channel_id=1, source_target_pairs={{0,4},{1,5},{2,6},{3,7},{4,0},{5,1},{6,2},{7,3},{8,12},{9,13},{10,... | collective-permute-start | bytes 1253384 | tf_op jit(solution)/shard_map/ppermute | solution.py:68
  433.8 25.7 %collective-permute-start.43 = (bf16[96,2176]{1,0:T(8,128)(2,1)}, bf16[96,2176]{1,0:T(8,128)(2,1)}, u32[]{:S(2)}, u32[]{:S(2)}) collective-permute-start(bf16[96,2176]{1,0:T(8,128)(2,1)} %get-tuple-element.392), channel_id=1, source_target_pairs={{0,2},{1,3},{2,0},{3,1},{4,6},{5,7},{6,4},{7,5},{8,10},{9,11},{10,... | collective-permute-start | bytes 1253384 | tf_op jit(solution)/shard_map/ppermute | solution.py:68
  494.2 25.7 %all-to-all-start.11 = ((bf16[4,96,2048]{2,1,0:T(8,128)(2,1)}), bf16[4,96,2048]{2,1,0:T(8,128)(2,1)S(1)}, u32[]{:S(2)}, u32[]{:S(2)}) async-start(bf16[4,96,2048]{2,1,0:T(8,128)(2,1)} %bitcast.173), calls=%async_computation.11 | async-start | bytes 3145728 | tf_op jit(solution)/shard_map/all_to_all | solution.py:709
  583.2 45.0 %collective-permute-start.59 = (bf16[512,768]{1,0:T(8,128)(2,1)}, bf16[512,768]{1,0:T(8,128)(2,1)}, u32[]{:S(2)}, u32[]{:S(2)}) collective-permute-start(bf16[512,768]{1,0:T(8,128)(2,1)} %add_convert_fusion.4), channel_id=1, source_target_pairs={{0,8},{8,24},{24,16},{16,0},{1,9},{9,25},{25,17},{17,1},{2,10},{10... | collective-permute-start | bytes 2359304 | tf_op jit(solution)/shard_map/ppermute | solution.py:71
  594.9 33.3 %all-to-all-start.13 = ((bf16[4,96,2048]{2,1,0:T(8,128)(2,1)}), bf16[4,96,2048]{2,1,0:T(8,128)(2,1)S(1)}, u32[]{:S(2)}, u32[]{:S(2)}) async-start(bf16[4,96,2048]{2,1,0:T(8,128)(2,1)} %bitcast.80), calls=%async_computation.13 | async-start | bytes 3145728 | tf_op jit(solution)/shard_map/all_to_all | solution.py:709
  630.7 30.0 %all-to-all-start.14 = ((bf16[4,96,2048]{2,1,0:T(8,128)(2,1)}), bf16[4,96,2048]{2,1,0:T(8,128)(2,1)}, u32[]{:S(2)}, u32[]{:S(2)}) async-start(bf16[4,96,2048]{2,1,0:T(8,128)(2,1)} %bitcast.83), calls=%async_computation.14 | async-start | bytes 3145728 | tf_op jit(solution)/shard_map/all_to_all | solution.py:709
  635.4 25.4 %collective-permute-start.67 = (bf16[512,768]{1,0:T(8,128)(2,1)}, bf16[512,768]{1,0:T(8,128)(2,1)}, u32[]{:S(2)}, u32[]{:S(2)}) collective-permute-start(bf16[512,768]{1,0:T(8,128)(2,1)} %add_convert_fusion.3), channel_id=1, source_target_pairs={{0,8},{8,24},{24,16},{16,0},{1,9},{9,25},{25,17},{17,1},{2,10},{10... | collective-permute-start | bytes 2359304 | tf_op jit(solution)/shard_map/ppermute | solution.py:71
  (163 other events, 1669.1 us)
